TPU v7x, 512 devices: a whole 4x4x16 slice. The times are simulated.
512 devices in a mesh: ctx: 64 (over z, x), head: 8 (over y, core).
Axes of the slice: x: 4, y: 4, z: 16, core: 2. Of those that a mesh axis runs over, the one named last changes fastest.
Arguments:
- inputs: bfloat16 [16384, 2048], P('ctx', 'head'), may hold values from -16 to 16
- w_query: bfloat16 [2048, 2048], P(None, 'head'), may hold values from -0.125 to 0.125
- w_key: bfloat16 [2048, 2048], P(None, 'head'), may hold values from -0.125 to 0.125
- w_value: bfloat16 [2048, 2048], P(None, 'head'), may hold values from -0.125 to 0.125
- w_out: bfloat16 [2048, 2048], P('head'), may hold values from -0.125 to 0.125
- reflect_dir: bfloat16 [16384, 2048], P('ctx', 'head'), may hold values from -25 to 25
- strength: float32 [16, 16384], P('head', 'ctx'), may hold values from 0.5 to 1.5
- hop_count: int32 [64], P('ctx'), may hold values from 1 to 8, as said below
Outputs:
- mixed: bfloat16 [16384, 2048], P('ctx', 'head')
Inputs may be any that keep to these rules, and one draw needn't show every extreme that they name: `hop_count`: some block has exactly 8.
All inputs are finite; a program needn't handle non-finite values.
Results may differ from a plain program's by a relative error of at most 0.019.
Values may be sent and summed in bfloat16 or wider, within the bound.
No kernel may reach another device: no remote copies, remote signals or barrier semaphores. Data moves between devices by JAX's collectives and lax.ppermute only.
A program may use at most 64 MiB of HBM per device.

v0:
```python
import jax
import jax.numpy as jnp
from jax import lax
from jax.sharding import PartitionSpec as P

HOPS = 8


def from_behind(shard, axis, by):
    length = lax.axis_size(axis)
    pairs = [(i, i + by) for i in range(length) if 0 <= i + by < length]
    return lax.ppermute(shard, axis, pairs)


def block_reflector(qblock, kblock, wblock, bblock):
    upper_bound = lax.Precision.HIGHEST
    solver = jax.scipy.linalg.solve_triangular
    length = qblock.shape[0]
    scale = 1.0 / qblock.shape[1] ** 0.5
    row = lax.broadcasted_iota(jnp.int32, (length, length), 0)
    col = lax.broadcasted_iota(jnp.int32, (length, length), 1)
    strict = row > col
    incl = row >= col
    eye_rows = jnp.eye(length, dtype=jnp.float32)
    gram = jnp.where(strict, jnp.dot(wblock, wblock.T, precision=upper_bound), 0.0)
    left_tri = eye_rows + gram * bblock[:, None]
    right_tri = eye_rows + gram * bblock[None, :]
    qdirs = jnp.where(incl, jnp.dot(qblock, wblock.T, precision=upper_bound), 0.0)
    coef = solver(left_tri, qdirs.T, trans=1, lower=True).T
    dir_keys = jnp.where(strict, jnp.dot(wblock, kblock.T, precision=upper_bound), 0.0)
    scaled = coef * bblock[None, :]
    own = jnp.dot(qblock, kblock.T, precision=upper_bound) - jnp.dot(
        scaled, dir_keys, precision=upper_bound
    )
    own = jnp.where(incl, own * scale, -jnp.inf)
    qhat = qblock - jnp.dot(scaled, wblock, precision=upper_bound)
    dkey = solver(right_tri, dir_keys, lower=True)
    weighted = wblock * bblock[:, None]
    khat = kblock - jnp.dot(dkey.T, weighted, precision=upper_bound)
    solved = solver(right_tri, wblock, lower=True)
    trans = jnp.eye(qblock.shape[1], dtype=jnp.float32) - jnp.dot(
        weighted.T, solved, precision=upper_bound
    )
    return (qhat, khat, trans, own)


def shards(inputs, w_query, w_key, w_value, w_out, reflect_dir, strength, hop_count):
    upper_bound = lax.Precision.HIGHEST
    tok_rows = inputs.shape[0]
    width = w_query.shape[1]
    heads = strength.shape[0]
    head_size = width // heads
    scale = 1.0 / head_size**0.5
    piece = lax.all_gather(inputs, "head", axis=1, tiled=True)
    qsum = jnp.dot(piece, w_query, preferred_element_type=jnp.float32)
    ksum = jnp.dot(piece, w_key, preferred_element_type=jnp.float32)
    vsum = jnp.dot(piece, w_value, preferred_element_type=jnp.float32)

    def split_heads(array):
        return array.reshape(tok_rows, heads, head_size).transpose(1, 0, 2)

    query = split_heads(qsum.astype(jnp.bfloat16)).astype(jnp.float32)
    keys = split_heads(ksum.astype(jnp.bfloat16)).astype(jnp.float32)
    values = split_heads(vsum.astype(jnp.bfloat16))
    dirs = split_heads(reflect_dir).astype(jnp.float32)
    dirs = dirs * lax.rsqrt(jnp.sum(dirs * dirs, axis=-1, keepdims=True) + 1e-06)
    qhat, khat, trans, own = jax.vmap(block_reflector)(query, keys, dirs, strength)
    window = hop_count[0]
    position = lax.axis_index("ctx")
    all_scores = [own]
    all_values = [values]
    current = khat
    carried = values
    for hop in range(1, HOPS + 1):
        current = from_behind(current, "ctx", 1)
        carried = from_behind(carried, "ctx", 1)
        valid = (hop <= window) & (position >= hop)
        block_scores = jnp.einsum("hqd,hkd->hqk", qhat, current, precision=upper_bound) * scale
        all_scores.append(jnp.where(valid, block_scores, -jnp.inf))
        all_values.append(carried)
        if hop < HOPS:
            current = jnp.einsum("hed,hkd->hke", trans, current, precision=upper_bound)
    scores = jnp.concatenate(all_scores, axis=2)
    stacked_values = jnp.concatenate(all_values, axis=1)
    top = jnp.max(scores, axis=2, keepdims=True)
    prob = jnp.exp(scores - top)
    total = jnp.sum(prob, axis=2, keepdims=True)
    weights = prob.astype(jnp.bfloat16)
    summed = jnp.einsum("hqk,hkd->hqd", weights, stacked_values, preferred_element_type=jnp.float32)
    attended = (summed / total).astype(jnp.bfloat16)
    attended = attended.transpose(1, 0, 2).reshape(tok_rows, width)
    partial_out = jnp.dot(attended, w_out, preferred_element_type=jnp.float32)
    return lax.psum_scatter(
        partial_out.astype(jnp.bfloat16), "head", scatter_dimension=1, tiled=True
    )


def solution(mesh):
    placed = (
        P("ctx", "head"),
        P(None, "head"),
        P(None, "head"),
        P(None, "head"),
        P("head", None),
        P("ctx", "head"),
        P("head", "ctx"),
        P("ctx"),
    )
    return jax.shard_map(
        shards, mesh=mesh, in_specs=placed, out_specs=P("ctx", "head"), check_vma=False
    )
```

profile of v0, /device:TPU:6, one launch (start us, length us, event | category | flops | bytes accessed | tf_op | source)
XLA Modules:
  0.0 305.2 jit_solution(10032253693452903084)
XLA Ops:
  10.4 4.3 %while.2 = (s32[]{:T(128)}, f32[2,256,256]{1,2,0:T(8,128)S(1)}, s32[2,2]{1,0:T(2,128)S(1)}, f32[2,2,128,128]{3,2,0,1:T(8,128)S(1)}, s32[]{:T(128)}) while((s32[]{:T(128)}, f32[2,256,256]{1,2,0:T(8,128)S(1)}, s32[2,2]{1,0:T(2,128)S(1)}, f32[2,2,128,128]{3,2,0,1:T(8,128)S(1)}, s32[]{:T(128)}) %tuple.48), condition=%wide.while_cond, body=%wide.while_body.sunk | while | flops 2 | bytes 786549 | solution.py:29
  14.8 39.9 %custom-call.11 = f32[2,2,128,128]{2,3,1,0:T(8,128)} custom-call(f32[2,2,128,128]{3,2,1,0:T(8,128)S(1)} %bitcast.138), custom_call_target="InvertDiagBlocksLowerTriangular" | custom-call | tf_op jit(solution)/shard_map/vmap(jit(_solve_triangular))/triangular_solve | solution.py:29
  54.8 4.2 %while.3 = (s32[]{:T(128)}, f32[2,256,256]{1,2,0:T(8,128)S(1)}, s32[2,2]{1,0:T(2,128)S(1)}, f32[2,2,128,128]{3,2,0,1:T(8,128)S(1)}, s32[]{:T(128)}) while((s32[]{:T(128)}, f32[2,256,256]{1,2,0:T(8,128)S(1)}, s32[2,2]{1,0:T(2,128)S(1)}, f32[2,2,128,128]{3,2,0,1:T(8,128)S(1)}, s32[]{:T(128)}) %tuple.58), condition=%wide.while_cond.1, body=%wide.while_body.1.sunk | while | flops 2 | bytes 786549 | solution.py:37
  59.0 39.3 %custom-call.12 = f32[2,2,128,128]{2,3,1,0:T(8,128)S(1)} custom-call(f32[2,2,128,128]{3,2,1,0:T(8,128)S(1)} %bitcast.137), custom_call_target="InvertDiagBlocksLowerTriangular" | custom-call | tf_op jit(solution)/shard_map/vmap(jit(_solve_triangular))/triangular_solve | solution.py:37
  101.7 2.1 convolution_convert_fusion.2
  104.6 2.1 convolution_convert_fusion.3
  108.7 2.0 fusion.45
  112.8 2.0 fusion.29
  120.2 3.9 %collective-permute-start.8 = (bf16[2,256,128]{1,2,0:T(8,128)(2,1)S(1)}, bf16[2,256,128]{1,2,0:T(8,128)(2,1)S(1)}, u32[]{:S(2)}, u32[]{:S(2)}) collective-permute-start(bf16[2,256,128]{1,2,0:T(8,128)(2,1)S(1)} %bitcast.132), channel_id=1, source_target_pairs={{0,8},{8,16},{16,24},{24,32},{32,40},{40,48},{48,56},{56,64},{64,7... | collective-permute-start | bytes 393224 | tf_op jit(solution)/shard_map/ppermute | solution.py:12
  129.0 3.4 %collective-permute-start = (f32[2,256,128]{2,1,0:T(8,128)S(1)}, f32[2,256,128]{2,1,0:T(8,128)S(1)}, u32[]{:S(2)}, u32[]{:S(2)}) collective-permute-start(f32[2,256,128]{2,1,0:T(8,128)S(1)} %convolution_subtract_fusion.1), channel_id=1, source_target_pairs={{0,8},{8,16},{16,24},{24,32},{32,40},{40,48},{48,56},{56,64},{64,7... | collective-permute-start | bytes 786440 | tf_op jit(solution)/shard_map/ppermute | solution.py:12
  133.2 5.5 %collective-permute-done = f32[2,256,128]{2,1,0:T(8,128)S(1)} collective-permute-done((f32[2,256,128]{2,1,0:T(8,128)S(1)}, f32[2,256,128]{2,1,0:T(8,128)S(1)}, u32[]{:S(2)}, u32[]{:S(2)}) %collective-permute-start) | collective-permute-done | bytes 262176 | tf_op jit(solution)/shard_map/ppermute | solution.py:12
  139.0 5.5 %collective-permute-start.1 = (f32[2,256,128]{2,1,0:T(8,128)S(1)}, f32[2,256,128]{2,1,0:T(8,128)S(1)}, u32[]{:S(2)}, u32[]{:S(2)}) collective-permute-start(f32[2,256,128]{2,1,0:T(8,128)S(1)} %fusion.71), channel_id=1, source_target_pairs={{0,8},{8,16},{16,24},{24,32},{32,40},{40,48},{48,56},{56,64},{64,7... | collective-permute-start | bytes 786440 | tf_op jit(solution)/shard_map/ppermute | solution.py:12
  145.2 1.9 collective-permute-start.9
  147.1 4.9 %collective-permute-done.9 = bf16[2,256,128]{1,2,0:T(8,128)(2,1)S(1)} collective-permute-done((bf16[2,256,128]{1,2,0:T(8,128)(2,1)S(1)}, bf16[2,256,128]{1,2,0:T(8,128)(2,1)S(1)}, u32[]{:S(2)}, u32[]{:S(2)}) %collective-permute-start.9) | collective-permute-done | bytes 131104 | tf_op jit(solution)/shard_map/ppermute | solution.py:12
  152.0 6.1 %collective-permute-start.10 = (bf16[2,256,128]{1,2,0:T(8,128)(2,1)S(1)}, bf16[2,256,128]{1,2,0:T(8,128)(2,1)S(1)}, u32[]{:S(2)}, u32[]{:S(2)}) collective-permute-start(bf16[2,256,128]{1,2,0:T(8,128)(2,1)S(1)} %collective-permute-done.9), channel_id=1, source_target_pairs={{0,8},{8,16},{16,24},{24,32},{32,40},{40,48},{48,56},{56,64},{64,7... | collective-permute-start | bytes 393224 | tf_op jit(solution)/shard_map/ppermute | solution.py:12
  158.6 1.9 collective-permute-start.2
  162.0 6.5 %collective-permute-start.11 = (bf16[2,256,128]{1,2,0:T(8,128)(2,1)S(1)}, bf16[2,256,128]{1,2,0:T(8,128)(2,1)S(1)}, u32[]{:S(2)}, u32[]{:S(2)}) collective-permute-start(bf16[2,256,128]{1,2,0:T(8,128)(2,1)S(1)} %collective-permute-done.10), channel_id=1, source_target_pairs={{0,8},{8,16},{16,24},{24,32},{32,40},{40,48},{48,56},{56,64},{64,7... | collective-permute-start | bytes 393224 | tf_op jit(solution)/shard_map/ppermute | solution.py:12
  168.6 2.5 collective-permute-done.11
  171.0 6.5 %collective-permute-start.12 = (bf16[2,256,128]{1,2,0:T(8,128)(2,1)S(1)}, bf16[2,256,128]{1,2,0:T(8,128)(2,1)S(1)}, u32[]{:S(2)}, u32[]{:S(2)}) collective-permute-start(bf16[2,256,128]{1,2,0:T(8,128)(2,1)S(1)} %collective-permute-done.11), channel_id=1, source_target_pairs={{0,8},{8,16},{16,24},{24,32},{32,40},{40,48},{48,56},{56,64},{64,7... | collective-permute-start | bytes 393224 | tf_op jit(solution)/shard_map/ppermute | solution.py:12
  177.9 1.9 collective-permute-start.3
  180.4 6.0 %collective-permute-start.13 = (bf16[2,256,128]{1,2,0:T(8,128)(2,1)S(1)}, bf16[2,256,128]{1,2,0:T(8,128)(2,1)S(1)}, u32[]{:S(2)}, u32[]{:S(2)}) collective-permute-start(bf16[2,256,128]{1,2,0:T(8,128)(2,1)S(1)} %collective-permute-done.12), channel_id=1, source_target_pairs={{0,8},{8,16},{16,24},{24,32},{32,40},{40,48},{48,56},{56,64},{64,7... | collective-permute-start | bytes 393224 | tf_op jit(solution)/shard_map/ppermute | solution.py:12
  186.5 2.5 collective-permute-done.13
  188.9 6.5 %collective-permute-start.14 = (bf16[2,256,128]{1,2,0:T(8,128)(2,1)S(1)}, bf16[2,256,128]{1,2,0:T(8,128)(2,1)S(1)}, u32[]{:S(2)}, u32[]{:S(2)}) collective-permute-start(bf16[2,256,128]{1,2,0:T(8,128)(2,1)S(1)} %collective-permute-done.13), channel_id=1, source_target_pairs={{0,8},{8,16},{16,24},{24,32},{32,40},{40,48},{48,56},{56,64},{64,7... | collective-permute-start | bytes 393224 | tf_op jit(solution)/shard_map/ppermute | solution.py:12
  195.8 1.9 collective-permute-start.4
  198.4 6.0 %collective-permute-start.15 = (bf16[2,256,128]{1,2,0:T(8,128)(2,1)S(1)}, bf16[2,256,128]{1,2,0:T(8,128)(2,1)S(1)}, u32[]{:S(2)}, u32[]{:S(2)}) collective-permute-start(bf16[2,256,128]{1,2,0:T(8,128)(2,1)S(1)} %collective-permute-done.14), channel_id=1, source_target_pairs={{0,8},{8,16},{16,24},{24,32},{32,40},{40,48},{48,56},{56,64},{64,7... | collective-permute-start | bytes 393224 | tf_op jit(solution)/shard_map/ppermute | solution.py:12
  205.2 4.5 %collective-permute-start.5 = (f32[2,256,128]{2,1,0:T(8,128)S(1)}, f32[2,256,128]{2,1,0:T(8,128)S(1)}, u32[]{:S(2)}, u32[]{:S(2)}) collective-permute-start(f32[2,256,128]{2,1,0:T(8,128)S(1)} %fusion.75), channel_id=1, source_target_pairs={{0,8},{8,16},{16,24},{24,32},{32,40},{40,48},{48,56},{56,64},{64,7... | collective-permute-start | bytes 786440 | tf_op jit(solution)/shard_map/ppermute | solution.py:12
  210.3 4.0 %collective-permute-done.5 = f32[2,256,128]{2,1,0:T(8,128)S(1)} collective-permute-done((f32[2,256,128]{2,1,0:T(8,128)S(1)}, f32[2,256,128]{2,1,0:T(8,128)S(1)}, u32[]{:S(2)}, u32[]{:S(2)}) %collective-permute-start.5) | collective-permute-done | bytes 262176 | tf_op jit(solution)/shard_map/ppermute | solution.py:12
  214.6 6.5 %collective-permute-start.6 = (f32[2,256,128]{2,1,0:T(8,128)S(1)}, f32[2,256,128]{2,1,0:T(8,128)S(1)}, u32[]{:S(2)}, u32[]{:S(2)}) collective-permute-start(f32[2,256,128]{2,1,0:T(8,128)S(1)} %fusion.76), channel_id=1, source_target_pairs={{0,8},{8,16},{16,24},{24,32},{32,40},{40,48},{48,56},{56,64},{64,7... | collective-permute-start | bytes 786440 | tf_op jit(solution)/shard_map/ppermute | solution.py:12
  221.8 5.1 %collective-permute-done.6 = f32[2,256,128]{2,1,0:T(8,128)S(1)} collective-permute-done((f32[2,256,128]{2,1,0:T(8,128)S(1)}, f32[2,256,128]{2,1,0:T(8,128)S(1)}, u32[]{:S(2)}, u32[]{:S(2)}) %collective-permute-start.6) | collective-permute-done | bytes 262176 | tf_op jit(solution)/shard_map/ppermute | solution.py:12
  227.3 6.7 %collective-permute-start.7 = (f32[2,256,128]{2,1,0:T(8,128)S(1)}, f32[2,256,128]{2,1,0:T(8,128)S(1)}, u32[]{:S(2)}, u32[]{:S(2)}) collective-permute-start(f32[2,256,128]{2,1,0:T(8,128)S(1)} %fusion.77), channel_id=1, source_target_pairs={{0,8},{8,16},{16,24},{24,32},{32,40},{40,48},{48,56},{56,64},{64,7... | collective-permute-start | bytes 786440 | tf_op jit(solution)/shard_map/ppermute | solution.py:12
  235.3 2.4 collective-permute-done.7
  241.4 57.0 %reduce-scatter.2.cloned.1.call-done = bf16[256,256]{1,0:T(8,128)(2,1)} async-done(((bf16[256,2048]{1,0:T(8,128)(2,1)}), bf16[256,256]{1,0:T(8,128)(2,1)}) %reduce-scatter.2.cloned.1.call-update) | async-done | bytes 131088 | tf_op jit(solution)/shard_map/reduce_scatter | solution.py:93
  (122 shorter events, 43.2 us)
Async XLA Ops:
  6.5 233.4 %copy-start = (bf16[256,2048]{1,0:T(8,128)(2,1)S(1)}, bf16[256,2048]{1,0:T(8,128)(2,1)}, u32[]{:S(2)}) copy-start(bf16[256,2048]{1,0:T(8,128)(2,1)} %param.12) | copy-start | bytes 3145732
  6.5 95.1 %all-gather.2.cloned.1.call-start = ((), (), s32[]{:S(2)}) async-start(), calls=%async_computation.1 | async-start | bytes 1179648 | tf_op jit(solution)/shard_map/all_gather | solution.py:54
  7.3 291.1 %reduce-scatter.2.cloned.1.call-start = ((), (), s32[]{:S(2)}) async-start(), calls=%async_computation.2 | async-start | bytes 1179648 | tf_op jit(solution)/shard_map/reduce_scatter | solution.py:93
  7.4 47.4 %copy-start.10 = (pred[256,256]{0,1:T(8,128)(4,1)}, pred[256,256]{0,1:T(8,128)(4,1)S(1)}, u32[]{:S(2)}) copy-start(pred[256,256]{0,1:T(8,128)(4,1)S(1)} %get-tuple-element.78) | copy-start | bytes 196612
  7.4 47.4 %copy-start.12 = (pred[256,256]{0,1:T(8,128)(4,1)}, pred[256,256]{0,1:T(8,128)(4,1)S(1)}, u32[]{:S(2)}) copy-start(pred[256,256]{0,1:T(8,128)(4,1)S(1)} %get-tuple-element.77) | copy-start | bytes 196612
  10.4 90.5 %copy-start.13 = (f32[2,256]{1,0:T(2,128)S(1)}, f32[2,256]{1,0:T(2,128)}, u32[]{:S(2)}) copy-start(f32[2,256]{1,0:T(2,128)} %param.14) | copy-start | bytes 6148
  14.8 86.8 %copy-start.2 = (f32[2,256,256]{1,2,0:T(8,128)}, f32[2,256,256]{1,2,0:T(8,128)S(1)}, u32[]{:S(2)}) copy-start(f32[2,256,256]{1,2,0:T(8,128)S(1)} %get-tuple-element.173) | copy-start | bytes 1572868
  98.3 2.1 copy-start.8
  101.6 16.8 %copy-start.1 = (bf16[256,2048]{1,0:T(8,128)(2,1)S(1)}, bf16[256,2048]{1,0:T(8,128)(2,1)}, u32[]{:S(2)}) copy-start(bf16[256,2048]{1,0:T(8,128)(2,1)} %all-gather.2.cloned.1.call-done) | copy-start | bytes 3145732
  112.0 0.8 copy-start.6
  116.6 10.8 %copy-start.9 = (f32[2,2,128,128]{2,3,1,0:T(8,128)S(1)}, f32[2,2,128,128]{2,3,1,0:T(8,128)}, u32[]{:S(2)}) copy-start(f32[2,2,128,128]{2,3,1,0:T(8,128)} %copy-done.8) | copy-start | bytes 786436
  116.6 11.2 %copy-start.5 = (bf16[256,2,128]{2,0,1:T(8,128)(2,1)S(1)}, bf16[256,2,128]{2,0,1:T(8,128)(2,1)}, u32[]{:S(2)}) copy-start(bf16[256,2,128]{2,0,1:T(8,128)(2,1)} %copy.30) | copy-start | bytes 393220
  116.6 15.8 %copy-start.3 = (f32[2,128,256]{1,2,0:T(8,128)S(1)}, f32[2,128,256]{1,2,0:T(8,128)}, u32[]{:S(2)}) copy-start(f32[2,128,256]{1,2,0:T(8,128)} %copy.40) | copy-start | bytes 786436
  116.6 15.8 %copy-start.7 = (f32[2,256,256]{1,2,0:T(8,128)S(1)}, f32[2,256,256]{1,2,0:T(8,128)}, u32[]{:S(2)}) copy-start(f32[2,256,256]{1,2,0:T(8,128)} %fusion.45) | copy-start | bytes 1572868
  116.6 15.8 %copy-start.11 = (pred[256,256]{0,1:T(8,128)(4,1)S(1)}, pred[256,256]{0,1:T(8,128)(4,1)}, u32[]{:S(2)}) copy-start(pred[256,256]{0,1:T(8,128)(4,1)} %copy-done.10) | copy-start | bytes 196612
  118.4 26.1 %copy-start.4 = (bf16[256,2,128]{2,0,1:T(8,128)(2,1)S(1)}, bf16[256,2,128]{2,0,1:T(8,128)(2,1)}, u32[]{:S(2)}) copy-start(bf16[256,2,128]{2,0,1:T(8,128)(2,1)} %copy.29) | copy-start | bytes 393220
  120.2 25.0 %collective-permute-start.8 = (bf16[2,256,128]{1,2,0:T(8,128)(2,1)S(1)}, bf16[2,256,128]{1,2,0:T(8,128)(2,1)S(1)}, u32[]{:S(2)}, u32[]{:S(2)}) collective-permute-start(bf16[2,256,128]{1,2,0:T(8,128)(2,1)S(1)} %bitcast.132), channel_id=1, source_target_pairs={{0,8},{8,16},{16,24},{24,32},{32,40},{40,48},{48,56},{56,64},{64,7... | collective-permute-start | bytes 393224 | tf_op jit(solution)/shard_map/ppermute | solution.py:12
  129.0 9.7 %collective-permute-start = (f32[2,256,128]{2,1,0:T(8,128)S(1)}, f32[2,256,128]{2,1,0:T(8,128)S(1)}, u32[]{:S(2)}, u32[]{:S(2)}) collective-permute-start(f32[2,256,128]{2,1,0:T(8,128)S(1)} %convolution_subtract_fusion.1), channel_id=1, source_target_pairs={{0,8},{8,16},{16,24},{24,32},{32,40},{40,48},{48,56},{56,64},{64,7... | collective-permute-start | bytes 786440 | tf_op jit(solution)/shard_map/ppermute | solution.py:12
  139.0 19.2 %collective-permute-start.1 = (f32[2,256,128]{2,1,0:T(8,128)S(1)}, f32[2,256,128]{2,1,0:T(8,128)S(1)}, u32[]{:S(2)}, u32[]{:S(2)}) collective-permute-start(f32[2,256,128]{2,1,0:T(8,128)S(1)} %fusion.71), channel_id=1, source_target_pairs={{0,8},{8,16},{16,24},{24,32},{32,40},{40,48},{48,56},{56,64},{64,7... | collective-permute-start | bytes 786440 | tf_op jit(solution)/shard_map/ppermute | solution.py:12
  145.2 6.9 %collective-permute-start.9 = (bf16[2,256,128]{1,2,0:T(8,128)(2,1)S(1)}, bf16[2,256,128]{1,2,0:T(8,128)(2,1)S(1)}, u32[]{:S(2)}, u32[]{:S(2)}) collective-permute-start(bf16[2,256,128]{1,2,0:T(8,128)(2,1)S(1)} %collective-permute-done.8), channel_id=1, source_target_pairs={{0,8},{8,16},{16,24},{24,32},{32,40},{40,48},{48,56},{56,64},{64,7... | collective-permute-start | bytes 393224 | tf_op jit(solution)/shard_map/ppermute | solution.py:12
  152.0 10.0 %collective-permute-start.10 = (bf16[2,256,128]{1,2,0:T(8,128)(2,1)S(1)}, bf16[2,256,128]{1,2,0:T(8,128)(2,1)S(1)}, u32[]{:S(2)}, u32[]{:S(2)}) collective-permute-start(bf16[2,256,128]{1,2,0:T(8,128)(2,1)S(1)} %collective-permute-done.9), channel_id=1, source_target_pairs={{0,8},{8,16},{16,24},{24,32},{32,40},{40,48},{48,56},{56,64},{64,7... | collective-permute-start | bytes 393224 | tf_op jit(solution)/shard_map/ppermute | solution.py:12
  158.6 18.9 %collective-permute-start.2 = (f32[2,256,128]{2,1,0:T(8,128)S(1)}, f32[2,256,128]{2,1,0:T(8,128)S(1)}, u32[]{:S(2)}, u32[]{:S(2)}) collective-permute-start(f32[2,256,128]{2,1,0:T(8,128)S(1)} %fusion.72), channel_id=1, source_target_pairs={{0,8},{8,16},{16,24},{24,32},{32,40},{40,48},{48,56},{56,64},{64,7... | collective-permute-start | bytes 786440 | tf_op jit(solution)/shard_map/ppermute | solution.py:12
  162.0 9.0 %collective-permute-start.11 = (bf16[2,256,128]{1,2,0:T(8,128)(2,1)S(1)}, bf16[2,256,128]{1,2,0:T(8,128)(2,1)S(1)}, u32[]{:S(2)}, u32[]{:S(2)}) collective-permute-start(bf16[2,256,128]{1,2,0:T(8,128)(2,1)S(1)} %collective-permute-done.10), channel_id=1, source_target_pairs={{0,8},{8,16},{16,24},{24,32},{32,40},{40,48},{48,56},{56,64},{64,7... | collective-permute-start | bytes 393224 | tf_op jit(solution)/shard_map/ppermute | solution.py:12
  171.0 9.4 %collective-permute-start.12 = (bf16[2,256,128]{1,2,0:T(8,128)(2,1)S(1)}, bf16[2,256,128]{1,2,0:T(8,128)(2,1)S(1)}, u32[]{:S(2)}, u32[]{:S(2)}) collective-permute-start(bf16[2,256,128]{1,2,0:T(8,128)(2,1)S(1)} %collective-permute-done.11), channel_id=1, source_target_pairs={{0,8},{8,16},{16,24},{24,32},{32,40},{40,48},{48,56},{56,64},{64,7... | collective-permute-start | bytes 393224 | tf_op jit(solution)/shard_map/ppermute | solution.py:12
  177.9 17.5 %collective-permute-start.3 = (f32[2,256,128]{2,1,0:T(8,128)S(1)}, f32[2,256,128]{2,1,0:T(8,128)S(1)}, u32[]{:S(2)}, u32[]{:S(2)}) collective-permute-start(f32[2,256,128]{2,1,0:T(8,128)S(1)} %fusion.73), channel_id=1, source_target_pairs={{0,8},{8,16},{16,24},{24,32},{32,40},{40,48},{48,56},{56,64},{64,7... | collective-permute-start | bytes 786440 | tf_op jit(solution)/shard_map/ppermute | solution.py:12
  180.4 8.5 %collective-permute-start.13 = (bf16[2,256,128]{1,2,0:T(8,128)(2,1)S(1)}, bf16[2,256,128]{1,2,0:T(8,128)(2,1)S(1)}, u32[]{:S(2)}, u32[]{:S(2)}) collective-permute-start(bf16[2,256,128]{1,2,0:T(8,128)(2,1)S(1)} %collective-permute-done.12), channel_id=1, source_target_pairs={{0,8},{8,16},{16,24},{24,32},{32,40},{40,48},{48,56},{56,64},{64,7... | collective-permute-start | bytes 393224 | tf_op jit(solution)/shard_map/ppermute | solution.py:12
  188.9 9.4 %collective-permute-start.14 = (bf16[2,256,128]{1,2,0:T(8,128)(2,1)S(1)}, bf16[2,256,128]{1,2,0:T(8,128)(2,1)S(1)}, u32[]{:S(2)}, u32[]{:S(2)}) collective-permute-start(bf16[2,256,128]{1,2,0:T(8,128)(2,1)S(1)} %collective-permute-done.13), channel_id=1, source_target_pairs={{0,8},{8,16},{16,24},{24,32},{32,40},{40,48},{48,56},{56,64},{64,7... | collective-permute-start | bytes 393224 | tf_op jit(solution)/shard_map/ppermute | solution.py:12
  195.8 9.0 %collective-permute-start.4 = (f32[2,256,128]{2,1,0:T(8,128)S(1)}, f32[2,256,128]{2,1,0:T(8,128)S(1)}, u32[]{:S(2)}, u32[]{:S(2)}) collective-permute-start(f32[2,256,128]{2,1,0:T(8,128)S(1)} %fusion.74), channel_id=1, source_target_pairs={{0,8},{8,16},{16,24},{24,32},{32,40},{40,48},{48,56},{56,64},{64,7... | collective-permute-start | bytes 786440 | tf_op jit(solution)/shard_map/ppermute | solution.py:12
  198.4 22.8 %collective-permute-start.15 = (bf16[2,256,128]{1,2,0:T(8,128)(2,1)S(1)}, bf16[2,256,128]{1,2,0:T(8,128)(2,1)S(1)}, u32[]{:S(2)}, u32[]{:S(2)}) collective-permute-start(bf16[2,256,128]{1,2,0:T(8,128)(2,1)S(1)} %collective-permute-done.14), channel_id=1, source_target_pairs={{0,8},{8,16},{16,24},{24,32},{32,40},{40,48},{48,56},{56,64},{64,7... | collective-permute-start | bytes 393224 | tf_op jit(solution)/shard_map/ppermute | solution.py:12
  205.2 9.1 %collective-permute-start.5 = (f32[2,256,128]{2,1,0:T(8,128)S(1)}, f32[2,256,128]{2,1,0:T(8,128)S(1)}, u32[]{:S(2)}, u32[]{:S(2)}) collective-permute-start(f32[2,256,128]{2,1,0:T(8,128)S(1)} %fusion.75), channel_id=1, source_target_pairs={{0,8},{8,16},{16,24},{24,32},{32,40},{40,48},{48,56},{56,64},{64,7... | collective-permute-start | bytes 786440 | tf_op jit(solution)/shard_map/ppermute | solution.py:12
  214.6 12.3 %collective-permute-start.6 = (f32[2,256,128]{2,1,0:T(8,128)S(1)}, f32[2,256,128]{2,1,0:T(8,128)S(1)}, u32[]{:S(2)}, u32[]{:S(2)}) collective-permute-start(f32[2,256,128]{2,1,0:T(8,128)S(1)} %fusion.76), channel_id=1, source_target_pairs={{0,8},{8,16},{16,24},{24,32},{32,40},{40,48},{48,56},{56,64},{64,7... | collective-permute-start | bytes 786440 | tf_op jit(solution)/shard_map/ppermute | solution.py:12
  227.3 10.4 %collective-permute-start.7 = (f32[2,256,128]{2,1,0:T(8,128)S(1)}, f32[2,256,128]{2,1,0:T(8,128)S(1)}, u32[]{:S(2)}, u32[]{:S(2)}) collective-permute-start(f32[2,256,128]{2,1,0:T(8,128)S(1)} %fusion.77), channel_id=1, source_target_pairs={{0,8},{8,16},{16,24},{24,32},{32,40},{40,48},{48,56},{56,64},{64,7... | collective-permute-start | bytes 786440 | tf_op jit(solution)/shard_map/ppermute | solution.py:12
Sparse Core Ops, SparseCore 0:
  9.5 35.6 all-gather.1
  241.5 56.8 reduce-scatter.1
where the time goes:
time: 306 us; the launch traced here: 305 us
  waiting for transfers between devices  85.9 us (28%)
  other arithmetic  80.9 us (26%)
  starting transfers between devices  75.7 us (25%)
  matrix products  33.8 us (11%)
  between operations  14.8 us (5%)
  local copies, waits for them, and re-layouts  13.9 us (5%)
    ppermute x16, starting transfers between devices, from_behind(): return lax.ppermute(shard, axis, pairs)  75.7 us
    reduce_scatter x1, waiting for transfers between devices, shards(): lax.psum_scatter(partial_out.astype(jnp.bfloat16), 'head', scatter_dimens...  57 us
    another operation x2, other arithmetic, block_reflector(): coef = solver(left_tri, qdirs.T, trans=1, lower=True).T  39.9 us
    another operation x1, other arithmetic, block_reflector(): dkey = solver(right_tri, dir_keys, lower=True)  39.3 us
    ppermute x16, waiting for transfers between devices, from_behind(): return lax.ppermute(shard, axis, pairs)  28.1 us
    another operation x20, local copies, waits for them, and re-layouts  8.4 us
  transfers between devices with their start and end apart: 18, of which 10 were waited for; matrix products, arithmetic and copies ran while one was open for 35% of the time, Pallas kernels for 0%

commit v1 on v0

v1 whole, which is shorter than its diff:
```python
import jax
import jax.numpy as jnp
from jax import lax
from jax.experimental import pallas as pl
from jax.experimental.pallas import tpu as pltpu
from jax.sharding import PartitionSpec as P

TOK = 256
DH = 128
SCALE = 1.4426950408889634 / DH**0.5
NEG = -1e30
F32 = jnp.float32
BF16 = jnp.bfloat16
HOP_ROW = 3 * TOK + DH
PACK = HOP_ROW + 16
PAIR = 4 * TOK + DH
VMEM = pl.BlockSpec(memory_space=pltpu.VMEM)
SMEM = pl.BlockSpec(memory_space=pltpu.SMEM)

NN = (((1,), (0,)), ((), ()))
NT = (((1,), (1,)), ((), ()))
TN = (((0,), (0,)), ((), ()))


def dot(a, b, dims=NN):
    return lax.dot_general(a, b, dims, preferred_element_type=F32)


def exact(a, b):
    return lax.dot_general(a, b, NN, precision=lax.Precision.HIGHEST, preferred_element_type=F32)


def call(body, outs, ins, scratch=(), flops=0, smem=0):
    return pl.pallas_call(
        body,
        out_shape=outs,
        in_specs=[SMEM] * smem + [VMEM] * (ins - smem),
        out_specs=jax.tree.map(lambda _: VMEM, outs),
        scratch_shapes=list(scratch),
        compiler_params=pltpu.CompilerParams(vmem_limit_bytes=48 * 2**20),
        cost_estimate=pl.CostEstimate(flops=flops, bytes_accessed=2**20, transcendentals=0),
    )


def lower_inverses(blocks, row, col):
    eye = (row == col).astype(F32)
    same = (row // 8) == (col // 8)
    small = [jnp.where(same, b, 0.0) for b in blocks]
    squares = [exact(s, s) for s in small]
    fourths = [exact(s, s) for s in squares]
    firsts = [exact(eye - s, eye + q) for s, q in zip(small, squares)]
    found = [exact(f, eye + q) for f, q in zip(firsts, fourths)]
    size = 8
    while size < DH:
        off = ((row // (2 * size)) == (col // (2 * size))) & ((row // size) != (col // size))
        left = [exact(x, jnp.where(off, b, 0.0)) for x, b in zip(found, blocks)]
        found = [x - exact(y, x) for x, y in zip(found, left)]
        size *= 2
    return found


def directions_kernel(dirs_ref, beta_ref, w_ref, t_ref, u_ref, y_ref, a_ref):
    row = lax.broadcasted_iota(jnp.int32, (TOK, TOK), 0)
    col = lax.broadcasted_iota(jnp.int32, (TOK, TOK), 1)
    strict = row > col
    r, c = row[:DH, :DH], col[:DH, :DH]
    dirs, lows, betas = [], [], []
    for h in range(2):
        d = dirs_ref[:, h * DH : (h + 1) * DH].astype(F32)
        d = d * lax.rsqrt(jnp.sum(d * d, axis=1, keepdims=True) + 1e-6)
        w = d.astype(BF16)
        dirs.append(w)
        beta = beta_ref[h : h + 1, :]
        column = jnp.sum(jnp.where(row == col, beta, 0.0), axis=1, keepdims=True)
        lows.append(jnp.where(strict, dot(w, w, NT) * column, 0.0))
        betas.append(beta)
    corners = []
    for low in lows:
        corners += [low[:DH, :DH], low[DH:, DH:]]
    found = lower_inverses(corners, r, c)
    for h in range(2):
        first, second = found[2 * h], found[2 * h + 1]
        cross = -exact(second, exact(lows[h][DH:, :DH], first))
        upper = jnp.concatenate([first, jnp.zeros((DH, DH), F32)], axis=1)
        lower = jnp.concatenate([cross, second], axis=1)
        t = (jnp.concatenate([upper, lower], axis=0) * betas[h]).astype(BF16)
        w = dirs[h]
        u = dot(t, w, TN).astype(BF16)
        w_ref[h] = w
        t_ref[h] = t
        u_ref[h] = u
        y_ref[h] = dot(t, w).astype(BF16)
        eye = (r == c).astype(F32)
        a_ref[h] = (eye - dot(u, w, TN)).astype(BF16)


def project_kernel(
    at_ref, hop_ref, x_ref, wq_ref, wk_ref, wv_ref, w_ref, u_ref, y_ref, a_ref,
    p0_ref, p1_ref, q_ref, k_ref, v_ref,
):
    def product(weights):
        total = dot(x_ref[0], weights[0:256, :])
        for p in range(1, 8):
            total += dot(x_ref[p], weights[p * 256 : (p + 1) * 256, :])
        return total.astype(BF16)

    query, key, value = product(wq_ref), product(wk_ref), product(wv_ref)
    for h in range(2):
        cut = slice(h * DH, (h + 1) * DH)
        q_ref[h] = query[:, cut]
        k_ref[h] = key[:, cut]
        v_ref[h] = value[:, cut]
    row = lax.broadcasted_iota(jnp.int32, (TOK, TOK), 0)
    col = lax.broadcasted_iota(jnp.int32, (TOK, TOK), 1)
    hops = hop_ref[0].astype(F32)
    for j, p_ref in enumerate((p0_ref, p1_ref)):
        h = lax.rem(at_ref[0] + j, 2)
        q, k, w = q_ref[h], k_ref[h], w_ref[h]
        qdirs = jnp.where(row >= col, dot(q, w, NT), 0.0).astype(BF16)
        keydirs = jnp.where(col > row, dot(k, w, NT), 0.0).astype(BF16)
        qhat = q.astype(F32) - dot(qdirs, y_ref[h])
        p_ref[0:TOK] = (qhat * SCALE).astype(BF16)
        p_ref[TOK : 2 * TOK] = (k.astype(F32) - dot(keydirs, u_ref[h])).astype(BF16)
        p_ref[2 * TOK : 3 * TOK] = v_ref[h]
        p_ref[3 * TOK : HOP_ROW] = a_ref[h]
        p_ref[HOP_ROW:PACK] = jnp.full((16, DH), hops, F32).astype(BF16)


def own_kernel(q_ref, k_ref, v_ref, w_ref, t_ref, acc_ref, lse_ref):
    row = lax.broadcasted_iota(jnp.int32, (TOK, TOK), 0)
    col = lax.broadcasted_iota(jnp.int32, (TOK, TOK), 1)
    for h in range(2):
        q, k, w = q_ref[h], k_ref[h], w_ref[h]
        qdirs = jnp.where(row >= col, dot(q, w, NT), 0.0).astype(BF16)
        dirkeys = jnp.where(row > col, dot(w, k, NT), 0.0).astype(BF16)
        coef = dot(qdirs, t_ref[h]).astype(BF16)
        own = (dot(q, k, NT) - dot(coef, dirkeys)) * SCALE
        own = jnp.where(row >= col, own, NEG)
        top = jnp.max(own, axis=1, keepdims=True)
        prob = jnp.exp2(own - top)
        total = jnp.sum(prob, axis=1, keepdims=True)
        acc_ref[h] = dot(prob.astype(BF16), v_ref[h]) / total
        lse_ref[h] = jnp.broadcast_to(top + jnp.log2(total), (TOK, DH))


def pair_kernel(at_ref, r0_ref, r1_ref, q_ref, pair_ref, hop_ref):
    swapped = at_ref[0] == 1

    def part(low, high):
        a, b = r0_ref[low:high], r1_ref[low:high]
        return jnp.where(swapped, b, a), jnp.where(swapped, a, b)

    q_even, q_odd = part(0, TOK)
    k_even, k_odd = part(TOK, 2 * TOK)
    v_even, v_odd = part(2 * TOK, 3 * TOK)
    a_even, a_odd = part(3 * TOK, HOP_ROW)
    h_even, h_odd = part(HOP_ROW, PACK)
    pair_ref[0:TOK] = dot(k_even, a_odd, NT).astype(BF16)
    pair_ref[TOK : 2 * TOK] = k_odd
    pair_ref[2 * TOK : 3 * TOK] = v_even
    pair_ref[3 * TOK : 4 * TOK] = v_odd
    pair_ref[4 * TOK : PAIR] = dot(a_odd, a_even).astype(BF16)
    q_ref[0, 0] = q_even
    q_ref[0, 1] = q_odd
    q_ref[1, 0] = q_even
    q_ref[1, 1] = dot(q_odd, a_even).astype(BF16)
    q_ref[2, 0] = k_even
    q_ref[2, 1] = v_even
    hop_ref[0] = h_even.astype(F32)
    hop_ref[1] = h_odd.astype(F32)


def mix_kernel(at_ref, a_ref, b_ref, out_ref):
    @pl.when(at_ref[1] == 0)
    def _():
        out_ref[...] = a_ref[...]

    @pl.when(at_ref[1] == 1)
    def _():
        out_ref[...] = b_ref[...]


def window_kernel(
    at_ref, q_ref, hop_ref, z1_ref, z2_ref, s1_ref, s2_ref, o0_ref, o1_ref, scores
):
    keys = (s1_ref, z1_ref, s2_ref, z2_ref)
    pair = at_ref[2]
    col = lax.broadcasted_iota(jnp.int32, (1, 2 * TOK), 1)
    odd_key = col >= TOK
    for j, out_ref in enumerate((o0_ref, o1_ref)):
        i = lax.rem(at_ref[0] + j, 2)
        hops = hop_ref[i, 0:1, 0:1]
        inside = dot(q_ref[0, i], q_ref[2, 0], NT) + jnp.where(i == 1, 0.0, NEG)
        scores[:, 0:TOK] = inside
        top = jnp.max(inside, axis=1, keepdims=True)
        q = q_ref[1, i]
        for d in range(1, 5):
            s = dot(q, keys[d - 1][0 : 2 * TOK], NT)
            distance = 2 * d + i - odd_key.astype(jnp.int32)
            valid = (distance.astype(F32) <= hops) & (pair >= d)
            s = s + jnp.where(valid, 0.0, NEG)
            scores[:, (2 * d - 1) * TOK : (2 * d + 1) * TOK] = s
            top = jnp.maximum(top, jnp.max(s, axis=1, keepdims=True))
            if d < 4:
                q = dot(q, keys[d - 1][4 * TOK : PAIR]).astype(BF16)
        prob = jnp.exp2(scores[:, 0:TOK] - top)
        total = jnp.sum(prob, axis=1, keepdims=True)
        acc = dot(prob.astype(BF16), q_ref[2, 1])
        for d in range(1, 5):
            prob = jnp.exp2(scores[:, (2 * d - 1) * TOK : (2 * d + 1) * TOK] - top)
            total += jnp.sum(prob, axis=1, keepdims=True)
            acc += dot(prob.astype(BF16), keys[d - 1][2 * TOK : 4 * TOK])
        lse = jnp.broadcast_to(top + jnp.log2(total), (TOK, DH))
        high = lse.astype(BF16).astype(F32)
        lane = lax.broadcasted_iota(jnp.int32, (TOK, DH), 1)
        out_ref[:, 0:DH] = (acc / total).astype(BF16)
        out_ref[:, DH:] = jnp.where(lane < DH // 2, high, lse - high).astype(BF16)


def output_kernel(at_ref, g0_ref, g1_ref, acc_ref, lse_ref, wo_ref, out_ref):
    swapped = at_ref[0] == 1
    parts = []
    for h in range(2):
        a, b = (g0_ref, g1_ref) if h == 0 else (g1_ref, g0_ref)
        got = jnp.where(swapped, b[...], a[...]).astype(F32)
        far = got[:, DH : DH + 1] + got[:, DH + DH // 2 : DH + DH // 2 + 1]
        own = lse_ref[h, :, 0:1]
        top = jnp.maximum(own, far)
        mine, theirs = jnp.exp2(own - top), jnp.exp2(far - top)
        mixed = (acc_ref[h] * mine + got[:, :DH] * theirs) / (mine + theirs)
        parts.append(mixed.astype(BF16))
    attended = jnp.concatenate(parts, axis=1)
    for p in range(8):
        out_ref[p] = dot(attended, wo_ref[:, p * 256 : (p + 1) * 256]).astype(BF16)


def sum_kernel(x_ref, out_ref):
    total = x_ref[0].astype(F32)
    for p in range(1, 8):
        total += x_ref[p].astype(F32)
    out_ref[...] = total.astype(BF16)


def regroup_pairs(j, rows, cross, groups):
    pairs = []
    for z in range(rows):
        for x in range(4):
            for y in range(groups):
                for c in range(2):
                    i = (x + j) % 2
                    pairs.append(((z * 4 + x) * cross + y * 2 + c, (z * 4 + 2 * c + i) * cross + y * 2 + x // 2))
    return pairs


def shape(dims, dtype=BF16):
    return jax.ShapeDtypeStruct(dims, dtype)


def shards(inputs, w_query, w_key, w_value, w_out, reflect_dir, strength, hop_count):
    both = ("ctx", "head")
    z = lax.axis_index("ctx") // 4
    x = lax.axis_index("ctx") % 4
    c = lax.axis_index("head") % 2
    at = jnp.stack([x % 2, c, 2 * z + c]).astype(jnp.int32)
    there = [regroup_pairs(j, 16, 8, 4) for j in range(2)]
    back = [[(b, a) for a, b in pairs] for pairs in there]
    down = [(b, b + 4) for b in range(60)]
    twin = [(h, h ^ 1) for h in range(8)]

    w, t, u, y, a = call(
        directions_kernel,
        [shape((2, TOK, DH)), shape((2, TOK, TOK)), shape((2, TOK, DH)), shape((2, TOK, DH)), shape((2, DH, DH))],
        2, flops=2**32,
    )(reflect_dir, strength)
    gathered = lax.all_to_all(jnp.broadcast_to(inputs[None], (8, TOK, 256)), "head", 0, 0)
    p0, p1, q, k, v = call(
        project_kernel,
        [shape((PACK, DH)), shape((PACK, DH))] + [shape((2, TOK, DH))] * 3,
        10, smem=2, flops=2**30,
    )(at, hop_count, gathered, w_query, w_key, w_value, w, u, y, a)
    r0 = lax.ppermute(p0, both, there[0])
    r1 = lax.ppermute(p1, both, there[1])
    acc, lse = call(
        own_kernel, [shape((2, TOK, DH), F32), shape((2, TOK, DH), F32)], 5, flops=2**31
    )(q, k, v, w, t)
    qs, own_pair, hops = call(
        pair_kernel,
        [shape((3, 2, TOK, DH)), shape((PAIR, DH)), shape((2, 16, DH), F32)],
        3, smem=1, flops=2**28,
    )(at, r0, r1)
    mix = call(mix_kernel, shape((PAIR, DH)), 3, smem=1, flops=2**27)
    z1 = lax.ppermute(own_pair, "ctx", down)
    z2 = lax.ppermute(z1, "ctx", down)
    s1 = lax.ppermute(mix(at, own_pair, z1), "head", twin)
    s2 = lax.ppermute(mix(at, z1, z2), "head", twin)
    o0, o1 = call(
        window_kernel,
        [shape((TOK, 2 * DH)), shape((TOK, 2 * DH))],
        7, smem=1, flops=2**30,
        scratch=[pltpu.VMEM((TOK, 9 * TOK), F32)],
    )(at, qs, hops, z1, z2, s1, s2)
    g0 = lax.ppermute(o0, both, back[0])
    g1 = lax.ppermute(o1, both, back[1])
    partial = call(output_kernel, shape((8, TOK, 256)), 6, smem=1, flops=2**29)(at, g0, g1, acc, lse, w_out)
    pieces = lax.all_to_all(partial, "head", 0, 0)
    return call(sum_kernel, shape((TOK, 256)), 1)(pieces)


def solution(mesh):
    placed = (
        P("ctx", "head"),
        P(None, "head"),
        P(None, "head"),
        P(None, "head"),
        P("head", None),
        P("ctx", "head"),
        P("head", "ctx"),
        P("ctx"),
    )
    return jax.shard_map(
        shards, mesh=mesh, in_specs=placed, out_specs=P("ctx", "head"), check_vma=False
    )
```

time: 306 us -> 102 us (0.33)
  the two profiles are of different devices: /device:TPU:6 before, /device:TPU:390 now
where the time goes in v1:
time: 102 us; the launch traced here: 101 us
  waiting for transfers between devices  31.7 us (31%)
  starting transfers between devices  28.8 us (28%)
  blocking collectives  18.5 us (18%)
  Pallas kernels  14.7 us (14%)
  local copies, waits for them, and re-layouts  6.87 us (7%)
    all_to_all x1, blocking collectives, shards(): pieces = lax.all_to_all(partial, 'head', 0, 0)  18.5 us
    all_to_all x1, waiting for transfers between devices, shards(): lax.all_to_all(jnp.broadcast_to(inputs[None], (8, TOK, 256)), 'head', 0, 0)  8.01 us
    ppermute x1, waiting for transfers between devices, shards(): z1 = lax.ppermute(own_pair, 'ctx', down)  6.89 us
    ppermute x1, starting transfers between devices, shards(): g0 = lax.ppermute(o0, both, back[0])  6.68 us
    ppermute x1, waiting for transfers between devices, shards(): z2 = lax.ppermute(z1, 'ctx', down)  5.39 us
    unnamed x20, local copies, waits for them, and re-layouts  4.91 us
    all_to_all x1, starting transfers between devices, shards(): lax.all_to_all(jnp.broadcast_to(inputs[None], (8, TOK, 256)), 'head', 0, 0)  4.47 us
    ppermute x1, starting transfers between devices, shards(): r1 = lax.ppermute(p1, both, there[1])  4.45 us
  transfers between devices with their start and end apart: 9, of which 7 were waited for; matrix products, arithmetic and copies ran while one was open for 0% of the time, Pallas kernels for 7%

profile of v1, /device:TPU:390, one launch (start us, length us, event | category | flops | bytes accessed | tf_op | source)
XLA Modules:
  0.0 101.5 jit_solution(3583326217408985799)
XLA Ops:
  0.0 2.0 %broadcast_in_dim.2 = bf16[8,256,256]{2,1,0:T(8,128)(2,1)} broadcast(bf16[256,256]{1,0:T(8,128)(2,1)} %param.8), dimensions={1,2} | broadcast | bytes 1179648 | tf_op jit(solution)/shard_map/broadcast_in_dim | solution.py:275
  2.0 4.5 %all-to-all-start = ((bf16[8,256,256]{2,1,0:T(8,128)(2,1)}), bf16[8,256,256]{2,1,0:T(8,128)(2,1)S(1)}, u32[]{:S(2)}, u32[]{:S(2)}) async-start(bf16[8,256,256]{2,1,0:T(8,128)(2,1)} %broadcast_in_dim.2), calls=%async_computation | async-start | bytes 2097152 | tf_op jit(solution)/shard_map/all_to_all | solution.py:275
  7.2 0.6 copy-done.7
  7.8 0.9 copy-done.6
  8.7 4.4 %shard_map.82 = (bf16[2,256,128]{2,1,0:T(8,128)(2,1)S(1)}, bf16[2,256,256]{2,1,0:T(8,128)(2,1)S(1)}, bf16[2,256,128]{2,1,0:T(8,128)(2,1)S(1)}, bf16[2,256,128]{2,1,0:T(8,128)(2,1)S(1)}, bf16[2,128,128]{2,1,0:T(8,128)(2,1)S(1)}) custom-call(bf16[256,256]{1,0:T(8,128)(2,1)S(1)} %copy-done.6, f32[2,256]{1,0:T(2,128)S(1)} %copy-done.7), custom_call_target="tpu_custom_call" | custom-call | flops 4294967296 | bytes 1048576 | tf_op jit(solution)/shard_map/pallas_call | solution.py:270
  13.1 0.6 copy-done.4
  13.7 0.7 copy-done.8
  14.4 8.0 %all-to-all-done.x_ref = bf16[8,256,256]{2,1,0:T(8,128)(2,1)S(1)} async-done(((bf16[8,256,256]{2,1,0:T(8,128)(2,1)}), bf16[8,256,256]{2,1,0:T(8,128)(2,1)S(1)}, u32[]{:S(2)}, u32[]{:S(2)}) %all-to-all-start) | async-done | bytes 1048608 | tf_op jit(solution)/shard_map/all_to_all | solution.py:275
  22.4 1.2 %copy-done.2 = bf16[2048,256]{1,0:T(8,128)(2,1)S(1)} copy-done((bf16[2048,256]{1,0:T(8,128)(2,1)S(1)}, bf16[2048,256]{1,0:T(8,128)(2,1)}, u32[]{:S(2)}) %copy-start.2) | copy-done | bytes 1048600
  23.6 0.8 copy-done.5
  24.5 1.9 %shard_map.83 = (bf16[912,128]{1,0:T(8,128)(2,1)S(1)}, bf16[912,128]{1,0:T(8,128)(2,1)S(1)}, bf16[2,256,128]{2,1,0:T(8,128)(2,1)S(1)}, bf16[2,256,128]{2,1,0:T(8,128)(2,1)S(1)}, bf16[2,256,128]{2,1,0:T(8,128)(2,1)S(1)}) custom-call(s32[3]{0:T(128)S(1)} %pad_add_fusion.at_ref, s32[1]{0:T(128)S(6)} %copy.9.hop_ref, ...), custom_call_target="tpu_custom_call" | custom-call | flops 1073741824 | bytes 1048576 | tf_op jit(solution)/shard_map/pallas_call | solution.py:276
  26.4 2.6 %collective-permute-start = (bf16[912,128]{1,0:T(8,128)(2,1)S(1)}, bf16[912,128]{1,0:T(8,128)(2,1)S(1)}, u32[]{:S(2)}, u32[]{:S(2)}) collective-permute-start(bf16[912,128]{1,0:T(8,128)(2,1)S(1)} %get-tuple-element.26), channel_id=1, source_target_pairs={{0,0},{1,16},{2,2},{3,18},{4,4},{5,20},{6,6},{7,22},{8,8},{9,24},{... | collective-permute-start | bytes 700424 | tf_op jit(solution)/shard_map/ppermute | solution.py:281
  29.0 4.5 %collective-permute-start.1 = (bf16[912,128]{1,0:T(8,128)(2,1)S(1)}, bf16[912,128]{1,0:T(8,128)(2,1)S(1)}, u32[]{:S(2)}, u32[]{:S(2)}) collective-permute-start(bf16[912,128]{1,0:T(8,128)(2,1)S(1)} %get-tuple-element.27), channel_id=1, source_target_pairs={{0,8},{1,24},{2,10},{3,26},{4,12},{5,28},{6,14},{7,30},{8,0},{9,16... | collective-permute-start | bytes 700424 | tf_op jit(solution)/shard_map/ppermute | solution.py:282
  33.4 4.1 %collective-permute-done.r0_ref = bf16[912,128]{1,0:T(8,128)(2,1)S(1)} collective-permute-done((bf16[912,128]{1,0:T(8,128)(2,1)S(1)}, bf16[912,128]{1,0:T(8,128)(2,1)S(1)}, u32[]{:S(2)}, u32[]{:S(2)}) %collective-permute-start) | collective-permute-done | bytes 233504 | tf_op jit(solution)/shard_map/ppermute | solution.py:281
  37.5 1.3 %collective-permute-done.1.r1_ref = bf16[912,128]{1,0:T(8,128)(2,1)S(1)} collective-permute-done((bf16[912,128]{1,0:T(8,128)(2,1)S(1)}, bf16[912,128]{1,0:T(8,128)(2,1)S(1)}, u32[]{:S(2)}, u32[]{:S(2)}) %collective-permute-start.1) | collective-permute-done | bytes 233504 | tf_op jit(solution)/shard_map/ppermute | solution.py:282
  38.9 0.8 shard_map.84
  39.7 2.9 %collective-permute-start.2 = (bf16[1152,128]{1,0:T(8,128)(2,1)S(1)}, bf16[1152,128]{1,0:T(8,128)(2,1)S(1)}, u32[]{:S(2)}, u32[]{:S(2)}) collective-permute-start(bf16[1152,128]{1,0:T(8,128)(2,1)S(1)} %get-tuple-element.30.a_ref), channel_id=1, source_target_pairs={{0,32},{8,40},{16,48},{24,56},{32,64},{40,72},{48,80},{56,88},{64,... | collective-permute-start | bytes 884744 | tf_op jit(solution)/shard_map/ppermute | solution.py:292
  42.6 6.9 %collective-permute-done.2.b_ref.a_ref.z1_ref = bf16[1152,128]{1,0:T(8,128)(2,1)S(1)} collective-permute-done((bf16[1152,128]{1,0:T(8,128)(2,1)S(1)}, bf16[1152,128]{1,0:T(8,128)(2,1)S(1)}, u32[]{:S(2)}, u32[]{:S(2)}) %collective-permute-start.2) | collective-permute-done | bytes 294944 | tf_op jit(solution)/shard_map/ppermute | solution.py:292
  49.5 1.9 %collective-permute-start.3 = (bf16[1152,128]{1,0:T(8,128)(2,1)S(1)}, bf16[1152,128]{1,0:T(8,128)(2,1)S(1)}, u32[]{:S(2)}, u32[]{:S(2)}) collective-permute-start(bf16[1152,128]{1,0:T(8,128)(2,1)S(1)} %collective-permute-done.2.b_ref.a_ref.z1_ref), channel_id=1, source_target_pairs={{0,32},{8,40},{16,48},{24,56},{32,64},{40,72},{48,80},{56,88},{64,... | collective-permute-start | bytes 884744 | tf_op jit(solution)/shard_map/ppermute | solution.py:293
  51.4 0.6 shard_map.85
  52.0 1.9 %collective-permute-start.4 = (bf16[1152,128]{1,0:T(8,128)(2,1)S(1)}, bf16[1152,128]{1,0:T(8,128)(2,1)S(1)}, u32[]{:S(2)}, u32[]{:S(2)}) collective-permute-start(bf16[1152,128]{1,0:T(8,128)(2,1)S(1)} %shard_map.85), channel_id=1, source_target_pairs={{0,1},{1,0},{2,3},{3,2},{4,5},{5,4},{6,7},{7,6},{8,9},{9,8},{10,11... | collective-permute-start | bytes 884744 | tf_op jit(solution)/shard_map/ppermute | solution.py:294
  53.9 5.4 %collective-permute-done.3.b_ref.z2_ref = bf16[1152,128]{1,0:T(8,128)(2,1)S(1)} collective-permute-done((bf16[1152,128]{1,0:T(8,128)(2,1)S(1)}, bf16[1152,128]{1,0:T(8,128)(2,1)S(1)}, u32[]{:S(2)}, u32[]{:S(2)}) %collective-permute-start.3) | collective-permute-done | bytes 294944 | tf_op jit(solution)/shard_map/ppermute | solution.py:293
  59.9 1.9 %collective-permute-start.5 = (bf16[1152,128]{1,0:T(8,128)(2,1)S(1)}, bf16[1152,128]{1,0:T(8,128)(2,1)S(1)}, u32[]{:S(2)}, u32[]{:S(2)}) collective-permute-start(bf16[1152,128]{1,0:T(8,128)(2,1)S(1)} %shard_map.86), channel_id=1, source_target_pairs={{0,1},{1,0},{2,3},{3,2},{4,5},{5,4},{6,7},{7,6},{8,9},{9,8},{10,11... | collective-permute-start | bytes 884744 | tf_op jit(solution)/shard_map/ppermute | solution.py:295
  61.8 1.5 %collective-permute-done.5.s2_ref = bf16[1152,128]{1,0:T(8,128)(2,1)S(1)} collective-permute-done((bf16[1152,128]{1,0:T(8,128)(2,1)S(1)}, bf16[1152,128]{1,0:T(8,128)(2,1)S(1)}, u32[]{:S(2)}, u32[]{:S(2)}) %collective-permute-start.5) | collective-permute-done | bytes 294944 | tf_op jit(solution)/shard_map/ppermute | solution.py:295
  63.4 3.4 %shard_map.87 = (bf16[256,256]{1,0:T(8,128)(2,1)S(1)}, bf16[256,256]{1,0:T(8,128)(2,1)S(1)}) custom-call(s32[3]{0:T(128)S(1)} %pad_add_fusion.at_ref, bf16[3,2,256,128]{3,2,1,0:T(8,128)(2,1)S(1)} %get-tuple-element.28.q_ref, f32[2,16,128]{2,1,0:T(8,128)S(1)} %get-tuple-element.29.hop_ref, bf16[1152,128]{1,0:T(8,128)(2,1)S(1)} %collective-permute-done.2.b_ref.a_ref.z1_ref, ...), custom_call_target="tpu_custom_call" | custom-call | flops 1073741824 | bytes 1048576 | tf_op jit(solution)/shard_map/pallas_call | solution.py:296
  66.7 6.7 %collective-permute-start.6 = (bf16[256,256]{1,0:T(8,128)(2,1)S(1)}, bf16[256,256]{1,0:T(8,128)(2,1)S(1)}, u32[]{:S(2)}, u32[]{:S(2)}) collective-permute-start(bf16[256,256]{1,0:T(8,128)(2,1)S(1)} %get-tuple-element.31), channel_id=1, source_target_pairs={{0,0},{16,1},{2,2},{18,3},{4,4},{20,5},{6,6},{22,7},{8,8},{24,9},{... | collective-permute-start | bytes 393224 | tf_op jit(solution)/shard_map/ppermute | solution.py:302
  73.4 1.9 %collective-permute-start.7 = (bf16[256,256]{1,0:T(8,128)(2,1)S(1)}, bf16[256,256]{1,0:T(8,128)(2,1)S(1)}, u32[]{:S(2)}, u32[]{:S(2)}) collective-permute-start(bf16[256,256]{1,0:T(8,128)(2,1)S(1)} %get-tuple-element.32), channel_id=1, source_target_pairs={{8,0},{24,1},{10,2},{26,3},{12,4},{28,5},{14,6},{30,7},{0,8},{16,9... | collective-permute-start | bytes 393224 | tf_op jit(solution)/shard_map/ppermute | solution.py:303
  75.4 1.1 %shard_map.88 = (f32[2,256,128]{2,1,0:T(8,128)S(1)}, f32[2,256,128]{2,1,0:T(8,128)S(1)}) custom-call(bf16[2,256,128]{2,1,0:T(8,128)(2,1)S(1)} %get-tuple-element.33.q_ref, bf16[2,256,128]{2,1,0:T(8,128)(2,1)S(1)} %get-tuple-element.34.k_ref, bf16[2,256,128]{2,1,0:T(8,128)(2,1)S(1)} %get-tuple-element.35.v_ref, ...), custom_call_target="tpu_custom_call" | custom-call | flops 2147483648 | bytes 1048576 | tf_op jit(solution)/shard_map/pallas_call | solution.py:283
  76.5 4.4 %collective-permute-done.7.g1_ref = bf16[256,256]{1,0:T(8,128)(2,1)S(1)} collective-permute-done((bf16[256,256]{1,0:T(8,128)(2,1)S(1)}, bf16[256,256]{1,0:T(8,128)(2,1)S(1)}, u32[]{:S(2)}, u32[]{:S(2)}) %collective-permute-start.7) | collective-permute-done | bytes 131104 | tf_op jit(solution)/shard_map/ppermute | solution.py:303
  80.9 1.2 %shard_map.89 = bf16[8,256,256]{2,1,0:T(8,128)(2,1)S(1)} custom-call(s32[3]{0:T(128)S(1)} %pad_add_fusion.at_ref, bf16[256,256]{1,0:T(8,128)(2,1)S(1)} %collective-permute-done.6.g0_ref, bf16[256,256]{1,0:T(8,128)(2,1)S(1)} %collective-permute-done.7.g1_ref, f32[2,256,128]{2,1,0:T(8,128)S(1)} %get-tuple-element.37.acc_ref, ...), custom_call_target="tpu_custom_call" | custom-call | flops 536870912 | bytes 1048576 | tf_op jit(solution)/shard_map/pallas_call | solution.py:304
  82.2 18.5 %all_to_all.10.x_ref = bf16[8,256,256]{2,1,0:T(8,128)(2,1)S(1)} all-to-all(bf16[8,256,256]{2,1,0:T(8,128)(2,1)S(1)} %shard_map.89), channel_id=1, replica_groups=mesh['ctx'=64,'head'=8] {'head'}, dimensions={0} | all-to-all | bytes 2097152 | tf_op jit(solution)/shard_map/all_to_all | solution.py:305
  100.7 0.8 shard_map.90
  (18 shorter events, 0.7 us)
Async XLA Ops:
  2.0 20.4 %all-to-all-start = ((bf16[8,256,256]{2,1,0:T(8,128)(2,1)}), bf16[8,256,256]{2,1,0:T(8,128)(2,1)S(1)}, u32[]{:S(2)}, u32[]{:S(2)}) async-start(bf16[8,256,256]{2,1,0:T(8,128)(2,1)} %broadcast_in_dim.2), calls=%async_computation | async-start | bytes 2097152 | tf_op jit(solution)/shard_map/all_to_all | solution.py:275
  7.1 0.7 copy-start.7
  7.8 0.9 copy-start.6
  8.7 13.7 %copy-start = (bf16[2048,256]{1,0:T(8,128)(2,1)S(1)}, bf16[2048,256]{1,0:T(8,128)(2,1)}, u32[]{:S(2)}) copy-start(bf16[2048,256]{1,0:T(8,128)(2,1)} %wq_ref.1) | copy-start | bytes 3145732
  8.7 13.7 %copy-start.1 = (bf16[2048,256]{1,0:T(8,128)(2,1)S(1)}, bf16[2048,256]{1,0:T(8,128)(2,1)}, u32[]{:S(2)}) copy-start(bf16[2048,256]{1,0:T(8,128)(2,1)} %wk_ref.1) | copy-start | bytes 3145732
  13.1 0.6 copy-start.4
  13.7 0.7 copy-start.8
  22.4 1.2 %copy-start.2 = (bf16[2048,256]{1,0:T(8,128)(2,1)S(1)}, bf16[2048,256]{1,0:T(8,128)(2,1)}, u32[]{:S(2)}) copy-start(bf16[2048,256]{1,0:T(8,128)(2,1)} %wv_ref.1) | copy-start | bytes 3145732
  23.6 0.8 copy-start.5
  26.4 11.1 %collective-permute-start = (bf16[912,128]{1,0:T(8,128)(2,1)S(1)}, bf16[912,128]{1,0:T(8,128)(2,1)S(1)}, u32[]{:S(2)}, u32[]{:S(2)}) collective-permute-start(bf16[912,128]{1,0:T(8,128)(2,1)S(1)} %get-tuple-element.26), channel_id=1, source_target_pairs={{0,0},{1,16},{2,2},{3,18},{4,4},{5,20},{6,6},{7,22},{8,8},{9,24},{... | collective-permute-start | bytes 700424 | tf_op jit(solution)/shard_map/ppermute | solution.py:281
  29.0 9.9 %collective-permute-start.1 = (bf16[912,128]{1,0:T(8,128)(2,1)S(1)}, bf16[912,128]{1,0:T(8,128)(2,1)S(1)}, u32[]{:S(2)}, u32[]{:S(2)}) collective-permute-start(bf16[912,128]{1,0:T(8,128)(2,1)S(1)} %get-tuple-element.27), channel_id=1, source_target_pairs={{0,8},{1,24},{2,10},{3,26},{4,12},{5,28},{6,14},{7,30},{8,0},{9,16... | collective-permute-start | bytes 700424 | tf_op jit(solution)/shard_map/ppermute | solution.py:282
  39.7 9.8 %collective-permute-start.2 = (bf16[1152,128]{1,0:T(8,128)(2,1)S(1)}, bf16[1152,128]{1,0:T(8,128)(2,1)S(1)}, u32[]{:S(2)}, u32[]{:S(2)}) collective-permute-start(bf16[1152,128]{1,0:T(8,128)(2,1)S(1)} %get-tuple-element.30.a_ref), channel_id=1, source_target_pairs={{0,32},{8,40},{16,48},{24,56},{32,64},{40,72},{48,80},{56,88},{64,... | collective-permute-start | bytes 884744 | tf_op jit(solution)/shard_map/ppermute | solution.py:292
  49.5 9.8 %collective-permute-start.3 = (bf16[1152,128]{1,0:T(8,128)(2,1)S(1)}, bf16[1152,128]{1,0:T(8,128)(2,1)S(1)}, u32[]{:S(2)}, u32[]{:S(2)}) collective-permute-start(bf16[1152,128]{1,0:T(8,128)(2,1)S(1)} %collective-permute-done.2.b_ref.a_ref.z1_ref), channel_id=1, source_target_pairs={{0,32},{8,40},{16,48},{24,56},{32,64},{40,72},{48,80},{56,88},{64,... | collective-permute-start | bytes 884744 | tf_op jit(solution)/shard_map/ppermute | solution.py:293
  52.0 9.8 %collective-permute-start.4 = (bf16[1152,128]{1,0:T(8,128)(2,1)S(1)}, bf16[1152,128]{1,0:T(8,128)(2,1)S(1)}, u32[]{:S(2)}, u32[]{:S(2)}) collective-permute-start(bf16[1152,128]{1,0:T(8,128)(2,1)S(1)} %shard_map.85), channel_id=1, source_target_pairs={{0,1},{1,0},{2,3},{3,2},{4,5},{5,4},{6,7},{7,6},{8,9},{9,8},{10,11... | collective-permute-start | bytes 884744 | tf_op jit(solution)/shard_map/ppermute | solution.py:294
  59.9 3.5 %collective-permute-start.5 = (bf16[1152,128]{1,0:T(8,128)(2,1)S(1)}, bf16[1152,128]{1,0:T(8,128)(2,1)S(1)}, u32[]{:S(2)}, u32[]{:S(2)}) collective-permute-start(bf16[1152,128]{1,0:T(8,128)(2,1)S(1)} %shard_map.86), channel_id=1, source_target_pairs={{0,1},{1,0},{2,3},{3,2},{4,5},{5,4},{6,7},{7,6},{8,9},{9,8},{10,11... | collective-permute-start | bytes 884744 | tf_op jit(solution)/shard_map/ppermute | solution.py:295
  63.4 12.0 %copy-start.9 = (bf16[2,256,256]{2,1,0:T(8,128)(2,1)S(1)}, bf16[2,256,256]{2,1,0:T(8,128)(2,1)}, u32[]{:S(2)}) copy-start(bf16[2,256,256]{2,1,0:T(8,128)(2,1)} %copy-done.8) | copy-start | bytes 786436
  66.7 9.8 %collective-permute-start.6 = (bf16[256,256]{1,0:T(8,128)(2,1)S(1)}, bf16[256,256]{1,0:T(8,128)(2,1)S(1)}, u32[]{:S(2)}, u32[]{:S(2)}) collective-permute-start(bf16[256,256]{1,0:T(8,128)(2,1)S(1)} %get-tuple-element.31), channel_id=1, source_target_pairs={{0,0},{16,1},{2,2},{18,3},{4,4},{20,5},{6,6},{22,7},{8,8},{24,9},{... | collective-permute-start | bytes 393224 | tf_op jit(solution)/shard_map/ppermute | solution.py:302
  73.4 7.5 %collective-permute-start.7 = (bf16[256,256]{1,0:T(8,128)(2,1)S(1)}, bf16[256,256]{1,0:T(8,128)(2,1)S(1)}, u32[]{:S(2)}, u32[]{:S(2)}) collective-permute-start(bf16[256,256]{1,0:T(8,128)(2,1)S(1)} %get-tuple-element.32), channel_id=1, source_target_pairs={{8,0},{24,1},{10,2},{26,3},{12,4},{28,5},{14,6},{30,7},{0,8},{16,9... | collective-permute-start | bytes 393224 | tf_op jit(solution)/shard_map/ppermute | solution.py:303
  75.3 5.6 %copy-start.3 = (bf16[256,2048]{1,0:T(8,128)(2,1)S(1)}, bf16[256,2048]{1,0:T(8,128)(2,1)}, u32[]{:S(2)}) copy-start(bf16[256,2048]{1,0:T(8,128)(2,1)} %wo_ref.1) | copy-start | bytes 3145732

commit v2 on v1

--- a/solution.py
+++ b/solution.py
@@ -14,6 +14,7 @@
 HOP_ROW = 3 * TOK + DH
 PACK = HOP_ROW + 16
 PAIR = 4 * TOK + DH
+BACK = TOK + 16
 VMEM = pl.BlockSpec(memory_space=pltpu.VMEM)
 SMEM = pl.BlockSpec(memory_space=pltpu.SMEM)
 
@@ -30,13 +31,12 @@
     return lax.dot_general(a, b, NN, precision=lax.Precision.HIGHEST, preferred_element_type=F32)
 
 
-def call(body, outs, ins, scratch=(), flops=0, smem=0):
+def call(body, outs, ins, flops=0, smem=0):
     return pl.pallas_call(
         body,
         out_shape=outs,
         in_specs=[SMEM] * smem + [VMEM] * (ins - smem),
         out_specs=jax.tree.map(lambda _: VMEM, outs),
-        scratch_shapes=list(scratch),
         compiler_params=pltpu.CompilerParams(vmem_limit_bytes=48 * 2**20),
         cost_estimate=pl.CostEstimate(flops=flops, bytes_accessed=2**20, transcendentals=0),
     )
@@ -95,13 +95,16 @@
 
 
 def project_kernel(
-    at_ref, hop_ref, x_ref, wq_ref, wk_ref, wv_ref, w_ref, u_ref, y_ref, a_ref,
+    at_ref, hop_ref, x_ref, o_ref, wq_ref, wk_ref, wv_ref, w_ref, u_ref, y_ref, a_ref,
     p0_ref, p1_ref, q_ref, k_ref, v_ref,
 ):
     def product(weights):
-        total = dot(x_ref[0], weights[0:256, :])
-        for p in range(1, 8):
-            total += dot(x_ref[p], weights[p * 256 : (p + 1) * 256, :])
+        total = None
+        for p in range(4):
+            for ref, c in ((x_ref, at_ref[1]), (o_ref, 1 - at_ref[1])):
+                rows = pl.ds(pl.multiple_of((2 * p + c) * 256, 256), 256)
+                term = dot(ref[p], weights[rows, :])
+                total = term if total is None else total + term
         return total.astype(BF16)
 
     query, key, value = product(wq_ref), product(wk_ref), product(wv_ref)
@@ -170,73 +173,109 @@
     hop_ref[1] = h_odd.astype(F32)
 
 
-def mix_kernel(at_ref, a_ref, b_ref, out_ref):
-    @pl.when(at_ref[1] == 0)
-    def _():
-        out_ref[...] = a_ref[...]
-
-    @pl.when(at_ref[1] == 1)
-    def _():
-        out_ref[...] = b_ref[...]
-
-
-def window_kernel(
-    at_ref, q_ref, hop_ref, z1_ref, z2_ref, s1_ref, s2_ref, o0_ref, o1_ref, scores
+def window_step(q, keys, d, i, hops, pair):
+    col = lax.broadcasted_iota(jnp.int32, (1, 2 * TOK), 1)
+    distance = 2 * d + i - (col >= TOK).astype(jnp.int32)
+    valid = (distance.astype(F32) <= hops) & (pair >= d)
+    return dot(q, keys[0 : 2 * TOK], NT) + jnp.where(valid, 0.0, NEG)
+
+
+def near_kernel(at_ref, q_ref, hop_ref, d1_ref, d2_ref, acc_ref, top_ref, total_ref, next_ref):
+    pair = at_ref[2]
+    for i in range(2):
+        hops = hop_ref[i, 0:1, 0:1]
+        q = q_ref[1, i]
+        first = window_step(q, d1_ref, 1, i, hops, pair)
+        q = dot(q, d1_ref[4 * TOK : PAIR]).astype(BF16)
+        second = window_step(q, d2_ref, 2, i, hops, pair)
+        next_ref[i] = dot(q, d2_ref[4 * TOK : PAIR]).astype(BF16)
+        top = jnp.maximum(jnp.max(first, axis=1, keepdims=True), jnp.max(second, axis=1, keepdims=True))
+        if i == 1:
+            inside = dot(q_ref[0, 1], q_ref[2, 0], NT)
+            top = jnp.maximum(top, jnp.max(inside, axis=1, keepdims=True))
+        first, second = jnp.exp2(first - top), jnp.exp2(second - top)
+        total = jnp.sum(first, axis=1, keepdims=True) + jnp.sum(second, axis=1, keepdims=True)
+        acc = dot(first.astype(BF16), d1_ref[2 * TOK : 4 * TOK])
+        acc += dot(second.astype(BF16), d2_ref[2 * TOK : 4 * TOK])
+        if i == 1:
+            inside = jnp.exp2(inside - top)
+            total += jnp.sum(inside, axis=1, keepdims=True)
+            acc += dot(inside.astype(BF16), q_ref[2, 1])
+        acc_ref[i] = acc
+        top_ref[i] = jnp.broadcast_to(top, (TOK, DH))
+        total_ref[i] = jnp.broadcast_to(total, (TOK, DH))
+
+
+def far_kernel(
+    at_ref, hop_ref, d3_ref, d4_ref, acc_ref, top_ref, total_ref, next_ref, o0_ref, o1_ref
 ):
-    keys = (s1_ref, z1_ref, s2_ref, z2_ref)
     pair = at_ref[2]
-    col = lax.broadcasted_iota(jnp.int32, (1, 2 * TOK), 1)
-    odd_key = col >= TOK
     for j, out_ref in enumerate((o0_ref, o1_ref)):
         i = lax.rem(at_ref[0] + j, 2)
         hops = hop_ref[i, 0:1, 0:1]
-        inside = dot(q_ref[0, i], q_ref[2, 0], NT) + jnp.where(i == 1, 0.0, NEG)
-        scores[:, 0:TOK] = inside
-        top = jnp.max(inside, axis=1, keepdims=True)
-        q = q_ref[1, i]
-        for d in range(1, 5):
-            s = dot(q, keys[d - 1][0 : 2 * TOK], NT)
-            distance = 2 * d + i - odd_key.astype(jnp.int32)
-            valid = (distance.astype(F32) <= hops) & (pair >= d)
-            s = s + jnp.where(valid, 0.0, NEG)
-            scores[:, (2 * d - 1) * TOK : (2 * d + 1) * TOK] = s
-            top = jnp.maximum(top, jnp.max(s, axis=1, keepdims=True))
-            if d < 4:
-                q = dot(q, keys[d - 1][4 * TOK : PAIR]).astype(BF16)
-        prob = jnp.exp2(scores[:, 0:TOK] - top)
-        total = jnp.sum(prob, axis=1, keepdims=True)
-        acc = dot(prob.astype(BF16), q_ref[2, 1])
-        for d in range(1, 5):
-            prob = jnp.exp2(scores[:, (2 * d - 1) * TOK : (2 * d + 1) * TOK] - top)
-            total += jnp.sum(prob, axis=1, keepdims=True)
-            acc += dot(prob.astype(BF16), keys[d - 1][2 * TOK : 4 * TOK])
-        lse = jnp.broadcast_to(top + jnp.log2(total), (TOK, DH))
+        q = next_ref[i]
+        third = window_step(q, d3_ref, 3, i, hops, pair)
+        q = dot(q, d3_ref[4 * TOK : PAIR]).astype(BF16)
+        fourth = window_step(q, d4_ref, 4, i, hops, pair)
+        before = top_ref[i, :, 0:1]
+        top = jnp.maximum(jnp.max(third, axis=1, keepdims=True), jnp.max(fourth, axis=1, keepdims=True))
+        top = jnp.maximum(top, before)
+        third, fourth = jnp.exp2(third - top), jnp.exp2(fourth - top)
+        kept = jnp.exp2(before - top)
+        total = total_ref[i, :, 0:1] * kept
+        total += jnp.sum(third, axis=1, keepdims=True) + jnp.sum(fourth, axis=1, keepdims=True)
+        acc = acc_ref[i] * kept
+        acc += dot(third.astype(BF16), d3_ref[2 * TOK : 4 * TOK])
+        acc += dot(fourth.astype(BF16), d4_ref[2 * TOK : 4 * TOK])
+        out_ref[0:TOK] = (acc / total).astype(BF16)
+        lse = jnp.broadcast_to(top + jnp.log2(total), (TOK, DH)).T[0:16]
         high = lse.astype(BF16).astype(F32)
-        lane = lax.broadcasted_iota(jnp.int32, (TOK, DH), 1)
-        out_ref[:, 0:DH] = (acc / total).astype(BF16)
-        out_ref[:, DH:] = jnp.where(lane < DH // 2, high, lse - high).astype(BF16)
-
-
-def output_kernel(at_ref, g0_ref, g1_ref, acc_ref, lse_ref, wo_ref, out_ref):
+        low = lse - high
+        line = lax.broadcasted_iota(jnp.int32, (16, DH), 0)
+        tile = jnp.where(line == 0, high[:, :DH], high[:, DH:])
+        tile = jnp.where(line == 2, low[:, :DH], tile)
+        tile = jnp.where(line == 3, low[:, DH:], tile)
+        out_ref[TOK:BACK] = tile.astype(BF16)
+
+
+def merge_kernel(at_ref, g0_ref, g1_ref, acc_ref, lse_ref, out_ref):
     swapped = at_ref[0] == 1
-    parts = []
+    row = lax.broadcasted_iota(jnp.int32, (DH, DH), 0)
+    col = lax.broadcasted_iota(jnp.int32, (DH, DH), 1)
     for h in range(2):
         a, b = (g0_ref, g1_ref) if h == 0 else (g1_ref, g0_ref)
         got = jnp.where(swapped, b[...], a[...]).astype(F32)
-        far = got[:, DH : DH + 1] + got[:, DH + DH // 2 : DH + DH // 2 + 1]
+        tile = got[TOK:BACK]
+        column = []
+        for part in range(2):
+            line = tile[part : part + 1] + tile[part + 2 : part + 3]
+            column.append(jnp.sum(jnp.where(row == col, line, 0.0), axis=1, keepdims=True))
+        far = jnp.concatenate(column, axis=0)
         own = lse_ref[h, :, 0:1]
         top = jnp.maximum(own, far)
         mine, theirs = jnp.exp2(own - top), jnp.exp2(far - top)
-        mixed = (acc_ref[h] * mine + got[:, :DH] * theirs) / (mine + theirs)
-        parts.append(mixed.astype(BF16))
-    attended = jnp.concatenate(parts, axis=1)
-    for p in range(8):
-        out_ref[p] = dot(attended, wo_ref[:, p * 256 : (p + 1) * 256]).astype(BF16)
+        mixed = (acc_ref[h] * mine + got[:TOK] * theirs) / (mine + theirs)
+        out_ref[:, h * DH : (h + 1) * DH] = mixed.astype(BF16)
+
+
+def columns(c, p):
+    return pl.ds(pl.multiple_of((2 * p + c) * 256, 256), 256)
+
+
+def halves_kernel(at_ref, wo_ref, out_ref):
+    for p in range(4):
+        out_ref[p] = wo_ref[:, columns(1 - at_ref[1], p)]
+
+
+def output_kernel(at_ref, mine_ref, theirs_ref, wo_ref, other_ref, out_ref):
+    for p in range(4):
+        total = dot(mine_ref[...], wo_ref[:, columns(at_ref[1], p)])
+        out_ref[p] = (total + dot(theirs_ref[...], other_ref[p])).astype(BF16)
 
 
 def sum_kernel(x_ref, out_ref):
     total = x_ref[0].astype(F32)
-    for p in range(1, 8):
+    for p in range(1, 4):
         total += x_ref[p].astype(F32)
     out_ref[...] = total.astype(BF16)
 
@@ -252,6 +291,16 @@
     return pairs
 
 
+def follow_pairs(rows, cross):
+    pairs = []
+    for b in range(4 * rows):
+        for y in range(0, cross, 2):
+            pairs.append((b * cross + y, b * cross + y + 1))
+            if b + 4 < 4 * rows:
+                pairs.append((b * cross + y + 1, (b + 4) * cross + y))
+    return pairs
+
+
 def shape(dims, dtype=BF16):
     return jax.ShapeDtypeStruct(dims, dtype)
 
@@ -264,6 +313,7 @@
     at = jnp.stack([x % 2, c, 2 * z + c]).astype(jnp.int32)
     there = [regroup_pairs(j, 16, 8, 4) for j in range(2)]
     back = [[(b, a) for a, b in pairs] for pairs in there]
+    follow = follow_pairs(16, 8)
     down = [(b, b + 4) for b in range(60)]
     twin = [(h, h ^ 1) for h in range(8)]
 
@@ -272,12 +322,17 @@
         [shape((2, TOK, DH)), shape((2, TOK, TOK)), shape((2, TOK, DH)), shape((2, TOK, DH)), shape((2, DH, DH))],
         2, flops=2**32,
     )(reflect_dir, strength)
-    gathered = lax.all_to_all(jnp.broadcast_to(inputs[None], (8, TOK, 256)), "head", 0, 0)
+    planes = [[0, 2, 4, 6], [1, 3, 5, 7]]
+    copies = jnp.broadcast_to(inputs[None], (4, TOK, 256))
+    gathered = lax.all_to_all(copies, "head", 0, 0, axis_index_groups=planes)
+    other = lax.ppermute(gathered, "head", twin)
+    halves = call(halves_kernel, shape((4, 256, 256)), 2, smem=1)(at, w_out)
+    other_out = lax.ppermute(halves, "head", twin)
     p0, p1, q, k, v = call(
         project_kernel,
         [shape((PACK, DH)), shape((PACK, DH))] + [shape((2, TOK, DH))] * 3,
-        10, smem=2, flops=2**30,
-    )(at, hop_count, gathered, w_query, w_key, w_value, w, u, y, a)
+        11, smem=2, flops=2**30,
+    )(at, hop_count, gathered, other, w_query, w_key, w_value, w, u, y, a)
     r0 = lax.ppermute(p0, both, there[0])
     r1 = lax.ppermute(p1, both, there[1])
     acc, lse = call(
@@ -288,21 +343,23 @@
         [shape((3, 2, TOK, DH)), shape((PAIR, DH)), shape((2, 16, DH), F32)],
         3, smem=1, flops=2**28,
     )(at, r0, r1)
-    mix = call(mix_kernel, shape((PAIR, DH)), 3, smem=1, flops=2**27)
-    z1 = lax.ppermute(own_pair, "ctx", down)
-    z2 = lax.ppermute(z1, "ctx", down)
-    s1 = lax.ppermute(mix(at, own_pair, z1), "head", twin)
-    s2 = lax.ppermute(mix(at, z1, z2), "head", twin)
+    d1 = lax.ppermute(own_pair, both, follow)
+    d2 = lax.ppermute(own_pair, "ctx", down)
+    d3 = lax.ppermute(d2, both, follow)
+    d4 = lax.ppermute(d2, "ctx", down)
+    state = [shape((2, TOK, DH), F32)] * 3 + [shape((2, TOK, DH))]
+    near = call(near_kernel, state, 5, smem=1, flops=2**31)(at, qs, hops, d1, d2)
     o0, o1 = call(
-        window_kernel,
-        [shape((TOK, 2 * DH)), shape((TOK, 2 * DH))],
-        7, smem=1, flops=2**30,
-        scratch=[pltpu.VMEM((TOK, 9 * TOK), F32)],
-    )(at, qs, hops, z1, z2, s1, s2)
+        far_kernel, [shape((BACK, DH)), shape((BACK, DH))], 8, smem=1, flops=2**30
+    )(at, hops, d3, d4, *near)
     g0 = lax.ppermute(o0, both, back[0])
     g1 = lax.ppermute(o1, both, back[1])
-    partial = call(output_kernel, shape((8, TOK, 256)), 6, smem=1, flops=2**29)(at, g0, g1, acc, lse, w_out)
-    pieces = lax.all_to_all(partial, "head", 0, 0)
+    mine = call(merge_kernel, shape((TOK, 2 * DH)), 5, smem=1, flops=2**28)(at, g0, g1, acc, lse)
+    theirs = lax.ppermute(mine, "head", twin)
+    partial = call(output_kernel, shape((4, TOK, 256)), 5, smem=1, flops=2**29)(
+        at, mine, theirs, w_out, other_out
+    )
+    pieces = lax.all_to_all(partial, "head", 0, 0, axis_index_groups=planes)
     return call(sum_kernel, shape((TOK, 256)), 1)(pieces)
 
 

time: 102 us -> 96.7 us (0.948)
  the two profiles are of different devices: /device:TPU:390 before, /device:TPU:384 now
where the time goes in v2:
time: 96.7 us; the launch traced here: 96.2 us
  starting transfers between devices  33.3 us (34%)
  blocking collectives  26.5 us (27%)
  waiting for transfers between devices  18.1 us (19%)
  Pallas kernels  15.6 us (16%)
  local copies, waits for them, and re-layouts  1.56 us (2%)
    all_to_all x1, blocking collectives, shards(): gathered = lax.all_to_all(copies, 'head', 0, 0, axis_index_groups=planes)  13.9 us
    all_to_all x1, blocking collectives, shards(): pieces = lax.all_to_all(partial, 'head', 0, 0, axis_index_groups=planes)  12.7 us
    ppermute x1, starting transfers between devices, shards(): theirs = lax.ppermute(mine, 'head', twin)  7.77 us
    ppermute x1, waiting for transfers between devices, shards(): r1 = lax.ppermute(p1, both, there[1])  6.76 us
    ppermute x1, waiting for transfers between devices, shards(): d4 = lax.ppermute(d2, 'ctx', down)  5.47 us
    ppermute x1, starting transfers between devices, shards(): d1 = lax.ppermute(own_pair, both, follow)  4.41 us
    pallas_call x1, Pallas kernels, shards(): call(directions_kernel, [shape((2, TOK, DH)), shape((2, TOK, TOK)), shape...  4.36 us
    ppermute x1, starting transfers between devices, shards(): g1 = lax.ppermute(o1, both, back[1])  4.17 us
  transfers between devices with their start and end apart: 11, of which 5 were waited for; matrix products, arithmetic and copies ran while one was open for 0% of the time, Pallas kernels for 12%

profile of v2, /device:TPU:384, one launch (start us, length us, event | category | flops | bytes accessed | tf_op | source)
XLA Modules:
  0.0 96.2 jit_solution(1468740184876642653)
XLA Ops:
  0.0 0.9 broadcast_in_dim.2
  1.0 13.9 %all_to_all.10.x_ref = bf16[4,256,256]{2,1,0:T(8,128)(2,1)S(1)} all-to-all(bf16[4,256,256]{2,1,0:T(8,128)(2,1)S(1)} %broadcast_in_dim.2), channel_id=1, replica_groups={{0,2,4,6},{1,3,5,7},{8,10,12,14},{9,11,13,15},{16,18,20,22},{17,19,21,2..., dimensions={0} | all-to-all | bytes 1048576 | tf_op jit(solution)/shard_map/all_to_all | solution.py:327
  14.8 1.9 %collective-permute-start = (bf16[4,256,256]{2,1,0:T(8,128)(2,1)S(1)}, bf16[4,256,256]{2,1,0:T(8,128)(2,1)S(1)}, u32[]{:S(2)}, u32[]{:S(2)}) collective-permute-start(bf16[4,256,256]{2,1,0:T(8,128)(2,1)S(1)} %all_to_all.10.x_ref), channel_id=1, source_target_pairs={{0,1},{1,0},{2,3},{3,2},{4,5},{5,4},{6,7},{7,6},{8,9},{9,8},{10,11... | collective-permute-start | bytes 1572872 | tf_op jit(solution)/shard_map/ppermute | solution.py:328
  17.4 0.0 copy-start.5
  17.4 0.1 pad_add_fusion.at_ref
  17.5 0.6 copy-done.5
  18.1 4.4 %shard_map.82 = (bf16[2,256,128]{2,1,0:T(8,128)(2,1)S(1)}, bf16[2,256,256]{2,1,0:T(8,128)(2,1)S(1)}, bf16[2,256,128]{2,1,0:T(8,128)(2,1)S(1)}, bf16[2,256,128]{2,1,0:T(8,128)(2,1)S(1)}, bf16[2,128,128]{2,1,0:T(8,128)(2,1)S(1)}) custom-call(bf16[256,256]{1,0:T(8,128)(2,1)S(1)} %copy-done.4, f32[2,256]{1,0:T(2,128)S(1)} %copy-done.5), custom_call_target="tpu_custom_call" | custom-call | flops 4294967296 | bytes 1048576 | tf_op jit(solution)/shard_map/pallas_call | solution.py:320
  22.5 1.9 %shard_map.83 = (bf16[912,128]{1,0:T(8,128)(2,1)S(1)}, bf16[912,128]{1,0:T(8,128)(2,1)S(1)}, bf16[2,256,128]{2,1,0:T(8,128)(2,1)S(1)}, bf16[2,256,128]{2,1,0:T(8,128)(2,1)S(1)}, bf16[2,256,128]{2,1,0:T(8,128)(2,1)S(1)}) custom-call(s32[3]{0:T(128)S(1)} %pad_add_fusion.at_ref, s32[1]{0:T(128)S(6)} %copy.9.hop_ref, bf16[4,256,256]{2,1,0:T(8,128)(2,1)S(1)} %all_to_all.10.x_ref, ...), custom_call_target="tpu_custom_call" | custom-call | flops 1073741824 | bytes 1048576 | tf_op jit(solution)/shard_map/pallas_call | solution.py:331
  24.4 0.7 collective-permute-start.1
  25.1 3.4 %collective-permute-start.2 = (bf16[912,128]{1,0:T(8,128)(2,1)S(1)}, bf16[912,128]{1,0:T(8,128)(2,1)S(1)}, u32[]{:S(2)}, u32[]{:S(2)}) collective-permute-start(bf16[912,128]{1,0:T(8,128)(2,1)S(1)} %get-tuple-element.31), channel_id=1, source_target_pairs={{0,8},{1,24},{2,10},{3,26},{4,12},{5,28},{6,14},{7,30},{8,0},{9,16... | collective-permute-start | bytes 700424 | tf_op jit(solution)/shard_map/ppermute | solution.py:337
  28.6 6.8 %collective-permute-done.2.r1_ref = bf16[912,128]{1,0:T(8,128)(2,1)S(1)} collective-permute-done((bf16[912,128]{1,0:T(8,128)(2,1)S(1)}, bf16[912,128]{1,0:T(8,128)(2,1)S(1)}, u32[]{:S(2)}, u32[]{:S(2)}) %collective-permute-start.2) | collective-permute-done | bytes 233504 | tf_op jit(solution)/shard_map/ppermute | solution.py:337
  35.3 0.8 shard_map.84
  36.1 2.9 %collective-permute-start.3 = (bf16[1152,128]{1,0:T(8,128)(2,1)S(1)}, bf16[1152,128]{1,0:T(8,128)(2,1)S(1)}, u32[]{:S(2)}, u32[]{:S(2)}) collective-permute-start(bf16[1152,128]{1,0:T(8,128)(2,1)S(1)} %get-tuple-element.33), channel_id=1, source_target_pairs={{0,32},{8,40},{16,48},{24,56},{32,64},{40,72},{48,80},{56,88},{64,... | collective-permute-start | bytes 884744 | tf_op jit(solution)/shard_map/ppermute | solution.py:347
  39.0 4.4 %collective-permute-start.6 = (bf16[1152,128]{1,0:T(8,128)(2,1)S(1)}, bf16[1152,128]{1,0:T(8,128)(2,1)S(1)}, u32[]{:S(2)}, u32[]{:S(2)}) collective-permute-start(bf16[1152,128]{1,0:T(8,128)(2,1)S(1)} %get-tuple-element.33), channel_id=1, source_target_pairs={{0,1},{1,32},{2,3},{3,34},{4,5},{5,36},{6,7},{7,38},{8,9},{9,40},{... | collective-permute-start | bytes 884744 | tf_op jit(solution)/shard_map/ppermute | solution.py:346
  43.5 3.8 %collective-permute-done.3.d2_ref = bf16[1152,128]{1,0:T(8,128)(2,1)S(1)} collective-permute-done((bf16[1152,128]{1,0:T(8,128)(2,1)S(1)}, bf16[1152,128]{1,0:T(8,128)(2,1)S(1)}, u32[]{:S(2)}, u32[]{:S(2)}) %collective-permute-start.3) | collective-permute-done | bytes 294944 | tf_op jit(solution)/shard_map/ppermute | solution.py:347
  47.2 3.6 %collective-permute-start.4 = (bf16[1152,128]{1,0:T(8,128)(2,1)S(1)}, bf16[1152,128]{1,0:T(8,128)(2,1)S(1)}, u32[]{:S(2)}, u32[]{:S(2)}) collective-permute-start(bf16[1152,128]{1,0:T(8,128)(2,1)S(1)} %collective-permute-done.3.d2_ref), channel_id=1, source_target_pairs={{0,1},{1,32},{2,3},{3,34},{4,5},{5,36},{6,7},{7,38},{8,9},{9,40},{... | collective-permute-start | bytes 884744 | tf_op jit(solution)/shard_map/ppermute | solution.py:348
  50.8 1.9 %collective-permute-start.5 = (bf16[1152,128]{1,0:T(8,128)(2,1)S(1)}, bf16[1152,128]{1,0:T(8,128)(2,1)S(1)}, u32[]{:S(2)}, u32[]{:S(2)}) collective-permute-start(bf16[1152,128]{1,0:T(8,128)(2,1)S(1)} %collective-permute-done.3.d2_ref), channel_id=1, source_target_pairs={{0,32},{8,40},{16,48},{24,56},{32,64},{40,72},{48,80},{56,88},{64,... | collective-permute-start | bytes 884744 | tf_op jit(solution)/shard_map/ppermute | solution.py:349
  52.8 0.6 shard_map.89
  53.4 1.9 %collective-permute-start.10 = (bf16[4,256,256]{2,1,0:T(8,128)(2,1)S(1)}, bf16[4,256,256]{2,1,0:T(8,128)(2,1)S(1)}, u32[]{:S(2)}, u32[]{:S(2)}) collective-permute-start(bf16[4,256,256]{2,1,0:T(8,128)(2,1)S(1)} %shard_map.89), channel_id=1, source_target_pairs={{0,1},{1,0},{2,3},{3,2},{4,5},{5,4},{6,7},{7,6},{8,9},{9,8},{10,11... | collective-permute-start | bytes 1572872 | tf_op jit(solution)/shard_map/ppermute | solution.py:330
  55.3 2.0 %shard_map.85 = (f32[2,256,128]{2,1,0:T(8,128)S(1)}, f32[2,256,128]{2,1,0:T(8,128)S(1)}, f32[2,256,128]{2,1,0:T(8,128)S(1)}, bf16[2,256,128]{2,1,0:T(8,128)(2,1)S(1)}) custom-call(s32[3]{0:T(128)S(1)} %pad_add_fusion.at_ref, bf16[3,2,256,128]{3,2,1,0:T(8,128)(2,1)S(1)} %get-tuple-element.34.q_ref, f32[2,16,128]{2,1,0:T(8,128)S(1)} %get-tuple-element.32.hop_ref, ...), custom_call_target="tpu_custom_call" | custom-call | flops 2147483648 | bytes 1048576 | tf_op jit(solution)/shard_map/pallas_call | solution.py:351
  57.4 5.5 %collective-permute-done.5.d4_ref = bf16[1152,128]{1,0:T(8,128)(2,1)S(1)} collective-permute-done((bf16[1152,128]{1,0:T(8,128)(2,1)S(1)}, bf16[1152,128]{1,0:T(8,128)(2,1)S(1)}, u32[]{:S(2)}, u32[]{:S(2)}) %collective-permute-start.5) | collective-permute-done | bytes 294944 | tf_op jit(solution)/shard_map/ppermute | solution.py:349
  62.9 2.1 %shard_map.86 = (bf16[272,128]{1,0:T(8,128)(2,1)S(1)}, bf16[272,128]{1,0:T(8,128)(2,1)S(1)}) custom-call(s32[3]{0:T(128)S(1)} %pad_add_fusion.at_ref, f32[2,16,128]{2,1,0:T(8,128)S(1)} %get-tuple-element.32.hop_ref, bf16[1152,128]{1,0:T(8,128)(2,1)S(1)} %collective-permute-done.4.d3_ref, bf16[1152,128]{1,0:T(8,128)(2,1)S(1)} %collective-permute-done.5.d4_ref, ...), custom_call_target="tpu_custom_call" | custom-call | flops 1073741824 | bytes 1048576 | tf_op jit(solution)/shard_map/pallas_call | solution.py:352
  64.9 0.7 collective-permute-start.7
  65.6 4.2 %collective-permute-start.8 = (bf16[272,128]{1,0:T(8,128)(2,1)S(1)}, bf16[272,128]{1,0:T(8,128)(2,1)S(1)}, u32[]{:S(2)}, u32[]{:S(2)}) collective-permute-start(bf16[272,128]{1,0:T(8,128)(2,1)S(1)} %get-tuple-element.40), channel_id=1, source_target_pairs={{8,0},{24,1},{10,2},{26,3},{12,4},{28,5},{14,6},{30,7},{0,8},{16,9... | collective-permute-start | bytes 208904 | tf_op jit(solution)/shard_map/ppermute | solution.py:356
  69.8 1.1 %shard_map.87 = (f32[2,256,128]{2,1,0:T(8,128)S(1)}, f32[2,256,128]{2,1,0:T(8,128)S(1)}) custom-call(bf16[2,256,128]{2,1,0:T(8,128)(2,1)S(1)} %get-tuple-element.41.q_ref, bf16[2,256,128]{2,1,0:T(8,128)(2,1)S(1)} %get-tuple-element.42.k_ref, bf16[2,256,128]{2,1,0:T(8,128)(2,1)S(1)} %get-tuple-element.43.v_ref, ...), custom_call_target="tpu_custom_call" | custom-call | flops 2147483648 | bytes 1048576 | tf_op jit(solution)/shard_map/pallas_call | solution.py:338
  70.9 1.1 %collective-permute-done.8.g1_ref = bf16[272,128]{1,0:T(8,128)(2,1)S(1)} collective-permute-done((bf16[272,128]{1,0:T(8,128)(2,1)S(1)}, bf16[272,128]{1,0:T(8,128)(2,1)S(1)}, u32[]{:S(2)}, u32[]{:S(2)}) %collective-permute-start.8) | collective-permute-done | bytes 69664 | tf_op jit(solution)/shard_map/ppermute | solution.py:356
  72.1 1.0 shard_map.88.mine_ref
  73.0 7.8 %collective-permute-start.9 = (bf16[256,256]{1,0:T(8,128)(2,1)S(1)}, bf16[256,256]{1,0:T(8,128)(2,1)S(1)}, u32[]{:S(2)}, u32[]{:S(2)}) collective-permute-start(bf16[256,256]{1,0:T(8,128)(2,1)S(1)} %shard_map.88.mine_ref), channel_id=1, source_target_pairs={{0,1},{1,0},{2,3},{3,2},{4,5},{5,4},{6,7},{7,6},{8,9},{9,8},{10,11... | collective-permute-start | bytes 393224 | tf_op jit(solution)/shard_map/ppermute | solution.py:358
  80.8 1.0 collective-permute-done.9.theirs_ref
  81.8 1.0 %shard_map.90 = bf16[4,256,256]{2,1,0:T(8,128)(2,1)S(1)} custom-call(s32[3]{0:T(128)S(1)} %pad_add_fusion.at_ref, bf16[256,256]{1,0:T(8,128)(2,1)S(1)} %shard_map.88.mine_ref, bf16[256,256]{1,0:T(8,128)(2,1)S(1)} %collective-permute-done.9.theirs_ref, bf16[256,2048]{1,0:T(8,128)(2,1)S(1)} %copy-done, bf16[4,256,256]{2,1,0:T(8,128)(2,1)S(1)} %collective-permute-done.10.other_ref), custom_call_target="tpu_custom_call" | custom-call | flops 536870912 | bytes 1048576 | tf_op jit(solution)/shard_map/pallas_call | solution.py:359
  82.8 12.7 %all_to_all.11.x_ref = bf16[4,256,256]{2,1,0:T(8,128)(2,1)S(1)} all-to-all(bf16[4,256,256]{2,1,0:T(8,128)(2,1)S(1)} %shard_map.90), channel_id=1, replica_groups={{0,2,4,6},{1,3,5,7},{8,10,12,14},{9,11,13,15},{16,18,20,22},{17,19,21,2..., dimensions={0} | all-to-all | bytes 1048576 | tf_op jit(solution)/shard_map/all_to_all | solution.py:362
  95.4 0.7 shard_map.91
  (16 shorter events, 0.0 us)
Async XLA Ops:
  0.9 16.6 %copy-start.4 = (bf16[256,256]{1,0:T(8,128)(2,1)S(1)}, bf16[256,256]{1,0:T(8,128)(2,1)}, u32[]{:S(2)}) copy-start(bf16[256,256]{1,0:T(8,128)(2,1)} %dirs_ref.1) | copy-start | bytes 393220
  14.8 7.7 %collective-permute-start = (bf16[4,256,256]{2,1,0:T(8,128)(2,1)S(1)}, bf16[4,256,256]{2,1,0:T(8,128)(2,1)S(1)}, u32[]{:S(2)}, u32[]{:S(2)}) collective-permute-start(bf16[4,256,256]{2,1,0:T(8,128)(2,1)S(1)} %all_to_all.10.x_ref), channel_id=1, source_target_pairs={{0,1},{1,0},{2,3},{3,2},{4,5},{5,4},{6,7},{7,6},{8,9},{9,8},{10,11... | collective-permute-start | bytes 1572872 | tf_op jit(solution)/shard_map/ppermute | solution.py:328
  17.4 0.7 copy-start.5
  18.1 4.4 %copy-start.1 = (bf16[2048,256]{1,0:T(8,128)(2,1)S(1)}, bf16[2048,256]{1,0:T(8,128)(2,1)}, u32[]{:S(2)}) copy-start(bf16[2048,256]{1,0:T(8,128)(2,1)} %wq_ref.1) | copy-start | bytes 3145732
  18.1 4.4 %copy-start.2 = (bf16[2048,256]{1,0:T(8,128)(2,1)S(1)}, bf16[2048,256]{1,0:T(8,128)(2,1)}, u32[]{:S(2)}) copy-start(bf16[2048,256]{1,0:T(8,128)(2,1)} %wk_ref.1) | copy-start | bytes 3145732
  18.1 4.4 %copy-start.3 = (bf16[2048,256]{1,0:T(8,128)(2,1)S(1)}, bf16[2048,256]{1,0:T(8,128)(2,1)}, u32[]{:S(2)}) copy-start(bf16[2048,256]{1,0:T(8,128)(2,1)} %wv_ref.1) | copy-start | bytes 3145732
  22.5 30.2 %copy-start = (bf16[256,2048]{1,0:T(8,128)(2,1)S(1)}, bf16[256,2048]{1,0:T(8,128)(2,1)}, u32[]{:S(2)}) copy-start(bf16[256,2048]{1,0:T(8,128)(2,1)} %wo_ref.3) | copy-start | bytes 3145732
  24.4 4.1 %collective-permute-start.1 = (bf16[912,128]{1,0:T(8,128)(2,1)S(1)}, bf16[912,128]{1,0:T(8,128)(2,1)S(1)}, u32[]{:S(2)}, u32[]{:S(2)}) collective-permute-start(bf16[912,128]{1,0:T(8,128)(2,1)S(1)} %get-tuple-element.30), channel_id=1, source_target_pairs={{0,0},{1,16},{2,2},{3,18},{4,4},{5,20},{6,6},{7,22},{8,8},{9,24},{... | collective-permute-start | bytes 700424 | tf_op jit(solution)/shard_map/ppermute | solution.py:336
  25.1 10.2 %collective-permute-start.2 = (bf16[912,128]{1,0:T(8,128)(2,1)S(1)}, bf16[912,128]{1,0:T(8,128)(2,1)S(1)}, u32[]{:S(2)}, u32[]{:S(2)}) collective-permute-start(bf16[912,128]{1,0:T(8,128)(2,1)S(1)} %get-tuple-element.31), channel_id=1, source_target_pairs={{0,8},{1,24},{2,10},{3,26},{4,12},{5,28},{6,14},{7,30},{8,0},{9,16... | collective-permute-start | bytes 700424 | tf_op jit(solution)/shard_map/ppermute | solution.py:337
  36.1 11.1 %collective-permute-start.3 = (bf16[1152,128]{1,0:T(8,128)(2,1)S(1)}, bf16[1152,128]{1,0:T(8,128)(2,1)S(1)}, u32[]{:S(2)}, u32[]{:S(2)}) collective-permute-start(bf16[1152,128]{1,0:T(8,128)(2,1)S(1)} %get-tuple-element.33), channel_id=1, source_target_pairs={{0,32},{8,40},{16,48},{24,56},{32,64},{40,72},{48,80},{56,88},{64,... | collective-permute-start | bytes 884744 | tf_op jit(solution)/shard_map/ppermute | solution.py:347
  39.0 16.3 %collective-permute-start.6 = (bf16[1152,128]{1,0:T(8,128)(2,1)S(1)}, bf16[1152,128]{1,0:T(8,128)(2,1)S(1)}, u32[]{:S(2)}, u32[]{:S(2)}) collective-permute-start(bf16[1152,128]{1,0:T(8,128)(2,1)S(1)} %get-tuple-element.33), channel_id=1, source_target_pairs={{0,1},{1,32},{2,3},{3,34},{4,5},{5,36},{6,7},{7,38},{8,9},{9,40},{... | collective-permute-start | bytes 884744 | tf_op jit(solution)/shard_map/ppermute | solution.py:346
  47.2 10.1 %collective-permute-start.4 = (bf16[1152,128]{1,0:T(8,128)(2,1)S(1)}, bf16[1152,128]{1,0:T(8,128)(2,1)S(1)}, u32[]{:S(2)}, u32[]{:S(2)}) collective-permute-start(bf16[1152,128]{1,0:T(8,128)(2,1)S(1)} %collective-permute-done.3.d2_ref), channel_id=1, source_target_pairs={{0,1},{1,32},{2,3},{3,34},{4,5},{5,36},{6,7},{7,38},{8,9},{9,40},{... | collective-permute-start | bytes 884744 | tf_op jit(solution)/shard_map/ppermute | solution.py:348
  50.8 12.0 %collective-permute-start.5 = (bf16[1152,128]{1,0:T(8,128)(2,1)S(1)}, bf16[1152,128]{1,0:T(8,128)(2,1)S(1)}, u32[]{:S(2)}, u32[]{:S(2)}) collective-permute-start(bf16[1152,128]{1,0:T(8,128)(2,1)S(1)} %collective-permute-done.3.d2_ref), channel_id=1, source_target_pairs={{0,32},{8,40},{16,48},{24,56},{32,64},{40,72},{48,80},{56,88},{64,... | collective-permute-start | bytes 884744 | tf_op jit(solution)/shard_map/ppermute | solution.py:349
  53.4 27.4 %collective-permute-start.10 = (bf16[4,256,256]{2,1,0:T(8,128)(2,1)S(1)}, bf16[4,256,256]{2,1,0:T(8,128)(2,1)S(1)}, u32[]{:S(2)}, u32[]{:S(2)}) collective-permute-start(bf16[4,256,256]{2,1,0:T(8,128)(2,1)S(1)} %shard_map.89), channel_id=1, source_target_pairs={{0,1},{1,0},{2,3},{3,2},{4,5},{5,4},{6,7},{7,6},{8,9},{9,8},{10,11... | collective-permute-start | bytes 1572872 | tf_op jit(solution)/shard_map/ppermute | solution.py:330
  64.9 6.0 %collective-permute-start.7 = (bf16[272,128]{1,0:T(8,128)(2,1)S(1)}, bf16[272,128]{1,0:T(8,128)(2,1)S(1)}, u32[]{:S(2)}, u32[]{:S(2)}) collective-permute-start(bf16[272,128]{1,0:T(8,128)(2,1)S(1)} %get-tuple-element.39), channel_id=1, source_target_pairs={{0,0},{16,1},{2,2},{18,3},{4,4},{20,5},{6,6},{22,7},{8,8},{24,9},{... | collective-permute-start | bytes 208904 | tf_op jit(solution)/shard_map/ppermute | solution.py:355
  65.6 6.5 %collective-permute-start.8 = (bf16[272,128]{1,0:T(8,128)(2,1)S(1)}, bf16[272,128]{1,0:T(8,128)(2,1)S(1)}, u32[]{:S(2)}, u32[]{:S(2)}) collective-permute-start(bf16[272,128]{1,0:T(8,128)(2,1)S(1)} %get-tuple-element.40), channel_id=1, source_target_pairs={{8,0},{24,1},{10,2},{26,3},{12,4},{28,5},{14,6},{30,7},{0,8},{16,9... | collective-permute-start | bytes 208904 | tf_op jit(solution)/shard_map/ppermute | solution.py:356
  73.0 8.7 %collective-permute-start.9 = (bf16[256,256]{1,0:T(8,128)(2,1)S(1)}, bf16[256,256]{1,0:T(8,128)(2,1)S(1)}, u32[]{:S(2)}, u32[]{:S(2)}) collective-permute-start(bf16[256,256]{1,0:T(8,128)(2,1)S(1)} %shard_map.88.mine_ref), channel_id=1, source_target_pairs={{0,1},{1,0},{2,3},{3,2},{4,5},{5,4},{6,7},{7,6},{8,9},{9,8},{10,11... | collective-permute-start | bytes 393224 | tf_op jit(solution)/shard_map/ppermute | solution.py:358

commit v3 on v2

--- a/solution.py
+++ b/solution.py
@@ -27,8 +27,14 @@
     return lax.dot_general(a, b, dims, preferred_element_type=F32)
 
 
+def split(a):
+    high = a.astype(BF16)
+    return high, (a - high.astype(F32)).astype(BF16)
+
+
 def exact(a, b):
-    return lax.dot_general(a, b, NN, precision=lax.Precision.HIGHEST, preferred_element_type=F32)
+    (ah, al), (bh, bl) = split(a), split(b)
+    return dot(ah, bh) + (dot(ah, bl) + dot(al, bh))
 
 
 def call(body, outs, ins, flops=0, smem=0):
@@ -44,13 +50,11 @@
 
 def lower_inverses(blocks, row, col):
     eye = (row == col).astype(F32)
-    same = (row // 8) == (col // 8)
+    same = (row // 4) == (col // 4)
     small = [jnp.where(same, b, 0.0) for b in blocks]
     squares = [exact(s, s) for s in small]
-    fourths = [exact(s, s) for s in squares]
-    firsts = [exact(eye - s, eye + q) for s, q in zip(small, squares)]
-    found = [exact(f, eye + q) for f, q in zip(firsts, fourths)]
-    size = 8
+    found = [exact(eye - s, eye + q) for s, q in zip(small, squares)]
+    size = 4
     while size < DH:
         off = ((row // (2 * size)) == (col // (2 * size))) & ((row // size) != (col // size))
         left = [exact(x, jnp.where(off, b, 0.0)) for x, b in zip(found, blocks)]
@@ -207,11 +211,11 @@
 
 
 def far_kernel(
-    at_ref, hop_ref, d3_ref, d4_ref, acc_ref, top_ref, total_ref, next_ref, o0_ref, o1_ref
+    at_ref, hop_ref, d3_ref, d4_ref, acc_ref, top_ref, total_ref, next_ref, out_ref
 ):
     pair = at_ref[2]
-    for j, out_ref in enumerate((o0_ref, o1_ref)):
-        i = lax.rem(at_ref[0] + j, 2)
+    for i in range(2):
+        piece = 2 * at_ref[1] + i
         hops = hop_ref[i, 0:1, 0:1]
         q = next_ref[i]
         third = window_step(q, d3_ref, 3, i, hops, pair)
@@ -227,7 +231,7 @@
         acc = acc_ref[i] * kept
         acc += dot(third.astype(BF16), d3_ref[2 * TOK : 4 * TOK])
         acc += dot(fourth.astype(BF16), d4_ref[2 * TOK : 4 * TOK])
-        out_ref[0:TOK] = (acc / total).astype(BF16)
+        out_ref[piece, 0:TOK] = (acc / total).astype(BF16)
         lse = jnp.broadcast_to(top + jnp.log2(total), (TOK, DH)).T[0:16]
         high = lse.astype(BF16).astype(F32)
         low = lse - high
@@ -235,16 +239,15 @@
         tile = jnp.where(line == 0, high[:, :DH], high[:, DH:])
         tile = jnp.where(line == 2, low[:, :DH], tile)
         tile = jnp.where(line == 3, low[:, DH:], tile)
-        out_ref[TOK:BACK] = tile.astype(BF16)
-
-
-def merge_kernel(at_ref, g0_ref, g1_ref, acc_ref, lse_ref, out_ref):
-    swapped = at_ref[0] == 1
+        out_ref[piece, TOK:BACK] = tile.astype(BF16)
+        out_ref[2 * (1 - at_ref[1]) + i] = jnp.zeros((BACK, DH), BF16)
+
+
+def merge_kernel(at_ref, g_ref, acc_ref, lse_ref, out_ref):
     row = lax.broadcasted_iota(jnp.int32, (DH, DH), 0)
     col = lax.broadcasted_iota(jnp.int32, (DH, DH), 1)
     for h in range(2):
-        a, b = (g0_ref, g1_ref) if h == 0 else (g1_ref, g0_ref)
-        got = jnp.where(swapped, b[...], a[...]).astype(F32)
+        got = g_ref[2 * at_ref[1] + h].astype(F32)
         tile = got[TOK:BACK]
         column = []
         for part in range(2):
@@ -301,6 +304,15 @@
     return pairs
 
 
+def return_groups(rows, cross):
+    groups = []
+    for z in range(rows):
+        for y in range(0, cross, 2):
+            for flip in (0, 1):
+                groups.append([(z * 4 + x) * cross + y + (x // 2 ^ flip) for x in range(4)])
+    return groups
+
+
 def shape(dims, dtype=BF16):
     return jax.ShapeDtypeStruct(dims, dtype)
 
@@ -312,7 +324,6 @@
     c = lax.axis_index("head") % 2
     at = jnp.stack([x % 2, c, 2 * z + c]).astype(jnp.int32)
     there = [regroup_pairs(j, 16, 8, 4) for j in range(2)]
-    back = [[(b, a) for a, b in pairs] for pairs in there]
     follow = follow_pairs(16, 8)
     down = [(b, b + 4) for b in range(60)]
     twin = [(h, h ^ 1) for h in range(8)]
@@ -349,12 +360,9 @@
     d4 = lax.ppermute(d2, "ctx", down)
     state = [shape((2, TOK, DH), F32)] * 3 + [shape((2, TOK, DH))]
     near = call(near_kernel, state, 5, smem=1, flops=2**31)(at, qs, hops, d1, d2)
-    o0, o1 = call(
-        far_kernel, [shape((BACK, DH)), shape((BACK, DH))], 8, smem=1, flops=2**30
-    )(at, hops, d3, d4, *near)
-    g0 = lax.ppermute(o0, both, back[0])
-    g1 = lax.ppermute(o1, both, back[1])
-    mine = call(merge_kernel, shape((TOK, 2 * DH)), 5, smem=1, flops=2**28)(at, g0, g1, acc, lse)
+    far = call(far_kernel, shape((4, BACK, DH)), 8, smem=1, flops=2**30)(at, hops, d3, d4, *near)
+    got = lax.all_to_all(far, both, 0, 0, axis_index_groups=return_groups(16, 8))
+    mine = call(merge_kernel, shape((TOK, 2 * DH)), 4, smem=1, flops=2**28)(at, got, acc, lse)
     theirs = lax.ppermute(mine, "head", twin)
     partial = call(output_kernel, shape((4, TOK, 256)), 5, smem=1, flops=2**29)(
         at, mine, theirs, w_out, other_out

time: 96.7 us -> 96.5 us (level)
  starting transfers between devices: 33.3 us -> 28.2 us
  waiting for transfers between devices: 18.1 us -> 22.6 us
    ppermute x1, starting transfers between devices: 7.77 us -> 2.03 us  [shards(): theirs = lax.ppermute(mine, 'head', twin)]
    all_to_all x0 -> x1, starting transfers between devices: none -> 5.41 us  [shards(): lax.all_to_all(far, both, 0, 0, axis_index_groups=return_groups(16, 8))]
    all_to_all x0 -> x1, waiting for transfers between devices: none -> 5.33 us  [shards(): lax.all_to_all(far, both, 0, 0, axis_index_groups=return_groups(16, 8))]
    ppermute x2 -> x0, starting transfers between devices: 4.83 us -> none  [the longest x1 4.17 us: shards(): g1 = lax.ppermute(o1, both, back[1])]
    ppermute x2 -> x0, waiting for transfers between devices: 1.12 us -> none  [the longest x1 1.12 us: shards(): g1 = lax.ppermute(o1, both, back[1])]
  transfers between devices with their start and end apart: 11 -> 10, of which waited for: 5 -> 5; matrix products, arithmetic and copies ran while one was open for 0% -> 0% of each run, Pallas kernels for 12% -> 11%
where the time goes in v3:
time: 96.5 us; the launch traced here: 96 us
  starting transfers between devices  28.2 us (29%)
  blocking collectives  26.3 us (27%)
  waiting for transfers between devices  22.6 us (23%)
  Pallas kernels  15.4 us (16%)
  local copies, waits for them, and re-layouts  2.51 us (3%)
    all_to_all x1, blocking collectives, shards(): gathered = lax.all_to_all(copies, 'head', 0, 0, axis_index_groups=planes)  13.9 us
    all_to_all x1, blocking collectives, shards(): pieces = lax.all_to_all(partial, 'head', 0, 0, axis_index_groups=planes)  12.5 us
    ppermute x1, waiting for transfers between devices, shards(): r1 = lax.ppermute(p1, both, there[1])  6.76 us
    ppermute x1, waiting for transfers between devices, shards(): d4 = lax.ppermute(d2, 'ctx', down)  5.47 us
    all_to_all x1, starting transfers between devices, shards(): lax.all_to_all(far, both, 0, 0, axis_index_groups=return_groups(16, 8))  5.41 us
    all_to_all x1, waiting for transfers between devices, shards(): lax.all_to_all(far, both, 0, 0, axis_index_groups=return_groups(16, 8))  5.33 us
    ppermute x1, starting transfers between devices, shards(): d1 = lax.ppermute(own_pair, both, follow)  4.39 us
    ppermute x1, waiting for transfers between devices, shards(): d2 = lax.ppermute(own_pair, 'ctx', down)  3.79 us
  transfers between devices with their start and end apart: 10, of which 5 were waited for; matrix products, arithmetic and copies ran while one was open for 0% of the time, Pallas kernels for 11%

profile of v3, /device:TPU:384, one launch (start us, length us, event | category | flops | bytes accessed | tf_op | source)
XLA Modules:
  0.0 96.0 jit_solution(8568254264096993412)
XLA Ops:
  0.0 0.9 broadcast_in_dim.2
  1.0 13.9 %all_to_all.15.x_ref = bf16[4,256,256]{2,1,0:T(8,128)(2,1)S(1)} all-to-all(bf16[4,256,256]{2,1,0:T(8,128)(2,1)S(1)} %broadcast_in_dim.2), channel_id=1, replica_groups={{0,2,4,6},{1,3,5,7},{8,10,12,14},{9,11,13,15},{16,18,20,22},{17,19,21,2..., dimensions={0} | all-to-all | bytes 1048576 | tf_op jit(solution)/shard_map/all_to_all | solution.py:338
  14.8 1.9 %collective-permute-start = (bf16[4,256,256]{2,1,0:T(8,128)(2,1)S(1)}, bf16[4,256,256]{2,1,0:T(8,128)(2,1)S(1)}, u32[]{:S(2)}, u32[]{:S(2)}) collective-permute-start(bf16[4,256,256]{2,1,0:T(8,128)(2,1)S(1)} %all_to_all.15.x_ref), channel_id=1, source_target_pairs={{0,1},{1,0},{2,3},{3,2},{4,5},{5,4},{6,7},{7,6},{8,9},{9,8},{10,11... | collective-permute-start | bytes 1572872 | tf_op jit(solution)/shard_map/ppermute | solution.py:339
  17.4 0.0 copy-start.5
  17.4 0.1 pad_add_fusion.at_ref
  17.5 0.6 copy-done.5
  18.1 3.5 %shard_map.82 = (bf16[2,256,128]{2,1,0:T(8,128)(2,1)S(1)}, bf16[2,256,256]{2,1,0:T(8,128)(2,1)S(1)}, bf16[2,256,128]{2,1,0:T(8,128)(2,1)S(1)}, bf16[2,256,128]{2,1,0:T(8,128)(2,1)S(1)}, bf16[2,128,128]{2,1,0:T(8,128)(2,1)S(1)}) custom-call(bf16[256,256]{1,0:T(8,128)(2,1)S(1)} %copy-done.4, f32[2,256]{1,0:T(2,128)S(1)} %copy-done.5), custom_call_target="tpu_custom_call" | custom-call | flops 4294967296 | bytes 1048576 | tf_op jit(solution)/shard_map/pallas_call | solution.py:331
  21.6 1.9 %shard_map.83 = (bf16[912,128]{1,0:T(8,128)(2,1)S(1)}, bf16[912,128]{1,0:T(8,128)(2,1)S(1)}, bf16[2,256,128]{2,1,0:T(8,128)(2,1)S(1)}, bf16[2,256,128]{2,1,0:T(8,128)(2,1)S(1)}, bf16[2,256,128]{2,1,0:T(8,128)(2,1)S(1)}) custom-call(s32[3]{0:T(128)S(1)} %pad_add_fusion.at_ref, s32[1]{0:T(128)S(6)} %copy.9.hop_ref, bf16[4,256,256]{2,1,0:T(8,128)(2,1)S(1)} %all_to_all.15.x_ref, ...), custom_call_target="tpu_custom_call" | custom-call | flops 1073741824 | bytes 1048576 | tf_op jit(solution)/shard_map/pallas_call | solution.py:342
  23.6 0.7 collective-permute-start.1
  24.2 3.4 %collective-permute-start.2 = (bf16[912,128]{1,0:T(8,128)(2,1)S(1)}, bf16[912,128]{1,0:T(8,128)(2,1)S(1)}, u32[]{:S(2)}, u32[]{:S(2)}) collective-permute-start(bf16[912,128]{1,0:T(8,128)(2,1)S(1)} %get-tuple-element.29), channel_id=1, source_target_pairs={{0,8},{1,24},{2,10},{3,26},{4,12},{5,28},{6,14},{7,30},{8,0},{9,16... | collective-permute-start | bytes 700424 | tf_op jit(solution)/shard_map/ppermute | solution.py:348
  27.7 6.8 %collective-permute-done.2.r1_ref = bf16[912,128]{1,0:T(8,128)(2,1)S(1)} collective-permute-done((bf16[912,128]{1,0:T(8,128)(2,1)S(1)}, bf16[912,128]{1,0:T(8,128)(2,1)S(1)}, u32[]{:S(2)}, u32[]{:S(2)}) %collective-permute-start.2) | collective-permute-done | bytes 233504 | tf_op jit(solution)/shard_map/ppermute | solution.py:348
  34.4 0.8 shard_map.84
  35.2 2.9 %collective-permute-start.3 = (bf16[1152,128]{1,0:T(8,128)(2,1)S(1)}, bf16[1152,128]{1,0:T(8,128)(2,1)S(1)}, u32[]{:S(2)}, u32[]{:S(2)}) collective-permute-start(bf16[1152,128]{1,0:T(8,128)(2,1)S(1)} %get-tuple-element.31), channel_id=1, source_target_pairs={{0,32},{8,40},{16,48},{24,56},{32,64},{40,72},{48,80},{56,88},{64,... | collective-permute-start | bytes 884744 | tf_op jit(solution)/shard_map/ppermute | solution.py:358
  38.2 4.4 %collective-permute-start.6 = (bf16[1152,128]{1,0:T(8,128)(2,1)S(1)}, bf16[1152,128]{1,0:T(8,128)(2,1)S(1)}, u32[]{:S(2)}, u32[]{:S(2)}) collective-permute-start(bf16[1152,128]{1,0:T(8,128)(2,1)S(1)} %get-tuple-element.31), channel_id=1, source_target_pairs={{0,1},{1,32},{2,3},{3,34},{4,5},{5,36},{6,7},{7,38},{8,9},{9,40},{... | collective-permute-start | bytes 884744 | tf_op jit(solution)/shard_map/ppermute | solution.py:357
  42.6 3.8 %collective-permute-done.3.d2_ref = bf16[1152,128]{1,0:T(8,128)(2,1)S(1)} collective-permute-done((bf16[1152,128]{1,0:T(8,128)(2,1)S(1)}, bf16[1152,128]{1,0:T(8,128)(2,1)S(1)}, u32[]{:S(2)}, u32[]{:S(2)}) %collective-permute-start.3) | collective-permute-done | bytes 294944 | tf_op jit(solution)/shard_map/ppermute | solution.py:358
  46.4 3.6 %collective-permute-start.4 = (bf16[1152,128]{1,0:T(8,128)(2,1)S(1)}, bf16[1152,128]{1,0:T(8,128)(2,1)S(1)}, u32[]{:S(2)}, u32[]{:S(2)}) collective-permute-start(bf16[1152,128]{1,0:T(8,128)(2,1)S(1)} %collective-permute-done.3.d2_ref), channel_id=1, source_target_pairs={{0,1},{1,32},{2,3},{3,34},{4,5},{5,36},{6,7},{7,38},{8,9},{9,40},{... | collective-permute-start | bytes 884744 | tf_op jit(solution)/shard_map/ppermute | solution.py:359
  49.9 1.9 %collective-permute-start.5 = (bf16[1152,128]{1,0:T(8,128)(2,1)S(1)}, bf16[1152,128]{1,0:T(8,128)(2,1)S(1)}, u32[]{:S(2)}, u32[]{:S(2)}) collective-permute-start(bf16[1152,128]{1,0:T(8,128)(2,1)S(1)} %collective-permute-done.3.d2_ref), channel_id=1, source_target_pairs={{0,32},{8,40},{16,48},{24,56},{32,64},{40,72},{48,80},{56,88},{64,... | collective-permute-start | bytes 884744 | tf_op jit(solution)/shard_map/ppermute | solution.py:360
  51.9 0.6 shard_map.89
  52.5 1.9 %collective-permute-start.8 = (bf16[4,256,256]{2,1,0:T(8,128)(2,1)S(1)}, bf16[4,256,256]{2,1,0:T(8,128)(2,1)S(1)}, u32[]{:S(2)}, u32[]{:S(2)}) collective-permute-start(bf16[4,256,256]{2,1,0:T(8,128)(2,1)S(1)} %shard_map.89), channel_id=1, source_target_pairs={{0,1},{1,0},{2,3},{3,2},{4,5},{5,4},{6,7},{7,6},{8,9},{9,8},{10,11... | collective-permute-start | bytes 1572872 | tf_op jit(solution)/shard_map/ppermute | solution.py:341
  54.4 2.0 %shard_map.85 = (f32[2,256,128]{2,1,0:T(8,128)S(1)}, f32[2,256,128]{2,1,0:T(8,128)S(1)}, f32[2,256,128]{2,1,0:T(8,128)S(1)}, bf16[2,256,128]{2,1,0:T(8,128)(2,1)S(1)}) custom-call(s32[3]{0:T(128)S(1)} %pad_add_fusion.at_ref, bf16[3,2,256,128]{3,2,1,0:T(8,128)(2,1)S(1)} %get-tuple-element.32.q_ref, f32[2,16,128]{2,1,0:T(8,128)S(1)} %get-tuple-element.30.hop_ref, ...), custom_call_target="tpu_custom_call" | custom-call | flops 2147483648 | bytes 1048576 | tf_op jit(solution)/shard_map/pallas_call | solution.py:362
  56.5 5.5 %collective-permute-done.5.d4_ref = bf16[1152,128]{1,0:T(8,128)(2,1)S(1)} collective-permute-done((bf16[1152,128]{1,0:T(8,128)(2,1)S(1)}, bf16[1152,128]{1,0:T(8,128)(2,1)S(1)}, u32[]{:S(2)}, u32[]{:S(2)}) %collective-permute-start.5) | collective-permute-done | bytes 294944 | tf_op jit(solution)/shard_map/ppermute | solution.py:360
  62.0 2.8 %shard_map.86 = bf16[4,272,128]{2,1,0:T(8,128)(2,1)} custom-call(s32[3]{0:T(128)S(1)} %pad_add_fusion.at_ref, f32[2,16,128]{2,1,0:T(8,128)S(1)} %get-tuple-element.30.hop_ref, bf16[1152,128]{1,0:T(8,128)(2,1)S(1)} %collective-permute-done.4.d3_ref, bf16[1152,128]{1,0:T(8,128)(2,1)S(1)} %collective-permute-done.5.d4_ref, ...), custom_call_target="tpu_custom_call" | custom-call | flops 1073741824 | bytes 1048576 | tf_op jit(solution)/shard_map/pallas_call | solution.py:363
  64.8 5.4 %all-to-all-start.1 = ((bf16[4,272,128]{2,1,0:T(8,128)(2,1)}), bf16[4,272,128]{2,1,0:T(8,128)(2,1)S(1)}, u32[]{:S(2)}, u32[]{:S(2)}) async-start(bf16[4,272,128]{2,1,0:T(8,128)(2,1)} %shard_map.86), calls=%async_computation.1 | async-start | bytes 557056 | tf_op jit(solution)/shard_map/all_to_all | solution.py:364
  70.2 0.9 copy-done.7
  71.2 1.1 %shard_map.87 = (f32[2,256,128]{2,1,0:T(8,128)S(1)}, f32[2,256,128]{2,1,0:T(8,128)S(1)}) custom-call(bf16[2,256,128]{2,1,0:T(8,128)(2,1)S(1)} %get-tuple-element.37.q_ref, bf16[2,256,128]{2,1,0:T(8,128)(2,1)S(1)} %get-tuple-element.38.k_ref, bf16[2,256,128]{2,1,0:T(8,128)(2,1)S(1)} %get-tuple-element.39.v_ref, ...), custom_call_target="tpu_custom_call" | custom-call | flops 2147483648 | bytes 1048576 | tf_op jit(solution)/shard_map/pallas_call | solution.py:349
  72.3 5.3 %all-to-all-done.1.g_ref = bf16[4,272,128]{2,1,0:T(8,128)(2,1)S(1)} async-done(((bf16[4,272,128]{2,1,0:T(8,128)(2,1)}), bf16[4,272,128]{2,1,0:T(8,128)(2,1)S(1)}, u32[]{:S(2)}, u32[]{:S(2)}) %all-to-all-start.1) | async-done | bytes 278560 | tf_op jit(solution)/shard_map/all_to_all | solution.py:364
  77.6 0.9 shard_map.88.mine_ref
  78.6 2.0 %collective-permute-start.7 = (bf16[256,256]{1,0:T(8,128)(2,1)S(1)}, bf16[256,256]{1,0:T(8,128)(2,1)S(1)}, u32[]{:S(2)}, u32[]{:S(2)}) collective-permute-start(bf16[256,256]{1,0:T(8,128)(2,1)S(1)} %shard_map.88.mine_ref), channel_id=1, source_target_pairs={{0,1},{1,0},{2,3},{3,2},{4,5},{5,4},{6,7},{7,6},{8,9},{9,8},{10,11... | collective-permute-start | bytes 393224 | tf_op jit(solution)/shard_map/ppermute | solution.py:366
  80.6 1.2 %collective-permute-done.7.theirs_ref = bf16[256,256]{1,0:T(8,128)(2,1)S(1)} collective-permute-done((bf16[256,256]{1,0:T(8,128)(2,1)S(1)}, bf16[256,256]{1,0:T(8,128)(2,1)S(1)}, u32[]{:S(2)}, u32[]{:S(2)}) %collective-permute-start.7) | collective-permute-done | bytes 131104 | tf_op jit(solution)/shard_map/ppermute | solution.py:366
  81.8 1.0 %shard_map.90 = bf16[4,256,256]{2,1,0:T(8,128)(2,1)S(1)} custom-call(s32[3]{0:T(128)S(1)} %pad_add_fusion.at_ref, bf16[256,256]{1,0:T(8,128)(2,1)S(1)} %shard_map.88.mine_ref, bf16[256,256]{1,0:T(8,128)(2,1)S(1)} %collective-permute-done.7.theirs_ref, bf16[256,2048]{1,0:T(8,128)(2,1)S(1)} %copy-done, bf16[4,256,256]{2,1,0:T(8,128)(2,1)S(1)} %collective-permute-done.8.other_ref), custom_call_target="tpu_custom_call" | custom-call | flops 536870912 | bytes 1048576 | tf_op jit(solution)/shard_map/pallas_call | solution.py:367
  82.8 12.5 %all_to_all.16.x_ref = bf16[4,256,256]{2,1,0:T(8,128)(2,1)S(1)} all-to-all(bf16[4,256,256]{2,1,0:T(8,128)(2,1)S(1)} %shard_map.90), channel_id=1, replica_groups={{0,2,4,6},{1,3,5,7},{8,10,12,14},{9,11,13,15},{16,18,20,22},{17,19,21,2..., dimensions={0} | all-to-all | bytes 1048576 | tf_op jit(solution)/shard_map/all_to_all | solution.py:370
  95.3 0.7 shard_map.91
  (18 shorter events, 0.0 us)
Async XLA Ops:
  0.9 16.6 %copy-start.4 = (bf16[256,256]{1,0:T(8,128)(2,1)S(1)}, bf16[256,256]{1,0:T(8,128)(2,1)}, u32[]{:S(2)}) copy-start(bf16[256,256]{1,0:T(8,128)(2,1)} %dirs_ref.1) | copy-start | bytes 393220
  14.8 6.8 %collective-permute-start = (bf16[4,256,256]{2,1,0:T(8,128)(2,1)S(1)}, bf16[4,256,256]{2,1,0:T(8,128)(2,1)S(1)}, u32[]{:S(2)}, u32[]{:S(2)}) collective-permute-start(bf16[4,256,256]{2,1,0:T(8,128)(2,1)S(1)} %all_to_all.15.x_ref), channel_id=1, source_target_pairs={{0,1},{1,0},{2,3},{3,2},{4,5},{5,4},{6,7},{7,6},{8,9},{9,8},{10,11... | collective-permute-start | bytes 1572872 | tf_op jit(solution)/shard_map/ppermute | solution.py:339
  17.4 0.7 copy-start.5
  18.1 3.5 %copy-start.1 = (bf16[2048,256]{1,0:T(8,128)(2,1)S(1)}, bf16[2048,256]{1,0:T(8,128)(2,1)}, u32[]{:S(2)}) copy-start(bf16[2048,256]{1,0:T(8,128)(2,1)} %wq_ref.1) | copy-start | bytes 3145732
  18.1 3.5 %copy-start.2 = (bf16[2048,256]{1,0:T(8,128)(2,1)S(1)}, bf16[2048,256]{1,0:T(8,128)(2,1)}, u32[]{:S(2)}) copy-start(bf16[2048,256]{1,0:T(8,128)(2,1)} %wk_ref.1) | copy-start | bytes 3145732
  18.1 3.5 %copy-start.3 = (bf16[2048,256]{1,0:T(8,128)(2,1)S(1)}, bf16[2048,256]{1,0:T(8,128)(2,1)}, u32[]{:S(2)}) copy-start(bf16[2048,256]{1,0:T(8,128)(2,1)} %wv_ref.1) | copy-start | bytes 3145732
  21.6 2.0 %copy-start.6 = (bf16[2,256,256]{2,1,0:T(8,128)(2,1)}, bf16[2,256,256]{2,1,0:T(8,128)(2,1)S(1)}, u32[]{:S(2)}) copy-start(bf16[2,256,256]{2,1,0:T(8,128)(2,1)S(1)} %get-tuple-element.40.t_ref) | copy-start | bytes 786436
  21.6 30.2 %copy-start = (bf16[256,2048]{1,0:T(8,128)(2,1)S(1)}, bf16[256,2048]{1,0:T(8,128)(2,1)}, u32[]{:S(2)}) copy-start(bf16[256,2048]{1,0:T(8,128)(2,1)} %wo_ref.3) | copy-start | bytes 3145732
  23.6 4.1 %collective-permute-start.1 = (bf16[912,128]{1,0:T(8,128)(2,1)S(1)}, bf16[912,128]{1,0:T(8,128)(2,1)S(1)}, u32[]{:S(2)}, u32[]{:S(2)}) collective-permute-start(bf16[912,128]{1,0:T(8,128)(2,1)S(1)} %get-tuple-element.28), channel_id=1, source_target_pairs={{0,0},{1,16},{2,2},{3,18},{4,4},{5,20},{6,6},{7,22},{8,8},{9,24},{... | collective-permute-start | bytes 700424 | tf_op jit(solution)/shard_map/ppermute | solution.py:347
  24.2 10.2 %collective-permute-start.2 = (bf16[912,128]{1,0:T(8,128)(2,1)S(1)}, bf16[912,128]{1,0:T(8,128)(2,1)S(1)}, u32[]{:S(2)}, u32[]{:S(2)}) collective-permute-start(bf16[912,128]{1,0:T(8,128)(2,1)S(1)} %get-tuple-element.29), channel_id=1, source_target_pairs={{0,8},{1,24},{2,10},{3,26},{4,12},{5,28},{6,14},{7,30},{8,0},{9,16... | collective-permute-start | bytes 700424 | tf_op jit(solution)/shard_map/ppermute | solution.py:348
  35.2 11.1 %collective-permute-start.3 = (bf16[1152,128]{1,0:T(8,128)(2,1)S(1)}, bf16[1152,128]{1,0:T(8,128)(2,1)S(1)}, u32[]{:S(2)}, u32[]{:S(2)}) collective-permute-start(bf16[1152,128]{1,0:T(8,128)(2,1)S(1)} %get-tuple-element.31), channel_id=1, source_target_pairs={{0,32},{8,40},{16,48},{24,56},{32,64},{40,72},{48,80},{56,88},{64,... | collective-permute-start | bytes 884744 | tf_op jit(solution)/shard_map/ppermute | solution.py:358
  38.2 16.3 %collective-permute-start.6 = (bf16[1152,128]{1,0:T(8,128)(2,1)S(1)}, bf16[1152,128]{1,0:T(8,128)(2,1)S(1)}, u32[]{:S(2)}, u32[]{:S(2)}) collective-permute-start(bf16[1152,128]{1,0:T(8,128)(2,1)S(1)} %get-tuple-element.31), channel_id=1, source_target_pairs={{0,1},{1,32},{2,3},{3,34},{4,5},{5,36},{6,7},{7,38},{8,9},{9,40},{... | collective-permute-start | bytes 884744 | tf_op jit(solution)/shard_map/ppermute | solution.py:357
  46.4 10.1 %collective-permute-start.4 = (bf16[1152,128]{1,0:T(8,128)(2,1)S(1)}, bf16[1152,128]{1,0:T(8,128)(2,1)S(1)}, u32[]{:S(2)}, u32[]{:S(2)}) collective-permute-start(bf16[1152,128]{1,0:T(8,128)(2,1)S(1)} %collective-permute-done.3.d2_ref), channel_id=1, source_target_pairs={{0,1},{1,32},{2,3},{3,34},{4,5},{5,36},{6,7},{7,38},{8,9},{9,40},{... | collective-permute-start | bytes 884744 | tf_op jit(solution)/shard_map/ppermute | solution.py:359
  49.9 12.0 %collective-permute-start.5 = (bf16[1152,128]{1,0:T(8,128)(2,1)S(1)}, bf16[1152,128]{1,0:T(8,128)(2,1)S(1)}, u32[]{:S(2)}, u32[]{:S(2)}) collective-permute-start(bf16[1152,128]{1,0:T(8,128)(2,1)S(1)} %collective-permute-done.3.d2_ref), channel_id=1, source_target_pairs={{0,32},{8,40},{16,48},{24,56},{32,64},{40,72},{48,80},{56,88},{64,... | collective-permute-start | bytes 884744 | tf_op jit(solution)/shard_map/ppermute | solution.py:360
  52.5 28.1 %collective-permute-start.8 = (bf16[4,256,256]{2,1,0:T(8,128)(2,1)S(1)}, bf16[4,256,256]{2,1,0:T(8,128)(2,1)S(1)}, u32[]{:S(2)}, u32[]{:S(2)}) collective-permute-start(bf16[4,256,256]{2,1,0:T(8,128)(2,1)S(1)} %shard_map.89), channel_id=1, source_target_pairs={{0,1},{1,0},{2,3},{3,2},{4,5},{5,4},{6,7},{7,6},{8,9},{9,8},{10,11... | collective-permute-start | bytes 1572872 | tf_op jit(solution)/shard_map/ppermute | solution.py:341
  64.8 12.8 %all-to-all-start.1 = ((bf16[4,272,128]{2,1,0:T(8,128)(2,1)}), bf16[4,272,128]{2,1,0:T(8,128)(2,1)S(1)}, u32[]{:S(2)}, u32[]{:S(2)}) async-start(bf16[4,272,128]{2,1,0:T(8,128)(2,1)} %shard_map.86), calls=%async_computation.1 | async-start | bytes 557056 | tf_op jit(solution)/shard_map/all_to_all | solution.py:364
  70.2 0.9 copy-start.7
  78.6 3.2 %collective-permute-start.7 = (bf16[256,256]{1,0:T(8,128)(2,1)S(1)}, bf16[256,256]{1,0:T(8,128)(2,1)S(1)}, u32[]{:S(2)}, u32[]{:S(2)}) collective-permute-start(bf16[256,256]{1,0:T(8,128)(2,1)S(1)} %shard_map.88.mine_ref), channel_id=1, source_target_pairs={{0,1},{1,0},{2,3},{3,2},{4,5},{5,4},{6,7},{7,6},{8,9},{9,8},{10,11... | collective-permute-start | bytes 393224 | tf_op jit(solution)/shard_map/ppermute | solution.py:366

commit v4 on v2

--- a/solution.py
+++ b/solution.py
@@ -27,15 +27,21 @@
     return lax.dot_general(a, b, dims, preferred_element_type=F32)
 
 
+def split(a):
+    high = a.astype(BF16)
+    return high, (a - high.astype(F32)).astype(BF16)
+
+
 def exact(a, b):
-    return lax.dot_general(a, b, NN, precision=lax.Precision.HIGHEST, preferred_element_type=F32)
-
-
-def call(body, outs, ins, flops=0, smem=0):
+    (ah, al), (bh, bl) = split(a), split(b)
+    return dot(ah, bh) + (dot(ah, bl) + dot(al, bh))
+
+
+def call(body, outs, ins, flops=0, smem=0, late=0):
     return pl.pallas_call(
         body,
         out_shape=outs,
-        in_specs=[SMEM] * smem + [VMEM] * (ins - smem),
+        in_specs=[SMEM] * smem + [VMEM] * (ins - smem) + [pl.BlockSpec(memory_space=pl.ANY)] * late,
         out_specs=jax.tree.map(lambda _: VMEM, outs),
         compiler_params=pltpu.CompilerParams(vmem_limit_bytes=48 * 2**20),
         cost_estimate=pl.CostEstimate(flops=flops, bytes_accessed=2**20, transcendentals=0),
@@ -44,13 +50,11 @@
 
 def lower_inverses(blocks, row, col):
     eye = (row == col).astype(F32)
-    same = (row // 8) == (col // 8)
+    same = (row // 4) == (col // 4)
     small = [jnp.where(same, b, 0.0) for b in blocks]
     squares = [exact(s, s) for s in small]
-    fourths = [exact(s, s) for s in squares]
-    firsts = [exact(eye - s, eye + q) for s, q in zip(small, squares)]
-    found = [exact(f, eye + q) for f, q in zip(firsts, fourths)]
-    size = 8
+    found = [exact(eye - s, eye + q) for s, q in zip(small, squares)]
+    size = 4
     while size < DH:
         off = ((row // (2 * size)) == (col // (2 * size))) & ((row // size) != (col // size))
         left = [exact(x, jnp.where(off, b, 0.0)) for x, b in zip(found, blocks)]
@@ -59,7 +63,8 @@
     return found
 
 
-def directions_kernel(dirs_ref, beta_ref, w_ref, t_ref, u_ref, y_ref, a_ref):
+def directions_kernel(dirs_ref, beta_ref, w_ref, t_ref, u_ref, y_ref, a_ref, mark_ref):
+    mark_ref[...] = jnp.zeros((8, DH), F32)
     row = lax.broadcasted_iota(jnp.int32, (TOK, TOK), 0)
     col = lax.broadcasted_iota(jnp.int32, (TOK, TOK), 1)
     strict = row > col
@@ -96,7 +101,7 @@
 
 def project_kernel(
     at_ref, hop_ref, x_ref, o_ref, wq_ref, wk_ref, wv_ref, w_ref, u_ref, y_ref, a_ref,
-    p0_ref, p1_ref, q_ref, k_ref, v_ref,
+    mark_ref, p0_ref, p1_ref, q_ref, k_ref, v_ref,
 ):
     def product(weights):
         total = None
@@ -107,6 +112,7 @@
                 total = term if total is None else total + term
         return total.astype(BF16)
 
+    del mark_ref
     query, key, value = product(wq_ref), product(wk_ref), product(wv_ref)
     for h in range(2):
         cut = slice(h * DH, (h + 1) * DH)
@@ -317,22 +323,23 @@
     down = [(b, b + 4) for b in range(60)]
     twin = [(h, h ^ 1) for h in range(8)]
 
-    w, t, u, y, a = call(
+    w, t, u, y, a, mark = call(
         directions_kernel,
-        [shape((2, TOK, DH)), shape((2, TOK, TOK)), shape((2, TOK, DH)), shape((2, TOK, DH)), shape((2, DH, DH))],
+        [shape((2, TOK, DH)), shape((2, TOK, TOK)), shape((2, TOK, DH)), shape((2, TOK, DH)), shape((2, DH, DH)), shape((8, DH), F32)],
         2, flops=2**32,
     )(reflect_dir, strength)
     planes = [[0, 2, 4, 6], [1, 3, 5, 7]]
     copies = jnp.broadcast_to(inputs[None], (4, TOK, 256))
     gathered = lax.all_to_all(copies, "head", 0, 0, axis_index_groups=planes)
+    gathered, mark = lax.optimization_barrier((gathered, mark))
     other = lax.ppermute(gathered, "head", twin)
     halves = call(halves_kernel, shape((4, 256, 256)), 2, smem=1)(at, w_out)
     other_out = lax.ppermute(halves, "head", twin)
     p0, p1, q, k, v = call(
         project_kernel,
         [shape((PACK, DH)), shape((PACK, DH))] + [shape((2, TOK, DH))] * 3,
-        11, smem=2, flops=2**30,
-    )(at, hop_count, gathered, other, w_query, w_key, w_value, w, u, y, a)
+        11, smem=2, flops=2**30, late=1,
+    )(at, hop_count, gathered, other, w_query, w_key, w_value, w, u, y, a, mark)
     r0 = lax.ppermute(p0, both, there[0])
     r1 = lax.ppermute(p1, both, there[1])
     acc, lse = call(

time: 96.7 us -> 95.1 us (0.983)
  blocking collectives: 26.5 us -> 12.7 us
  waiting for transfers between devices: 18.1 us -> 24.1 us
  starting transfers between devices: 33.3 us -> 37 us
  local copies, waits for them, and re-layouts: 1.56 us -> 5.17 us
    all_to_all x1 -> x0, blocking collectives: 13.9 us -> none  [shards(): gathered = lax.all_to_all(copies, 'head', 0, 0, axis_index_groups=planes)]
    all_to_all x0 -> x1, waiting for transfers between devices: none -> 4.64 us  [shards(): gathered = lax.all_to_all(copies, 'head', 0, 0, axis_index_groups=planes)]
    all_to_all x0 -> x1, starting transfers between devices: none -> 4.59 us  [shards(): gathered = lax.all_to_all(copies, 'head', 0, 0, axis_index_groups=planes)]
    unnamed x12 -> x20, local copies, waits for them, and re-layouts: 0.62 us -> 3.43 us
    ppermute x1, starting transfers between devices: 7.77 us -> 6.6 us  [shards(): theirs = lax.ppermute(mine, 'head', twin)]
    ppermute x1, waiting for transfers between devices: 0.01 us -> 1.11 us  [shards(): other = lax.ppermute(gathered, 'head', twin)]
  transfers between devices with their start and end apart: 11 -> 12, of which waited for: 5 -> 7; matrix products, arithmetic and copies ran while one was open for 0% -> 0% of each run, Pallas kernels for 12% -> 11%
where the time goes in v4:
time: 95.1 us; the launch traced here: 94.6 us
  starting transfers between devices  37 us (39%)
  waiting for transfers between devices  24.1 us (25%)
  Pallas kernels  14.7 us (15%)
  blocking collectives  12.7 us (13%)
  local copies, waits for them, and re-layouts  5.17 us (5%)
    all_to_all x1, blocking collectives, shards(): pieces = lax.all_to_all(partial, 'head', 0, 0, axis_index_groups=planes)  12.7 us
    ppermute x1, waiting for transfers between devices, shards(): r1 = lax.ppermute(p1, both, there[1])  6.75 us
    ppermute x1, starting transfers between devices, shards(): theirs = lax.ppermute(mine, 'head', twin)  6.6 us
    ppermute x1, waiting for transfers between devices, shards(): d4 = lax.ppermute(d2, 'ctx', down)  5.47 us
    all_to_all x1, waiting for transfers between devices, shards(): gathered = lax.all_to_all(copies, 'head', 0, 0, axis_index_groups=planes)  4.64 us
    all_to_all x1, starting transfers between devices, shards(): gathered = lax.all_to_all(copies, 'head', 0, 0, axis_index_groups=planes)  4.59 us
    ppermute x1, starting transfers between devices, shards(): d1 = lax.ppermute(own_pair, both, follow)  4.39 us
    ppermute x1, starting transfers between devices, shards(): g1 = lax.ppermute(o1, both, back[1])  4.37 us
  transfers between devices with their start and end apart: 12, of which 7 were waited for; matrix products, arithmetic and copies ran while one was open for 0% of the time, Pallas kernels for 11%

profile of v4, /device:TPU:384, one launch (start us, length us, event | category | flops | bytes accessed | tf_op | source)
XLA Modules:
  0.0 94.6 jit_solution(12252978843744890218)
XLA Ops:
  0.0 1.7 %broadcast_in_dim.2 = bf16[4,256,256]{2,1,0:T(8,128)(2,1)} broadcast(bf16[256,256]{1,0:T(8,128)(2,1)} %param.8), dimensions={1,2} | broadcast | bytes 655360 | tf_op jit(solution)/shard_map/broadcast_in_dim | solution.py:332
  1.8 4.6 %all-to-all-start = ((bf16[4,256,256]{2,1,0:T(8,128)(2,1)}), bf16[4,256,256]{2,1,0:T(8,128)(2,1)S(1)}, u32[]{:S(2)}, u32[]{:S(2)}) async-start(bf16[4,256,256]{2,1,0:T(8,128)(2,1)} %broadcast_in_dim.2), calls=%async_computation | async-start | bytes 1048576 | tf_op jit(solution)/shard_map/all_to_all | solution.py:333
  6.4 3.5 %shard_map.82 = (bf16[2,256,128]{2,1,0:T(8,128)(2,1)S(1)}, bf16[2,256,256]{2,1,0:T(8,128)(2,1)S(1)}, bf16[2,256,128]{2,1,0:T(8,128)(2,1)S(1)}, bf16[2,256,128]{2...) custom-call(bf16[256,256]{1,0:T(8,128)(2,1)S(1)} %copy-done.6, f32[2,256]{1,0:T(2,128)S(1)} %copy-done.7), custom_call_target="tpu_custom_call" | custom-call | flops 4294967296 | bytes 1048576 | tf_op jit(solution)/shard_map/pallas_call | solution.py:326
  10.5 0.7 copy-done.8
  11.2 4.6 %all-to-all-done.x_ref = bf16[4,256,256]{2,1,0:T(8,128)(2,1)S(1)} async-done(((bf16[4,256,256]{2,1,0:T(8,128)(2,1)}), bf16[4,256,256]{2,1,0:T(8,128)(2,1)S(1)}, u32[]{:S(2)}, u32[]{:S(2)}) %all-to-all-start) | async-done | bytes 524320 | tf_op jit(solution)/shard_map/all_to_all | solution.py:333
  15.8 1.9 %collective-permute-start = (bf16[4,256,256]{2,1,0:T(8,128)(2,1)S(1)}, bf16[4,256,256]{2,1,0:T(8,128)(2,1)S(1)}, u32[]{:S(2)}, u32[]{:S(2)}) collective-permute-start(bf16[4,256,256]{2,1,0:T(8,128)(2,1)S(1)} %all-to-all-done.x_ref), channel_id=1, source_target_pairs={{0,1},{1,0},{2,3},{3,2},{4,5},{5,4},{6,7},{7,6},{8,9},{9,8},{10,11... | collective-permute-start | bytes 1572872 | tf_op jit(solution)/shard_map/ppermute | solution.py:335
  18.5 1.1 %collective-permute-done.o_ref = bf16[4,256,256]{2,1,0:T(8,128)(2,1)S(1)} collective-permute-done((bf16[4,256,256]{2,1,0:T(8,128)(2,1)S(1)}, bf16[4,256,256]{2,1,0:T(8,128)(2,1)S(1)}, u32[]{:S(2)}, u32[]{:S(2)}) %collective-permute-start) | collective-permute-done | bytes 524320 | tf_op jit(solution)/shard_map/ppermute | solution.py:335
  19.6 1.2 %copy-done.3 = bf16[2048,256]{1,0:T(8,128)(2,1)S(1)} copy-done((bf16[2048,256]{1,0:T(8,128)(2,1)S(1)}, bf16[2048,256]{1,0:T(8,128)(2,1)}, u32[]{:S(2)}) %copy-start.3) | copy-done | bytes 1048600
  20.9 0.8 copy-done.5
  21.7 1.9 %shard_map.83 = (bf16[912,128]{1,0:T(8,128)(2,1)S(1)}, bf16[912,128]{1,0:T(8,128)(2,1)S(1)}, bf16[2,256,128]{2,1,0:T(8,128)(2,1)S(1)}, bf16[2,256,128]{2,1,0:T(8,128)(2,1)S(1)}, bf16[2,256,128]{2,1,0:T(8,128)(2,1)S(1)}) custom-call(s32[3]{0:T(128)S(1)} %pad_add_fusion.at_ref, s32[1]{0:T(128)S(6)} %copy.9.hop_ref, ...), custom_call_target="tpu_custom_call" | custom-call | flops 1073741824 | bytes 1048576 | tf_op jit(solution)/shard_map/pallas_call | solution.py:338
  23.6 0.7 collective-permute-start.1
  24.3 3.4 %collective-permute-start.2 = (bf16[912,128]{1,0:T(8,128)(2,1)S(1)}, bf16[912,128]{1,0:T(8,128)(2,1)S(1)}, u32[]{:S(2)}, u32[]{:S(2)}) collective-permute-start(bf16[912,128]{1,0:T(8,128)(2,1)S(1)} %get-tuple-element.37), channel_id=1, source_target_pairs={{0,8},{1,24},{2,10},{3,26},{4,12},{5,28},{6,14},{7,30},{8,0},{9,16... | collective-permute-start | bytes 700424 | tf_op jit(solution)/shard_map/ppermute | solution.py:344
  27.7 6.7 %collective-permute-done.2.r1_ref = bf16[912,128]{1,0:T(8,128)(2,1)S(1)} collective-permute-done((bf16[912,128]{1,0:T(8,128)(2,1)S(1)}, bf16[912,128]{1,0:T(8,128)(2,1)S(1)}, u32[]{:S(2)}, u32[]{:S(2)}) %collective-permute-start.2) | collective-permute-done | bytes 233504 | tf_op jit(solution)/shard_map/ppermute | solution.py:344
  34.5 0.8 shard_map.84
  35.2 2.9 %collective-permute-start.3 = (bf16[1152,128]{1,0:T(8,128)(2,1)S(1)}, bf16[1152,128]{1,0:T(8,128)(2,1)S(1)}, u32[]{:S(2)}, u32[]{:S(2)}) collective-permute-start(bf16[1152,128]{1,0:T(8,128)(2,1)S(1)} %get-tuple-element.39), channel_id=1, source_target_pairs={{0,32},{8,40},{16,48},{24,56},{32,64},{40,72},{48,80},{56,88},{64,... | collective-permute-start | bytes 884744 | tf_op jit(solution)/shard_map/ppermute | solution.py:354
  38.2 4.4 %collective-permute-start.6 = (bf16[1152,128]{1,0:T(8,128)(2,1)S(1)}, bf16[1152,128]{1,0:T(8,128)(2,1)S(1)}, u32[]{:S(2)}, u32[]{:S(2)}) collective-permute-start(bf16[1152,128]{1,0:T(8,128)(2,1)S(1)} %get-tuple-element.39), channel_id=1, source_target_pairs={{0,1},{1,32},{2,3},{3,34},{4,5},{5,36},{6,7},{7,38},{8,9},{9,40},{... | collective-permute-start | bytes 884744 | tf_op jit(solution)/shard_map/ppermute | solution.py:353
  42.6 3.8 %collective-permute-done.3.d2_ref = bf16[1152,128]{1,0:T(8,128)(2,1)S(1)} collective-permute-done((bf16[1152,128]{1,0:T(8,128)(2,1)S(1)}, bf16[1152,128]{1,0:T(8,128)(2,1)S(1)}, u32[]{:S(2)}, u32[]{:S(2)}) %collective-permute-start.3) | collective-permute-done | bytes 294944 | tf_op jit(solution)/shard_map/ppermute | solution.py:354
  46.4 3.6 %collective-permute-start.4 = (bf16[1152,128]{1,0:T(8,128)(2,1)S(1)}, bf16[1152,128]{1,0:T(8,128)(2,1)S(1)}, u32[]{:S(2)}, u32[]{:S(2)}) collective-permute-start(bf16[1152,128]{1,0:T(8,128)(2,1)S(1)} %collective-permute-done.3.d2_ref), channel_id=1, source_target_pairs={{0,1},{1,32},{2,3},{3,34},{4,5},{5,36},{6,7},{7,38},{8,9},{9,40},{... | collective-permute-start | bytes 884744 | tf_op jit(solution)/shard_map/ppermute | solution.py:355
  50.0 1.9 %collective-permute-start.5 = (bf16[1152,128]{1,0:T(8,128)(2,1)S(1)}, bf16[1152,128]{1,0:T(8,128)(2,1)S(1)}, u32[]{:S(2)}, u32[]{:S(2)}) collective-permute-start(bf16[1152,128]{1,0:T(8,128)(2,1)S(1)} %collective-permute-done.3.d2_ref), channel_id=1, source_target_pairs={{0,32},{8,40},{16,48},{24,56},{32,64},{40,72},{48,80},{56,88},{64,... | collective-permute-start | bytes 884744 | tf_op jit(solution)/shard_map/ppermute | solution.py:356
  52.5 1.9 %collective-permute-start.10 = (bf16[4,256,256]{2,1,0:T(8,128)(2,1)S(1)}, bf16[4,256,256]{2,1,0:T(8,128)(2,1)S(1)}, u32[]{:S(2)}, u32[]{:S(2)}) collective-permute-start(bf16[4,256,256]{2,1,0:T(8,128)(2,1)S(1)} %shard_map.89), channel_id=1, source_target_pairs={{0,1},{1,0},{2,3},{3,2},{4,5},{5,4},{6,7},{7,6},{8,9},{9,8},{10,11... | collective-permute-start | bytes 1572872 | tf_op jit(solution)/shard_map/ppermute | solution.py:337
  54.5 2.0 %shard_map.85 = (f32[2,256,128]{2,1,0:T(8,128)S(1)}, f32[2,256,128]{2,1,0:T(8,128)S(1)}, f32[2,256,128]{2,1,0:T(8,128)S(1)}, bf16[2,256,128]{2,1,0:T(8,128)(2,1)S(1)}) custom-call(s32[3]{0:T(128)S(1)} %pad_add_fusion.at_ref, bf16[3,2,256,128]{3,2,1,0:T(8,128)(2,1)S(1)} %get-tuple-element.40.q_ref, f32[2,16,128]{2,1,0:T(8,128)S(1)} %get-tuple-element.38.hop_ref, ...), custom_call_target="tpu_custom_call" | custom-call | flops 2147483648 | bytes 1048576 | tf_op jit(solution)/shard_map/pallas_call | solution.py:358
  56.5 5.5 %collective-permute-done.5.d4_ref = bf16[1152,128]{1,0:T(8,128)(2,1)S(1)} collective-permute-done((bf16[1152,128]{1,0:T(8,128)(2,1)S(1)}, bf16[1152,128]{1,0:T(8,128)(2,1)S(1)}, u32[]{:S(2)}, u32[]{:S(2)}) %collective-permute-start.5) | collective-permute-done | bytes 294944 | tf_op jit(solution)/shard_map/ppermute | solution.py:356
  62.0 2.1 %shard_map.86 = (bf16[272,128]{1,0:T(8,128)(2,1)S(1)}, bf16[272,128]{1,0:T(8,128)(2,1)S(1)}) custom-call(s32[3]{0:T(128)S(1)} %pad_add_fusion.at_ref, f32[2,16,128]{2,1,0:T(8,128)S(1)} %get-tuple-element.38.hop_ref, bf16[1152,128]{1,0:T(8,128)(2,1)S(1)} %collective-permute-done.4.d3_ref, bf16[1152,128]{1,0:T(8,128)(2,1)S(1)} %collective-permute-done.5.d4_ref, ...), custom_call_target="tpu_custom_call" | custom-call | flops 1073741824 | bytes 1048576 | tf_op jit(solution)/shard_map/pallas_call | solution.py:359
  64.8 4.4 %collective-permute-start.8 = (bf16[272,128]{1,0:T(8,128)(2,1)S(1)}, bf16[272,128]{1,0:T(8,128)(2,1)S(1)}, u32[]{:S(2)}, u32[]{:S(2)}) collective-permute-start(bf16[272,128]{1,0:T(8,128)(2,1)S(1)} %get-tuple-element.46), channel_id=1, source_target_pairs={{8,0},{24,1},{10,2},{26,3},{12,4},{28,5},{14,6},{30,7},{0,8},{16,9... | collective-permute-start | bytes 208904 | tf_op jit(solution)/shard_map/ppermute | solution.py:363
  69.1 1.1 %shard_map.87 = (f32[2,256,128]{2,1,0:T(8,128)S(1)}, f32[2,256,128]{2,1,0:T(8,128)S(1)}) custom-call(bf16[2,256,128]{2,1,0:T(8,128)(2,1)S(1)} %get-tuple-element.47.q_ref, bf16[2,256,128]{2,1,0:T(8,128)(2,1)S(1)} %get-tuple-element.48.k_ref, bf16[2,256,128]{2,1,0:T(8,128)(2,1)S(1)} %get-tuple-element.49.v_ref, ...), custom_call_target="tpu_custom_call" | custom-call | flops 2147483648 | bytes 1048576 | tf_op jit(solution)/shard_map/pallas_call | solution.py:345
  70.3 1.3 %collective-permute-done.8.g1_ref = bf16[272,128]{1,0:T(8,128)(2,1)S(1)} collective-permute-done((bf16[272,128]{1,0:T(8,128)(2,1)S(1)}, bf16[272,128]{1,0:T(8,128)(2,1)S(1)}, u32[]{:S(2)}, u32[]{:S(2)}) %collective-permute-start.8) | collective-permute-done | bytes 69664 | tf_op jit(solution)/shard_map/ppermute | solution.py:363
  71.6 1.0 %shard_map.88.mine_ref = bf16[256,256]{1,0:T(8,128)(2,1)S(1)} custom-call(s32[3]{0:T(128)S(1)} %pad_add_fusion.at_ref, bf16[272,128]{1,0:T(8,128)(2,1)S(1)} %collective-permute-done.7.g0_ref, bf16[272,128]{1,0:T(8,128)(2,1)S(1)} %collective-permute-done.8.g1_ref, f32[2,256,128]{2,1,0:T(8,128)S(1)} %get-tuple-element.51.acc_ref, ...), custom_call_target="tpu_custom_call" | custom-call | flops 268435456 | bytes 1048576 | tf_op jit(solution)/shard_map/pallas_call | solution.py:364
  72.6 6.6 %collective-permute-start.9 = (bf16[256,256]{1,0:T(8,128)(2,1)S(1)}, bf16[256,256]{1,0:T(8,128)(2,1)S(1)}, u32[]{:S(2)}, u32[]{:S(2)}) collective-permute-start(bf16[256,256]{1,0:T(8,128)(2,1)S(1)} %shard_map.88.mine_ref), channel_id=1, source_target_pairs={{0,1},{1,0},{2,3},{3,2},{4,5},{5,4},{6,7},{7,6},{8,9},{9,8},{10,11... | collective-permute-start | bytes 393224 | tf_op jit(solution)/shard_map/ppermute | solution.py:365
  79.2 1.0 %collective-permute-done.9.theirs_ref = bf16[256,256]{1,0:T(8,128)(2,1)S(1)} collective-permute-done((bf16[256,256]{1,0:T(8,128)(2,1)S(1)}, bf16[256,256]{1,0:T(8,128)(2,1)S(1)}, u32[]{:S(2)}, u32[]{:S(2)}) %collective-permute-start.9) | collective-permute-done | bytes 131104 | tf_op jit(solution)/shard_map/ppermute | solution.py:365
  80.2 1.0 %shard_map.90 = bf16[4,256,256]{2,1,0:T(8,128)(2,1)S(1)} custom-call(s32[3]{0:T(128)S(1)} %pad_add_fusion.at_ref, bf16[256,256]{1,0:T(8,128)(2,1)S(1)} %shard_map.88.mine_ref, bf16[256,256]{1,0:T(8,128)(2,1)S(1)} %collective-permute-done.9.theirs_ref, bf16[256,2048]{1,0:T(8,128)(2,1)S(1)} %copy-done, bf16[4,256,256]{2,1,0:T(8,128)(2,1)S(1)} %collective-permute-done.10.other_ref), custom_call_target="tpu_custom_call" | custom-call | flops 536870912 | bytes 1048576 | tf_op jit(solution)/shard_map/pallas_call | solution.py:366
  81.2 12.7 %all_to_all.10.x_ref = bf16[4,256,256]{2,1,0:T(8,128)(2,1)S(1)} all-to-all(bf16[4,256,256]{2,1,0:T(8,128)(2,1)S(1)} %shard_map.90), channel_id=1, replica_groups={{0,2,4,6},{1,3,5,7},{8,10,12,14},{9,11,13,15},{16,18,20,22},{17,19,21,2..., dimensions={0} | all-to-all | bytes 1048576 | tf_op jit(solution)/shard_map/all_to_all | solution.py:369
  93.9 0.7 shard_map.91
  (25 shorter events, 2.0 us)
Async XLA Ops:
  1.7 4.6 %copy-start.6 = (bf16[256,256]{1,0:T(8,128)(2,1)S(1)}, bf16[256,256]{1,0:T(8,128)(2,1)}, u32[]{:S(2)}) copy-start(bf16[256,256]{1,0:T(8,128)(2,1)} %dirs_ref.1) | copy-start | bytes 393220
  1.8 4.6 %copy-start.7 = (f32[2,256]{1,0:T(2,128)S(1)}, f32[2,256]{1,0:T(2,128)}, u32[]{:S(2)}) copy-start(f32[2,256]{1,0:T(2,128)} %beta_ref.1) | copy-start | bytes 6148
  1.8 14.1 %all-to-all-start = ((bf16[4,256,256]{2,1,0:T(8,128)(2,1)}), bf16[4,256,256]{2,1,0:T(8,128)(2,1)S(1)}, u32[]{:S(2)}, u32[]{:S(2)}) async-start(bf16[4,256,256]{2,1,0:T(8,128)(2,1)} %broadcast_in_dim.2), calls=%async_computation | async-start | bytes 1048576 | tf_op jit(solution)/shard_map/all_to_all | solution.py:333
  6.4 13.3 %copy-start.1 = (bf16[2048,256]{1,0:T(8,128)(2,1)S(1)}, bf16[2048,256]{1,0:T(8,128)(2,1)}, u32[]{:S(2)}) copy-start(bf16[2048,256]{1,0:T(8,128)(2,1)} %wq_ref.1) | copy-start | bytes 3145732
  6.4 13.3 %copy-start.2 = (bf16[2048,256]{1,0:T(8,128)(2,1)S(1)}, bf16[2048,256]{1,0:T(8,128)(2,1)}, u32[]{:S(2)}) copy-start(bf16[2048,256]{1,0:T(8,128)(2,1)} %wk_ref.1) | copy-start | bytes 3145732
  9.8 0.6 copy-start.4
  10.5 0.7 copy-start.8
  15.8 3.8 %collective-permute-start = (bf16[4,256,256]{2,1,0:T(8,128)(2,1)S(1)}, bf16[4,256,256]{2,1,0:T(8,128)(2,1)S(1)}, u32[]{:S(2)}, u32[]{:S(2)}) collective-permute-start(bf16[4,256,256]{2,1,0:T(8,128)(2,1)S(1)} %all-to-all-done.x_ref), channel_id=1, source_target_pairs={{0,1},{1,0},{2,3},{3,2},{4,5},{5,4},{6,7},{7,6},{8,9},{9,8},{10,11... | collective-permute-start | bytes 1572872 | tf_op jit(solution)/shard_map/ppermute | solution.py:335
  19.6 1.2 %copy-start.3 = (bf16[2048,256]{1,0:T(8,128)(2,1)S(1)}, bf16[2048,256]{1,0:T(8,128)(2,1)}, u32[]{:S(2)}) copy-start(bf16[2048,256]{1,0:T(8,128)(2,1)} %wv_ref.1) | copy-start | bytes 3145732
  20.9 0.8 copy-start.5
  21.7 30.2 %copy-start = (bf16[256,2048]{1,0:T(8,128)(2,1)S(1)}, bf16[256,2048]{1,0:T(8,128)(2,1)}, u32[]{:S(2)}) copy-start(bf16[256,2048]{1,0:T(8,128)(2,1)} %wo_ref.3) | copy-start | bytes 3145732
  23.6 4.1 %collective-permute-start.1 = (bf16[912,128]{1,0:T(8,128)(2,1)S(1)}, bf16[912,128]{1,0:T(8,128)(2,1)S(1)}, u32[]{:S(2)}, u32[]{:S(2)}) collective-permute-start(bf16[912,128]{1,0:T(8,128)(2,1)S(1)} %get-tuple-element.36), channel_id=1, source_target_pairs={{0,0},{1,16},{2,2},{3,18},{4,4},{5,20},{6,6},{7,22},{8,8},{9,24},{... | collective-permute-start | bytes 700424 | tf_op jit(solution)/shard_map/ppermute | solution.py:343
  24.3 10.2 %collective-permute-start.2 = (bf16[912,128]{1,0:T(8,128)(2,1)S(1)}, bf16[912,128]{1,0:T(8,128)(2,1)S(1)}, u32[]{:S(2)}, u32[]{:S(2)}) collective-permute-start(bf16[912,128]{1,0:T(8,128)(2,1)S(1)} %get-tuple-element.37), channel_id=1, source_target_pairs={{0,8},{1,24},{2,10},{3,26},{4,12},{5,28},{6,14},{7,30},{8,0},{9,16... | collective-permute-start | bytes 700424 | tf_op jit(solution)/shard_map/ppermute | solution.py:344
  35.2 11.1 %collective-permute-start.3 = (bf16[1152,128]{1,0:T(8,128)(2,1)S(1)}, bf16[1152,128]{1,0:T(8,128)(2,1)S(1)}, u32[]{:S(2)}, u32[]{:S(2)}) collective-permute-start(bf16[1152,128]{1,0:T(8,128)(2,1)S(1)} %get-tuple-element.39), channel_id=1, source_target_pairs={{0,32},{8,40},{16,48},{24,56},{32,64},{40,72},{48,80},{56,88},{64,... | collective-permute-start | bytes 884744 | tf_op jit(solution)/shard_map/ppermute | solution.py:354
  38.2 16.3 %collective-permute-start.6 = (bf16[1152,128]{1,0:T(8,128)(2,1)S(1)}, bf16[1152,128]{1,0:T(8,128)(2,1)S(1)}, u32[]{:S(2)}, u32[]{:S(2)}) collective-permute-start(bf16[1152,128]{1,0:T(8,128)(2,1)S(1)} %get-tuple-element.39), channel_id=1, source_target_pairs={{0,1},{1,32},{2,3},{3,34},{4,5},{5,36},{6,7},{7,38},{8,9},{9,40},{... | collective-permute-start | bytes 884744 | tf_op jit(solution)/shard_map/ppermute | solution.py:353
  46.4 10.1 %collective-permute-start.4 = (bf16[1152,128]{1,0:T(8,128)(2,1)S(1)}, bf16[1152,128]{1,0:T(8,128)(2,1)S(1)}, u32[]{:S(2)}, u32[]{:S(2)}) collective-permute-start(bf16[1152,128]{1,0:T(8,128)(2,1)S(1)} %collective-permute-done.3.d2_ref), channel_id=1, source_target_pairs={{0,1},{1,32},{2,3},{3,34},{4,5},{5,36},{6,7},{7,38},{8,9},{9,40},{... | collective-permute-start | bytes 884744 | tf_op jit(solution)/shard_map/ppermute | solution.py:355
  50.0 12.0 %collective-permute-start.5 = (bf16[1152,128]{1,0:T(8,128)(2,1)S(1)}, bf16[1152,128]{1,0:T(8,128)(2,1)S(1)}, u32[]{:S(2)}, u32[]{:S(2)}) collective-permute-start(bf16[1152,128]{1,0:T(8,128)(2,1)S(1)} %collective-permute-done.3.d2_ref), channel_id=1, source_target_pairs={{0,32},{8,40},{16,48},{24,56},{32,64},{40,72},{48,80},{56,88},{64,... | collective-permute-start | bytes 884744 | tf_op jit(solution)/shard_map/ppermute | solution.py:356
  52.5 26.7 %collective-permute-start.10 = (bf16[4,256,256]{2,1,0:T(8,128)(2,1)S(1)}, bf16[4,256,256]{2,1,0:T(8,128)(2,1)S(1)}, u32[]{:S(2)}, u32[]{:S(2)}) collective-permute-start(bf16[4,256,256]{2,1,0:T(8,128)(2,1)S(1)} %shard_map.89), channel_id=1, source_target_pairs={{0,1},{1,0},{2,3},{3,2},{4,5},{5,4},{6,7},{7,6},{8,9},{9,8},{10,11... | collective-permute-start | bytes 1572872 | tf_op jit(solution)/shard_map/ppermute | solution.py:337
  62.0 7.1 %copy-start.9 = (bf16[2,256,256]{2,1,0:T(8,128)(2,1)S(1)}, bf16[2,256,256]{2,1,0:T(8,128)(2,1)}, u32[]{:S(2)}) copy-start(bf16[2,256,256]{2,1,0:T(8,128)(2,1)} %copy-done.8) | copy-start | bytes 786436
  64.1 6.2 %collective-permute-start.7 = (bf16[272,128]{1,0:T(8,128)(2,1)S(1)}, bf16[272,128]{1,0:T(8,128)(2,1)S(1)}, u32[]{:S(2)}, u32[]{:S(2)}) collective-permute-start(bf16[272,128]{1,0:T(8,128)(2,1)S(1)} %get-tuple-element.45), channel_id=1, source_target_pairs={{0,0},{16,1},{2,2},{18,3},{4,4},{20,5},{6,6},{22,7},{8,8},{24,9},{... | collective-permute-start | bytes 208904 | tf_op jit(solution)/shard_map/ppermute | solution.py:362
  64.8 6.9 %collective-permute-start.8 = (bf16[272,128]{1,0:T(8,128)(2,1)S(1)}, bf16[272,128]{1,0:T(8,128)(2,1)S(1)}, u32[]{:S(2)}, u32[]{:S(2)}) collective-permute-start(bf16[272,128]{1,0:T(8,128)(2,1)S(1)} %get-tuple-element.46), channel_id=1, source_target_pairs={{8,0},{24,1},{10,2},{26,3},{12,4},{28,5},{14,6},{30,7},{0,8},{16,9... | collective-permute-start | bytes 208904 | tf_op jit(solution)/shard_map/ppermute | solution.py:363
  72.6 7.6 %collective-permute-start.9 = (bf16[256,256]{1,0:T(8,128)(2,1)S(1)}, bf16[256,256]{1,0:T(8,128)(2,1)S(1)}, u32[]{:S(2)}, u32[]{:S(2)}) collective-permute-start(bf16[256,256]{1,0:T(8,128)(2,1)S(1)} %shard_map.88.mine_ref), channel_id=1, source_target_pairs={{0,1},{1,0},{2,3},{3,2},{4,5},{5,4},{6,7},{7,6},{8,9},{9,8},{10,11... | collective-permute-start | bytes 393224 | tf_op jit(solution)/shard_map/ppermute | solution.py:365

commit v5 on v4

--- a/solution.py
+++ b/solution.py
@@ -63,7 +63,7 @@
     return found
 
 
-def directions_kernel(dirs_ref, beta_ref, w_ref, t_ref, u_ref, y_ref, a_ref, mark_ref):
+def directions_kernel(dirs_ref, beta_ref, w_ref, t_ref, mark_ref):
     mark_ref[...] = jnp.zeros((8, DH), F32)
     row = lax.broadcasted_iota(jnp.int32, (TOK, TOK), 0)
     col = lax.broadcasted_iota(jnp.int32, (TOK, TOK), 1)
@@ -89,19 +89,21 @@
         upper = jnp.concatenate([first, jnp.zeros((DH, DH), F32)], axis=1)
         lower = jnp.concatenate([cross, second], axis=1)
         t = (jnp.concatenate([upper, lower], axis=0) * betas[h]).astype(BF16)
-        w = dirs[h]
-        u = dot(t, w, TN).astype(BF16)
-        w_ref[h] = w
+        w_ref[h] = dirs[h]
         t_ref[h] = t
-        u_ref[h] = u
-        y_ref[h] = dot(t, w).astype(BF16)
-        eye = (r == c).astype(F32)
-        a_ref[h] = (eye - dot(u, w, TN)).astype(BF16)
+
+
+def copies_kernel(x_ref, out_ref, sems):
+    copies = [pltpu.make_async_copy(x_ref, out_ref.at[p], sems.at[p]) for p in range(4)]
+    for copy in copies:
+        copy.start()
+    for copy in copies:
+        copy.wait()
 
 
 def project_kernel(
-    at_ref, hop_ref, x_ref, o_ref, wq_ref, wk_ref, wv_ref, w_ref, u_ref, y_ref, a_ref,
-    mark_ref, p0_ref, p1_ref, q_ref, k_ref, v_ref,
+    at_ref, hop_ref, x_ref, o_ref, wq_ref, wk_ref, wv_ref, w_ref, t_ref,
+    mark_ref, p0_ref, p1_ref, q_ref, k_ref, v_ref, c_ref,
 ):
     def product(weights):
         total = None
@@ -122,28 +124,30 @@
     row = lax.broadcasted_iota(jnp.int32, (TOK, TOK), 0)
     col = lax.broadcasted_iota(jnp.int32, (TOK, TOK), 1)
     hops = hop_ref[0].astype(F32)
+    eye = (row == col).astype(F32)[:DH, :DH]
     for j, p_ref in enumerate((p0_ref, p1_ref)):
         h = lax.rem(at_ref[0] + j, 2)
-        q, k, w = q_ref[h], k_ref[h], w_ref[h]
+        q, k, w, t = q_ref[h], k_ref[h], w_ref[h], t_ref[h]
+        u = dot(t, w, TN).astype(BF16)
         qdirs = jnp.where(row >= col, dot(q, w, NT), 0.0).astype(BF16)
         keydirs = jnp.where(col > row, dot(k, w, NT), 0.0).astype(BF16)
-        qhat = q.astype(F32) - dot(qdirs, y_ref[h])
+        coef = dot(qdirs, t).astype(BF16)
+        c_ref[h] = coef
+        qhat = q.astype(F32) - dot(coef, w)
         p_ref[0:TOK] = (qhat * SCALE).astype(BF16)
-        p_ref[TOK : 2 * TOK] = (k.astype(F32) - dot(keydirs, u_ref[h])).astype(BF16)
+        p_ref[TOK : 2 * TOK] = (k.astype(F32) - dot(keydirs, u)).astype(BF16)
         p_ref[2 * TOK : 3 * TOK] = v_ref[h]
-        p_ref[3 * TOK : HOP_ROW] = a_ref[h]
+        p_ref[3 * TOK : HOP_ROW] = (eye - dot(u, w, TN)).astype(BF16)
         p_ref[HOP_ROW:PACK] = jnp.full((16, DH), hops, F32).astype(BF16)
 
 
-def own_kernel(q_ref, k_ref, v_ref, w_ref, t_ref, acc_ref, lse_ref):
+def own_kernel(q_ref, k_ref, v_ref, w_ref, c_ref, acc_ref, lse_ref):
     row = lax.broadcasted_iota(jnp.int32, (TOK, TOK), 0)
     col = lax.broadcasted_iota(jnp.int32, (TOK, TOK), 1)
     for h in range(2):
         q, k, w = q_ref[h], k_ref[h], w_ref[h]
-        qdirs = jnp.where(row >= col, dot(q, w, NT), 0.0).astype(BF16)
         dirkeys = jnp.where(row > col, dot(w, k, NT), 0.0).astype(BF16)
-        coef = dot(qdirs, t_ref[h]).astype(BF16)
-        own = (dot(q, k, NT) - dot(coef, dirkeys)) * SCALE
+        own = (dot(q, k, NT) - dot(c_ref[h], dirkeys)) * SCALE
         own = jnp.where(row >= col, own, NEG)
         top = jnp.max(own, axis=1, keepdims=True)
         prob = jnp.exp2(own - top)
@@ -323,28 +327,34 @@
     down = [(b, b + 4) for b in range(60)]
     twin = [(h, h ^ 1) for h in range(8)]
 
-    w, t, u, y, a, mark = call(
-        directions_kernel,
-        [shape((2, TOK, DH)), shape((2, TOK, TOK)), shape((2, TOK, DH)), shape((2, TOK, DH)), shape((2, DH, DH)), shape((8, DH), F32)],
-        2, flops=2**32,
+    w, t, mark = call(
+        directions_kernel, [shape((2, TOK, DH)), shape((2, TOK, TOK)), shape((8, DH), F32)], 2, flops=2**32
     )(reflect_dir, strength)
     planes = [[0, 2, 4, 6], [1, 3, 5, 7]]
-    copies = jnp.broadcast_to(inputs[None], (4, TOK, 256))
+    copies = pl.pallas_call(
+        copies_kernel,
+        out_shape=shape((4, TOK, 256)),
+        in_specs=[pl.BlockSpec(memory_space=pl.ANY)],
+        out_specs=pl.BlockSpec(memory_space=pl.ANY),
+        scratch_shapes=[pltpu.SemaphoreType.DMA((4,))],
+        compiler_params=pltpu.CompilerParams(vmem_limit_bytes=62 * 2**20),
+        cost_estimate=pl.CostEstimate(flops=0, bytes_accessed=2**20, transcendentals=0),
+    )(inputs)
     gathered = lax.all_to_all(copies, "head", 0, 0, axis_index_groups=planes)
     gathered, mark = lax.optimization_barrier((gathered, mark))
     other = lax.ppermute(gathered, "head", twin)
     halves = call(halves_kernel, shape((4, 256, 256)), 2, smem=1)(at, w_out)
     other_out = lax.ppermute(halves, "head", twin)
-    p0, p1, q, k, v = call(
+    p0, p1, q, k, v, coef = call(
         project_kernel,
-        [shape((PACK, DH)), shape((PACK, DH))] + [shape((2, TOK, DH))] * 3,
-        11, smem=2, flops=2**30, late=1,
-    )(at, hop_count, gathered, other, w_query, w_key, w_value, w, u, y, a, mark)
+        [shape((PACK, DH)), shape((PACK, DH))] + [shape((2, TOK, DH))] * 3 + [shape((2, TOK, TOK))],
+        9, smem=2, flops=2**30, late=1,
+    )(at, hop_count, gathered, other, w_query, w_key, w_value, w, t, mark)
     r0 = lax.ppermute(p0, both, there[0])
     r1 = lax.ppermute(p1, both, there[1])
     acc, lse = call(
         own_kernel, [shape((2, TOK, DH), F32), shape((2, TOK, DH), F32)], 5, flops=2**31
-    )(q, k, v, w, t)
+    )(q, k, v, w, coef)
     qs, own_pair, hops = call(
         pair_kernel,
         [shape((3, 2, TOK, DH)), shape((PAIR, DH)), shape((2, 16, DH), F32)],

time: 95.1 us -> 110 us (1.16)
  Pallas kernels: 14.7 us -> 30.9 us
  local copies, waits for them, and re-layouts: 5.17 us -> 1.25 us
  waiting for transfers between devices: 24.1 us -> 26.2 us
    pallas_call x0 -> x1, Pallas kernels: none -> 17 us  [shards(): pl.pallas_call(copies_kernel, out_shape=shape((4, TOK, 256)), in_specs=[p...]
    all_to_all x1, waiting for transfers between devices: 4.64 us -> 6.82 us  [shards(): gathered = lax.all_to_all(copies, 'head', 0, 0, axis_index_groups=planes)]
    unnamed x20 -> x12, local copies, waits for them, and re-layouts: 3.43 us -> 1.25 us
    broadcast_in_dim x1 -> x0, local copies, waits for them, and re-layouts: 1.75 us -> none  [shards(): copies = jnp.broadcast_to(inputs[None], (4, TOK, 256))]
  transfers between devices with their start and end apart: 12 -> 12, of which waited for: 7 -> 7; matrix products, arithmetic and copies ran while one was open for 0% -> 0% of each run, Pallas kernels for 11% -> 8%
where the time goes in v5:
time: 110 us; the launch traced here: 109 us
  starting transfers between devices  37.3 us (34%)
  Pallas kernels  30.9 us (28%)
  waiting for transfers between devices  26.2 us (24%)
  blocking collectives  12.7 us (12%)
  local copies, waits for them, and re-layouts  1.25 us (1%)
    pallas_call x1, Pallas kernels, shards(): pl.pallas_call(copies_kernel, out_shape=shape((4, TOK, 256)), in_specs=[p...  17 us
    all_to_all x1, blocking collectives, shards(): pieces = lax.all_to_all(partial, 'head', 0, 0, axis_index_groups=planes)  12.7 us
    all_to_all x1, waiting for transfers between devices, shards(): gathered = lax.all_to_all(copies, 'head', 0, 0, axis_index_groups=planes)  6.82 us
    ppermute x1, starting transfers between devices, shards(): theirs = lax.ppermute(mine, 'head', twin)  6.76 us
    ppermute x1, waiting for transfers between devices, shards(): r1 = lax.ppermute(p1, both, there[1])  6.69 us
    ppermute x1, waiting for transfers between devices, shards(): d4 = lax.ppermute(d2, 'ctx', down)  5.47 us
    all_to_all x1, starting transfers between devices, shards(): gathered = lax.all_to_all(copies, 'head', 0, 0, axis_index_groups=planes)  4.61 us
    ppermute x1, starting transfers between devices, shards(): d1 = lax.ppermute(own_pair, both, follow)  4.48 us
  transfers between devices with their start and end apart: 12, of which 7 were waited for; matrix products, arithmetic and copies ran while one was open for 0% of the time, Pallas kernels for 8%

profile of v5, /device:TPU:384, one launch (start us, length us, event | category | flops | bytes accessed | tf_op | source)
XLA Modules:
  0.0 109.4 jit_solution(15068166292834426681)
XLA Ops:
  0.0 17.0 %shard_map.82 = bf16[4,256,256]{2,1,0:T(8,128)(2,1)} custom-call(bf16[256,256]{1,0:T(8,128)(2,1)} %x_ref.1), custom_call_target="tpu_custom_call" | custom-call | bytes 1048576 | tf_op jit(solution)/shard_map/pallas_call | solution.py:334
  17.0 4.6 %all-to-all-start = ((bf16[4,256,256]{2,1,0:T(8,128)(2,1)}), bf16[4,256,256]{2,1,0:T(8,128)(2,1)S(1)}, u32[]{:S(2)}, u32[]{:S(2)}) async-start(bf16[4,256,256]{2,1,0:T(8,128)(2,1)} %shard_map.82), calls=%async_computation | async-start | bytes 1048576 | tf_op jit(solution)/shard_map/all_to_all | solution.py:343
  21.7 2.6 %shard_map.83 = (bf16[2,256,128]{2,1,0:T(8,128)(2,1)S(1)}, bf16[2,256,256]{2,1,0:T(8,128)(2,1)S(1)}, f32[8,128]{1,0:T(8,128)S(1)}) custom-call(bf16[256,256]{1,0:T(8,128)(2,1)S(1)} %copy-done.4, f32[2,256]{1,0:T(2,128)S(1)} %copy-done.5), custom_call_target="tpu_custom_call" | custom-call | flops 4294967296 | bytes 1048576 | tf_op jit(solution)/shard_map/pallas_call | solution.py:330
  24.3 6.8 %all-to-all-done.x_ref = bf16[4,256,256]{2,1,0:T(8,128)(2,1)S(1)} async-done(((bf16[4,256,256]{2,1,0:T(8,128)(2,1)}), bf16[4,256,256]{2,1,0:T(8,128)(2,1)S(1)}, u32[]{:S(2)}, u32[]{:S(2)}) %all-to-all-start) | async-done | bytes 524320 | tf_op jit(solution)/shard_map/all_to_all | solution.py:343
  31.1 1.9 %collective-permute-start = (bf16[4,256,256]{2,1,0:T(8,128)(2,1)S(1)}, bf16[4,256,256]{2,1,0:T(8,128)(2,1)S(1)}, u32[]{:S(2)}, u32[]{:S(2)}) collective-permute-start(bf16[4,256,256]{2,1,0:T(8,128)(2,1)S(1)} %all-to-all-done.x_ref), channel_id=1, source_target_pairs={{0,1},{1,0},{2,3},{3,2},{4,5},{5,4},{6,7},{7,6},{8,9},{9,8},{10,11... | collective-permute-start | bytes 1572872 | tf_op jit(solution)/shard_map/ppermute | solution.py:345
  33.8 1.1 %collective-permute-done.o_ref = bf16[4,256,256]{2,1,0:T(8,128)(2,1)S(1)} collective-permute-done((bf16[4,256,256]{2,1,0:T(8,128)(2,1)S(1)}, bf16[4,256,256]{2,1,0:T(8,128)(2,1)S(1)}, u32[]{:S(2)}, u32[]{:S(2)}) %collective-permute-start) | collective-permute-done | bytes 524320 | tf_op jit(solution)/shard_map/ppermute | solution.py:345
  34.9 1.2 %copy-done.3 = bf16[2048,256]{1,0:T(8,128)(2,1)S(1)} copy-done((bf16[2048,256]{1,0:T(8,128)(2,1)S(1)}, bf16[2048,256]{1,0:T(8,128)(2,1)}, u32[]{:S(2)}) %copy-start.3) | copy-done | bytes 1048600
  36.2 2.2 %shard_map.84 = (bf16[912,128]{1,0:T(8,128)(2,1)S(1)}, bf16[912,128]{1,0:T(8,128)(2,1)S(1)}, bf16[2,256,128]{2,1,0:T(8,128)(2,1)S(1)}, bf16[2,256,128]{2,1,0:T(8...) custom-call(s32[3]{0:T(128)S(1)} %pad_add_fusion.at_ref, s32[1]{0:T(128)S(6)} %copy.9.hop_ref, ...), custom_call_target="tpu_custom_call" | custom-call | flops 1073741824 | bytes 1048576 | tf_op jit(solution)/shard_map/pallas_call | solution.py:348
  38.4 0.7 collective-permute-start.1
  39.0 3.4 %collective-permute-start.2 = (bf16[912,128]{1,0:T(8,128)(2,1)S(1)}, bf16[912,128]{1,0:T(8,128)(2,1)S(1)}, u32[]{:S(2)}, u32[]{:S(2)}) collective-permute-start(bf16[912,128]{1,0:T(8,128)(2,1)S(1)} %get-tuple-element.33), channel_id=1, source_target_pairs={{0,8},{1,24},{2,10},{3,26},{4,12},{5,28},{6,14},{7,30},{8,0},{9,16... | collective-permute-start | bytes 700424 | tf_op jit(solution)/shard_map/ppermute | solution.py:354
  42.5 6.7 %collective-permute-done.2.r1_ref = bf16[912,128]{1,0:T(8,128)(2,1)S(1)} collective-permute-done((bf16[912,128]{1,0:T(8,128)(2,1)S(1)}, bf16[912,128]{1,0:T(8,128)(2,1)S(1)}, u32[]{:S(2)}, u32[]{:S(2)}) %collective-permute-start.2) | collective-permute-done | bytes 233504 | tf_op jit(solution)/shard_map/ppermute | solution.py:354
  49.2 0.8 shard_map.85
  49.9 2.9 %collective-permute-start.3 = (bf16[1152,128]{1,0:T(8,128)(2,1)S(1)}, bf16[1152,128]{1,0:T(8,128)(2,1)S(1)}, u32[]{:S(2)}, u32[]{:S(2)}) collective-permute-start(bf16[1152,128]{1,0:T(8,128)(2,1)S(1)} %get-tuple-element.35), channel_id=1, source_target_pairs={{0,32},{8,40},{16,48},{24,56},{32,64},{40,72},{48,80},{56,88},{64,... | collective-permute-start | bytes 884744 | tf_op jit(solution)/shard_map/ppermute | solution.py:364
  52.9 4.5 %collective-permute-start.6 = (bf16[1152,128]{1,0:T(8,128)(2,1)S(1)}, bf16[1152,128]{1,0:T(8,128)(2,1)S(1)}, u32[]{:S(2)}, u32[]{:S(2)}) collective-permute-start(bf16[1152,128]{1,0:T(8,128)(2,1)S(1)} %get-tuple-element.35), channel_id=1, source_target_pairs={{0,1},{1,32},{2,3},{3,34},{4,5},{5,36},{6,7},{7,38},{8,9},{9,40},{... | collective-permute-start | bytes 884744 | tf_op jit(solution)/shard_map/ppermute | solution.py:363
  57.4 3.6 %collective-permute-done.3.d2_ref = bf16[1152,128]{1,0:T(8,128)(2,1)S(1)} collective-permute-done((bf16[1152,128]{1,0:T(8,128)(2,1)S(1)}, bf16[1152,128]{1,0:T(8,128)(2,1)S(1)}, u32[]{:S(2)}, u32[]{:S(2)}) %collective-permute-start.3) | collective-permute-done | bytes 294944 | tf_op jit(solution)/shard_map/ppermute | solution.py:364
  61.0 3.7 %collective-permute-start.4 = (bf16[1152,128]{1,0:T(8,128)(2,1)S(1)}, bf16[1152,128]{1,0:T(8,128)(2,1)S(1)}, u32[]{:S(2)}, u32[]{:S(2)}) collective-permute-start(bf16[1152,128]{1,0:T(8,128)(2,1)S(1)} %collective-permute-done.3.d2_ref), channel_id=1, source_target_pairs={{0,1},{1,32},{2,3},{3,34},{4,5},{5,36},{6,7},{7,38},{8,9},{9,40},{... | collective-permute-start | bytes 884744 | tf_op jit(solution)/shard_map/ppermute | solution.py:365
  64.7 1.9 %collective-permute-start.5 = (bf16[1152,128]{1,0:T(8,128)(2,1)S(1)}, bf16[1152,128]{1,0:T(8,128)(2,1)S(1)}, u32[]{:S(2)}, u32[]{:S(2)}) collective-permute-start(bf16[1152,128]{1,0:T(8,128)(2,1)S(1)} %collective-permute-done.3.d2_ref), channel_id=1, source_target_pairs={{0,32},{8,40},{16,48},{24,56},{32,64},{40,72},{48,80},{56,88},{64,... | collective-permute-start | bytes 884744 | tf_op jit(solution)/shard_map/ppermute | solution.py:366
  66.6 0.6 shard_map.90
  67.2 1.9 %collective-permute-start.10 = (bf16[4,256,256]{2,1,0:T(8,128)(2,1)S(1)}, bf16[4,256,256]{2,1,0:T(8,128)(2,1)S(1)}, u32[]{:S(2)}, u32[]{:S(2)}) collective-permute-start(bf16[4,256,256]{2,1,0:T(8,128)(2,1)S(1)} %shard_map.90), channel_id=1, source_target_pairs={{0,1},{1,0},{2,3},{3,2},{4,5},{5,4},{6,7},{7,6},{8,9},{9,8},{10,11... | collective-permute-start | bytes 1572872 | tf_op jit(solution)/shard_map/ppermute | solution.py:347
  69.2 2.0 %shard_map.86 = (f32[2,256,128]{2,1,0:T(8,128)S(1)}, f32[2,256,128]{2,1,0:T(8,128)S(1)}, f32[2,256,128]{2,1,0:T(8,128)S(1)}, bf16[2,256,128]{2,1,0:T(8,128)(2,1)S(1)}) custom-call(s32[3]{0:T(128)S(1)} %pad_add_fusion.at_ref, bf16[3,2,256,128]{3,2,1,0:T(8,128)(2,1)S(1)} %get-tuple-element.36.q_ref, f32[2,16,128]{2,1,0:T(8,128)S(1)} %get-tuple-element.34.hop_ref, ...), custom_call_target="tpu_custom_call" | custom-call | flops 2147483648 | bytes 1048576 | tf_op jit(solution)/shard_map/pallas_call | solution.py:368
  71.2 5.5 %collective-permute-done.5.d4_ref = bf16[1152,128]{1,0:T(8,128)(2,1)S(1)} collective-permute-done((bf16[1152,128]{1,0:T(8,128)(2,1)S(1)}, bf16[1152,128]{1,0:T(8,128)(2,1)S(1)}, u32[]{:S(2)}, u32[]{:S(2)}) %collective-permute-start.5) | collective-permute-done | bytes 294944 | tf_op jit(solution)/shard_map/ppermute | solution.py:366
  76.7 2.1 %shard_map.87 = (bf16[272,128]{1,0:T(8,128)(2,1)S(1)}, bf16[272,128]{1,0:T(8,128)(2,1)S(1)}) custom-call(s32[3]{0:T(128)S(1)} %pad_add_fusion.at_ref, f32[2,16,128]{2,1,0:T(8,128)S(1)} %get-tuple-element.34.hop_ref, bf16[1152,128]{1,0:T(8,128)(2,1)S(1)} %collective-permute-done.4.d3_ref, bf16[1152,128]{1,0:T(8,128)(2,1)S(1)} %collective-permute-done.5.d4_ref, ...), custom_call_target="tpu_custom_call" | custom-call | flops 1073741824 | bytes 1048576 | tf_op jit(solution)/shard_map/pallas_call | solution.py:369
  78.8 0.7 collective-permute-start.7
  79.4 4.4 %collective-permute-start.8 = (bf16[272,128]{1,0:T(8,128)(2,1)S(1)}, bf16[272,128]{1,0:T(8,128)(2,1)S(1)}, u32[]{:S(2)}, u32[]{:S(2)}) collective-permute-start(bf16[272,128]{1,0:T(8,128)(2,1)S(1)} %get-tuple-element.42), channel_id=1, source_target_pairs={{8,0},{24,1},{10,2},{26,3},{12,4},{28,5},{14,6},{30,7},{0,8},{16,9... | collective-permute-start | bytes 208904 | tf_op jit(solution)/shard_map/ppermute | solution.py:373
  83.9 0.9 shard_map.88
  84.8 1.5 %collective-permute-done.8.g1_ref = bf16[272,128]{1,0:T(8,128)(2,1)S(1)} collective-permute-done((bf16[272,128]{1,0:T(8,128)(2,1)S(1)}, bf16[272,128]{1,0:T(8,128)(2,1)S(1)}, u32[]{:S(2)}, u32[]{:S(2)}) %collective-permute-start.8) | collective-permute-done | bytes 69664 | tf_op jit(solution)/shard_map/ppermute | solution.py:373
  86.3 1.0 shard_map.89.mine_ref
  87.3 6.8 %collective-permute-start.9 = (bf16[256,256]{1,0:T(8,128)(2,1)S(1)}, bf16[256,256]{1,0:T(8,128)(2,1)S(1)}, u32[]{:S(2)}, u32[]{:S(2)}) collective-permute-start(bf16[256,256]{1,0:T(8,128)(2,1)S(1)} %shard_map.89.mine_ref), channel_id=1, source_target_pairs={{0,1},{1,0},{2,3},{3,2},{4,5},{5,4},{6,7},{7,6},{8,9},{9,8},{10,11... | collective-permute-start | bytes 393224 | tf_op jit(solution)/shard_map/ppermute | solution.py:375
  94.0 1.0 collective-permute-done.9.theirs_ref
  95.0 1.0 shard_map.91
  96.0 12.7 %all_to_all.10.x_ref = bf16[4,256,256]{2,1,0:T(8,128)(2,1)S(1)} all-to-all(bf16[4,256,256]{2,1,0:T(8,128)(2,1)S(1)} %shard_map.91), channel_id=1, replica_groups={{0,2,4,6},{1,3,5,7},{8,10,12,14},{9,11,13,15},{16,18,20,22},{17,19,21,2..., dimensions={0} | all-to-all | bytes 1048576 | tf_op jit(solution)/shard_map/all_to_all | solution.py:379
  108.7 0.7 shard_map.92
  (17 shorter events, 0.1 us)
Async XLA Ops:
  17.0 4.6 %copy-start.4 = (bf16[256,256]{1,0:T(8,128)(2,1)S(1)}, bf16[256,256]{1,0:T(8,128)(2,1)}, u32[]{:S(2)}) copy-start(bf16[256,256]{1,0:T(8,128)(2,1)} %dirs_ref.1) | copy-start | bytes 393220
  17.0 4.6 %copy-start.5 = (f32[2,256]{1,0:T(2,128)S(1)}, f32[2,256]{1,0:T(2,128)}, u32[]{:S(2)}) copy-start(f32[2,256]{1,0:T(2,128)} %beta_ref.1) | copy-start | bytes 6148
  17.0 14.1 %all-to-all-start = ((bf16[4,256,256]{2,1,0:T(8,128)(2,1)}), bf16[4,256,256]{2,1,0:T(8,128)(2,1)S(1)}, u32[]{:S(2)}, u32[]{:S(2)}) async-start(bf16[4,256,256]{2,1,0:T(8,128)(2,1)} %shard_map.82), calls=%async_computation | async-start | bytes 1048576 | tf_op jit(solution)/shard_map/all_to_all | solution.py:343
  21.7 13.3 %copy-start.1 = (bf16[2048,256]{1,0:T(8,128)(2,1)S(1)}, bf16[2048,256]{1,0:T(8,128)(2,1)}, u32[]{:S(2)}) copy-start(bf16[2048,256]{1,0:T(8,128)(2,1)} %wq_ref.1) | copy-start | bytes 3145732
  21.7 13.3 %copy-start.2 = (bf16[2048,256]{1,0:T(8,128)(2,1)S(1)}, bf16[2048,256]{1,0:T(8,128)(2,1)}, u32[]{:S(2)}) copy-start(bf16[2048,256]{1,0:T(8,128)(2,1)} %wk_ref.1) | copy-start | bytes 3145732
  31.1 3.8 %collective-permute-start = (bf16[4,256,256]{2,1,0:T(8,128)(2,1)S(1)}, bf16[4,256,256]{2,1,0:T(8,128)(2,1)S(1)}, u32[]{:S(2)}, u32[]{:S(2)}) collective-permute-start(bf16[4,256,256]{2,1,0:T(8,128)(2,1)S(1)} %all-to-all-done.x_ref), channel_id=1, source_target_pairs={{0,1},{1,0},{2,3},{3,2},{4,5},{5,4},{6,7},{7,6},{8,9},{9,8},{10,11... | collective-permute-start | bytes 1572872 | tf_op jit(solution)/shard_map/ppermute | solution.py:345
  34.9 1.2 %copy-start.3 = (bf16[2048,256]{1,0:T(8,128)(2,1)S(1)}, bf16[2048,256]{1,0:T(8,128)(2,1)}, u32[]{:S(2)}) copy-start(bf16[2048,256]{1,0:T(8,128)(2,1)} %wv_ref.1) | copy-start | bytes 3145732
  36.2 30.4 %copy-start = (bf16[256,2048]{1,0:T(8,128)(2,1)S(1)}, bf16[256,2048]{1,0:T(8,128)(2,1)}, u32[]{:S(2)}) copy-start(bf16[256,2048]{1,0:T(8,128)(2,1)} %wo_ref.3) | copy-start | bytes 3145732
  38.4 4.1 %collective-permute-start.1 = (bf16[912,128]{1,0:T(8,128)(2,1)S(1)}, bf16[912,128]{1,0:T(8,128)(2,1)S(1)}, u32[]{:S(2)}, u32[]{:S(2)}) collective-permute-start(bf16[912,128]{1,0:T(8,128)(2,1)S(1)} %get-tuple-element.32), channel_id=1, source_target_pairs={{0,0},{1,16},{2,2},{3,18},{4,4},{5,20},{6,6},{7,22},{8,8},{9,24},{... | collective-permute-start | bytes 700424 | tf_op jit(solution)/shard_map/ppermute | solution.py:353
  39.0 10.1 %collective-permute-start.2 = (bf16[912,128]{1,0:T(8,128)(2,1)S(1)}, bf16[912,128]{1,0:T(8,128)(2,1)S(1)}, u32[]{:S(2)}, u32[]{:S(2)}) collective-permute-start(bf16[912,128]{1,0:T(8,128)(2,1)S(1)} %get-tuple-element.33), channel_id=1, source_target_pairs={{0,8},{1,24},{2,10},{3,26},{4,12},{5,28},{6,14},{7,30},{8,0},{9,16... | collective-permute-start | bytes 700424 | tf_op jit(solution)/shard_map/ppermute | solution.py:354
  49.9 11.0 %collective-permute-start.3 = (bf16[1152,128]{1,0:T(8,128)(2,1)S(1)}, bf16[1152,128]{1,0:T(8,128)(2,1)S(1)}, u32[]{:S(2)}, u32[]{:S(2)}) collective-permute-start(bf16[1152,128]{1,0:T(8,128)(2,1)S(1)} %get-tuple-element.35), channel_id=1, source_target_pairs={{0,32},{8,40},{16,48},{24,56},{32,64},{40,72},{48,80},{56,88},{64,... | collective-permute-start | bytes 884744 | tf_op jit(solution)/shard_map/ppermute | solution.py:364
  52.9 16.3 %collective-permute-start.6 = (bf16[1152,128]{1,0:T(8,128)(2,1)S(1)}, bf16[1152,128]{1,0:T(8,128)(2,1)S(1)}, u32[]{:S(2)}, u32[]{:S(2)}) collective-permute-start(bf16[1152,128]{1,0:T(8,128)(2,1)S(1)} %get-tuple-element.35), channel_id=1, source_target_pairs={{0,1},{1,32},{2,3},{3,34},{4,5},{5,36},{6,7},{7,38},{8,9},{9,40},{... | collective-permute-start | bytes 884744 | tf_op jit(solution)/shard_map/ppermute | solution.py:363
  61.0 10.2 %collective-permute-start.4 = (bf16[1152,128]{1,0:T(8,128)(2,1)S(1)}, bf16[1152,128]{1,0:T(8,128)(2,1)S(1)}, u32[]{:S(2)}, u32[]{:S(2)}) collective-permute-start(bf16[1152,128]{1,0:T(8,128)(2,1)S(1)} %collective-permute-done.3.d2_ref), channel_id=1, source_target_pairs={{0,1},{1,32},{2,3},{3,34},{4,5},{5,36},{6,7},{7,38},{8,9},{9,40},{... | collective-permute-start | bytes 884744 | tf_op jit(solution)/shard_map/ppermute | solution.py:365
  64.7 12.0 %collective-permute-start.5 = (bf16[1152,128]{1,0:T(8,128)(2,1)S(1)}, bf16[1152,128]{1,0:T(8,128)(2,1)S(1)}, u32[]{:S(2)}, u32[]{:S(2)}) collective-permute-start(bf16[1152,128]{1,0:T(8,128)(2,1)S(1)} %collective-permute-done.3.d2_ref), channel_id=1, source_target_pairs={{0,32},{8,40},{16,48},{24,56},{32,64},{40,72},{48,80},{56,88},{64,... | collective-permute-start | bytes 884744 | tf_op jit(solution)/shard_map/ppermute | solution.py:366
  67.2 26.8 %collective-permute-start.10 = (bf16[4,256,256]{2,1,0:T(8,128)(2,1)S(1)}, bf16[4,256,256]{2,1,0:T(8,128)(2,1)S(1)}, u32[]{:S(2)}, u32[]{:S(2)}) collective-permute-start(bf16[4,256,256]{2,1,0:T(8,128)(2,1)S(1)} %shard_map.90), channel_id=1, source_target_pairs={{0,1},{1,0},{2,3},{3,2},{4,5},{5,4},{6,7},{7,6},{8,9},{9,8},{10,11... | collective-permute-start | bytes 1572872 | tf_op jit(solution)/shard_map/ppermute | solution.py:347
  78.8 6.0 %collective-permute-start.7 = (bf16[272,128]{1,0:T(8,128)(2,1)S(1)}, bf16[272,128]{1,0:T(8,128)(2,1)S(1)}, u32[]{:S(2)}, u32[]{:S(2)}) collective-permute-start(bf16[272,128]{1,0:T(8,128)(2,1)S(1)} %get-tuple-element.41), channel_id=1, source_target_pairs={{0,0},{16,1},{2,2},{18,3},{4,4},{20,5},{6,6},{22,7},{8,8},{24,9},{... | collective-permute-start | bytes 208904 | tf_op jit(solution)/shard_map/ppermute | solution.py:372
  79.4 6.9 %collective-permute-start.8 = (bf16[272,128]{1,0:T(8,128)(2,1)S(1)}, bf16[272,128]{1,0:T(8,128)(2,1)S(1)}, u32[]{:S(2)}, u32[]{:S(2)}) collective-permute-start(bf16[272,128]{1,0:T(8,128)(2,1)S(1)} %get-tuple-element.42), channel_id=1, source_target_pairs={{8,0},{24,1},{10,2},{26,3},{12,4},{28,5},{14,6},{30,7},{0,8},{16,9... | collective-permute-start | bytes 208904 | tf_op jit(solution)/shard_map/ppermute | solution.py:373
  87.3 7.7 %collective-permute-start.9 = (bf16[256,256]{1,0:T(8,128)(2,1)S(1)}, bf16[256,256]{1,0:T(8,128)(2,1)S(1)}, u32[]{:S(2)}, u32[]{:S(2)}) collective-permute-start(bf16[256,256]{1,0:T(8,128)(2,1)S(1)} %shard_map.89.mine_ref), channel_id=1, source_target_pairs={{0,1},{1,0},{2,3},{3,2},{4,5},{5,4},{6,7},{7,6},{8,9},{9,8},{10,11... | collective-permute-start | bytes 393224 | tf_op jit(solution)/shard_map/ppermute | solution.py:375

commit v6 on v5

--- a/solution.py
+++ b/solution.py
@@ -37,12 +37,13 @@
     return dot(ah, bh) + (dot(ah, bl) + dot(al, bh))
 
 
-def call(body, outs, ins, flops=0, smem=0, late=0):
+def call(body, outs, ins, flops=0, smem=0, late=0, scratch=()):
     return pl.pallas_call(
         body,
         out_shape=outs,
         in_specs=[SMEM] * smem + [VMEM] * (ins - smem) + [pl.BlockSpec(memory_space=pl.ANY)] * late,
         out_specs=jax.tree.map(lambda _: VMEM, outs),
+        scratch_shapes=list(scratch),
         compiler_params=pltpu.CompilerParams(vmem_limit_bytes=48 * 2**20),
         cost_estimate=pl.CostEstimate(flops=flops, bytes_accessed=2**20, transcendentals=0),
     )
@@ -93,29 +94,16 @@
         t_ref[h] = t
 
 
-def copies_kernel(x_ref, out_ref, sems):
-    copies = [pltpu.make_async_copy(x_ref, out_ref.at[p], sems.at[p]) for p in range(4)]
-    for copy in copies:
-        copy.start()
-    for copy in copies:
-        copy.wait()
-
-
 def project_kernel(
     at_ref, hop_ref, x_ref, o_ref, wq_ref, wk_ref, wv_ref, w_ref, t_ref,
-    mark_ref, p0_ref, p1_ref, q_ref, k_ref, v_ref, c_ref,
+    mark_ref, p0_ref, p1_ref, q_ref, k_ref, v_ref, c_ref, rows_ref,
 ):
-    def product(weights):
-        total = None
-        for p in range(4):
-            for ref, c in ((x_ref, at_ref[1]), (o_ref, 1 - at_ref[1])):
-                rows = pl.ds(pl.multiple_of((2 * p + c) * 256, 256), 256)
-                term = dot(ref[p], weights[rows, :])
-                total = term if total is None else total + term
-        return total.astype(BF16)
-
     del mark_ref
-    query, key, value = product(wq_ref), product(wk_ref), product(wv_ref)
+    for p in range(4):
+        rows_ref[:, columns(at_ref[1], p)] = x_ref[p]
+        rows_ref[:, columns(1 - at_ref[1], p)] = o_ref[p]
+    rows = rows_ref[...]
+    query, key, value = (dot(rows, ref[...]).astype(BF16) for ref in (wq_ref, wk_ref, wv_ref))
     for h in range(2):
         cut = slice(h * DH, (h + 1) * DH)
         q_ref[h] = query[:, cut]
@@ -199,12 +187,12 @@
         q = dot(q, d1_ref[4 * TOK : PAIR]).astype(BF16)
         second = window_step(q, d2_ref, 2, i, hops, pair)
         next_ref[i] = dot(q, d2_ref[4 * TOK : PAIR]).astype(BF16)
-        top = jnp.maximum(jnp.max(first, axis=1, keepdims=True), jnp.max(second, axis=1, keepdims=True))
+        top = jnp.max(jnp.maximum(first, second), axis=1, keepdims=True)
         if i == 1:
             inside = dot(q_ref[0, 1], q_ref[2, 0], NT)
             top = jnp.maximum(top, jnp.max(inside, axis=1, keepdims=True))
         first, second = jnp.exp2(first - top), jnp.exp2(second - top)
-        total = jnp.sum(first, axis=1, keepdims=True) + jnp.sum(second, axis=1, keepdims=True)
+        total = jnp.sum(first + second, axis=1, keepdims=True)
         acc = dot(first.astype(BF16), d1_ref[2 * TOK : 4 * TOK])
         acc += dot(second.astype(BF16), d2_ref[2 * TOK : 4 * TOK])
         if i == 1:
@@ -228,12 +216,11 @@
         q = dot(q, d3_ref[4 * TOK : PAIR]).astype(BF16)
         fourth = window_step(q, d4_ref, 4, i, hops, pair)
         before = top_ref[i, :, 0:1]
-        top = jnp.maximum(jnp.max(third, axis=1, keepdims=True), jnp.max(fourth, axis=1, keepdims=True))
-        top = jnp.maximum(top, before)
+        top = jnp.maximum(jnp.max(jnp.maximum(third, fourth), axis=1, keepdims=True), before)
         third, fourth = jnp.exp2(third - top), jnp.exp2(fourth - top)
         kept = jnp.exp2(before - top)
         total = total_ref[i, :, 0:1] * kept
-        total += jnp.sum(third, axis=1, keepdims=True) + jnp.sum(fourth, axis=1, keepdims=True)
+        total += jnp.sum(third + fourth, axis=1, keepdims=True)
         acc = acc_ref[i] * kept
         acc += dot(third.astype(BF16), d3_ref[2 * TOK : 4 * TOK])
         acc += dot(fourth.astype(BF16), d4_ref[2 * TOK : 4 * TOK])
@@ -331,15 +318,7 @@
         directions_kernel, [shape((2, TOK, DH)), shape((2, TOK, TOK)), shape((8, DH), F32)], 2, flops=2**32
     )(reflect_dir, strength)
     planes = [[0, 2, 4, 6], [1, 3, 5, 7]]
-    copies = pl.pallas_call(
-        copies_kernel,
-        out_shape=shape((4, TOK, 256)),
-        in_specs=[pl.BlockSpec(memory_space=pl.ANY)],
-        out_specs=pl.BlockSpec(memory_space=pl.ANY),
-        scratch_shapes=[pltpu.SemaphoreType.DMA((4,))],
-        compiler_params=pltpu.CompilerParams(vmem_limit_bytes=62 * 2**20),
-        cost_estimate=pl.CostEstimate(flops=0, bytes_accessed=2**20, transcendentals=0),
-    )(inputs)
+    copies = jnp.broadcast_to(inputs[None], (4, TOK, 256))
     gathered = lax.all_to_all(copies, "head", 0, 0, axis_index_groups=planes)
     gathered, mark = lax.optimization_barrier((gathered, mark))
     other = lax.ppermute(gathered, "head", twin)
@@ -348,7 +327,7 @@
     p0, p1, q, k, v, coef = call(
         project_kernel,
         [shape((PACK, DH)), shape((PACK, DH))] + [shape((2, TOK, DH))] * 3 + [shape((2, TOK, TOK))],
-        9, smem=2, flops=2**30, late=1,
+        9, smem=2, flops=2**30, late=1, scratch=[pltpu.VMEM((TOK, 2048), BF16)],
     )(at, hop_count, gathered, other, w_query, w_key, w_value, w, t, mark)
     r0 = lax.ppermute(p0, both, there[0])
     r1 = lax.ppermute(p1, both, there[1])

time: 110 us -> 94.9 us (0.86)
  Pallas kernels: 30.9 us -> 14.2 us
  local copies, waits for them, and re-layouts: 1.25 us -> 2.99 us
    pallas_call x1 -> x0, Pallas kernels: 17 us -> none  [shards(): pl.pallas_call(copies_kernel, out_shape=shape((4, TOK, 256)), in_specs=[p...]
    broadcast_in_dim x0 -> x1, local copies, waits for them, and re-layouts: none -> 1.75 us  [shards(): copies = jnp.broadcast_to(inputs[None], (4, TOK, 256))]
  transfers between devices with their start and end apart: 12 -> 12, of which waited for: 7 -> 7; matrix products, arithmetic and copies ran while one was open for 0% -> 0% of each run, Pallas kernels for 8% -> 10%
where the time goes in v6:
time: 94.9 us; the launch traced here: 94.3 us
  starting transfers between devices  37.4 us (39%)
  waiting for transfers between devices  26.1 us (28%)
  Pallas kernels  14.2 us (15%)
  blocking collectives  12.7 us (13%)
  local copies, waits for them, and re-layouts  2.99 us (3%)
    all_to_all x1, blocking collectives, shards(): pieces = lax.all_to_all(partial, 'head', 0, 0, axis_index_groups=planes)  12.7 us
    all_to_all x1, waiting for transfers between devices, shards(): gathered = lax.all_to_all(copies, 'head', 0, 0, axis_index_groups=planes)  6.82 us
    ppermute x1, starting transfers between devices, shards(): theirs = lax.ppermute(mine, 'head', twin)  6.77 us
    ppermute x1, waiting for transfers between devices, shards(): r1 = lax.ppermute(p1, both, there[1])  6.69 us
    ppermute x1, waiting for transfers between devices, shards(): d4 = lax.ppermute(d2, 'ctx', down)  5.39 us
    all_to_all x1, starting transfers between devices, shards(): gathered = lax.all_to_all(copies, 'head', 0, 0, axis_index_groups=planes)  4.59 us
    ppermute x1, starting transfers between devices, shards(): d1 = lax.ppermute(own_pair, both, follow)  4.47 us
    ppermute x1, starting transfers between devices, shards(): g1 = lax.ppermute(o1, both, back[1])  4.41 us
  transfers between devices with their start and end apart: 12, of which 7 were waited for; matrix products, arithmetic and copies ran while one was open for 0% of the time, Pallas kernels for 10%

profile of v6, /device:TPU:384, one launch (start us, length us, event | category | flops | bytes accessed | tf_op | source)
XLA Modules:
  0.0 94.3 jit_solution(7540750121639655341)
XLA Ops:
  0.0 1.7 %broadcast_in_dim.2 = bf16[4,256,256]{2,1,0:T(8,128)(2,1)} broadcast(bf16[256,256]{1,0:T(8,128)(2,1)} %param.8), dimensions={1,2} | broadcast | bytes 655360 | tf_op jit(solution)/shard_map/broadcast_in_dim | solution.py:321
  1.8 4.6 %all-to-all-start = ((bf16[4,256,256]{2,1,0:T(8,128)(2,1)}), bf16[4,256,256]{2,1,0:T(8,128)(2,1)S(1)}, u32[]{:S(2)}, u32[]{:S(2)}) async-start(bf16[4,256,256]{2,1,0:T(8,128)(2,1)} %broadcast_in_dim.2), calls=%async_computation | async-start | bytes 1048576 | tf_op jit(solution)/shard_map/all_to_all | solution.py:322
  6.4 2.6 %shard_map.82 = (bf16[2,256,128]{2,1,0:T(8,128)(2,1)S(1)}, bf16[2,256,256]{2,1,0:T(8,128)(2,1)S(1)}, f32[8,128]{1,0:T(8,128)S(1)}) custom-call(bf16[256,256]{1,0:T(8,128)(2,1)S(1)} %copy-done.4, f32[2,256]{1,0:T(2,128)S(1)} %copy-done.5), custom_call_target="tpu_custom_call" | custom-call | flops 4294967296 | bytes 1048576 | tf_op jit(solution)/shard_map/pallas_call | solution.py:317
  9.0 6.8 %all-to-all-done.x_ref = bf16[4,256,256]{2,1,0:T(8,128)(2,1)S(1)} async-done(((bf16[4,256,256]{2,1,0:T(8,128)(2,1)}), bf16[4,256,256]{2,1,0:T(8,128)(2,1)S(1)}, u32[]{:S(2)}, u32[]{:S(2)}) %all-to-all-start) | async-done | bytes 524320 | tf_op jit(solution)/shard_map/all_to_all | solution.py:322
  15.8 1.9 %collective-permute-start = (bf16[4,256,256]{2,1,0:T(8,128)(2,1)S(1)}, bf16[4,256,256]{2,1,0:T(8,128)(2,1)S(1)}, u32[]{:S(2)}, u32[]{:S(2)}) collective-permute-start(bf16[4,256,256]{2,1,0:T(8,128)(2,1)S(1)} %all-to-all-done.x_ref), channel_id=1, source_target_pairs={{0,1},{1,0},{2,3},{3,2},{4,5},{5,4},{6,7},{7,6},{8,9},{9,8},{10,11... | collective-permute-start | bytes 1572872 | tf_op jit(solution)/shard_map/ppermute | solution.py:324
  18.5 1.1 %collective-permute-done.o_ref = bf16[4,256,256]{2,1,0:T(8,128)(2,1)S(1)} collective-permute-done((bf16[4,256,256]{2,1,0:T(8,128)(2,1)S(1)}, bf16[4,256,256]{2,1,0:T(8,128)(2,1)S(1)}, u32[]{:S(2)}, u32[]{:S(2)}) %collective-permute-start) | collective-permute-done | bytes 524320 | tf_op jit(solution)/shard_map/ppermute | solution.py:324
  19.6 1.2 %copy-done.3 = bf16[2048,256]{1,0:T(8,128)(2,1)S(1)} copy-done((bf16[2048,256]{1,0:T(8,128)(2,1)S(1)}, bf16[2048,256]{1,0:T(8,128)(2,1)}, u32[]{:S(2)}) %copy-start.3) | copy-done | bytes 1048600
  20.9 2.3 %shard_map.83 = (bf16[912,128]{1,0:T(8,128)(2,1)S(1)}, bf16[912,128]{1,0:T(8,128)(2,1)S(1)}, bf16[2,256,128]{2,1,0:T(8,128)(2,1)S(1)}, bf16[2,256,128]{2,1,0:T(8...) custom-call(s32[3]{0:T(128)S(1)} %pad_add_fusion.at_ref, s32[1]{0:T(128)S(6)} %copy.9.hop_ref, ...), custom_call_target="tpu_custom_call" | custom-call | flops 1073741824 | bytes 1048576 | tf_op jit(solution)/shard_map/pallas_call | solution.py:327
  23.2 0.7 collective-permute-start.1
  23.8 3.4 %collective-permute-start.2 = (bf16[912,128]{1,0:T(8,128)(2,1)S(1)}, bf16[912,128]{1,0:T(8,128)(2,1)S(1)}, u32[]{:S(2)}, u32[]{:S(2)}) collective-permute-start(bf16[912,128]{1,0:T(8,128)(2,1)S(1)} %get-tuple-element.33), channel_id=1, source_target_pairs={{0,8},{1,24},{2,10},{3,26},{4,12},{5,28},{6,14},{7,30},{8,0},{9,16... | collective-permute-start | bytes 700424 | tf_op jit(solution)/shard_map/ppermute | solution.py:333
  27.3 6.7 %collective-permute-done.2.r1_ref = bf16[912,128]{1,0:T(8,128)(2,1)S(1)} collective-permute-done((bf16[912,128]{1,0:T(8,128)(2,1)S(1)}, bf16[912,128]{1,0:T(8,128)(2,1)S(1)}, u32[]{:S(2)}, u32[]{:S(2)}) %collective-permute-start.2) | collective-permute-done | bytes 233504 | tf_op jit(solution)/shard_map/ppermute | solution.py:333
  34.0 0.8 shard_map.84
  34.7 2.9 %collective-permute-start.3 = (bf16[1152,128]{1,0:T(8,128)(2,1)S(1)}, bf16[1152,128]{1,0:T(8,128)(2,1)S(1)}, u32[]{:S(2)}, u32[]{:S(2)}) collective-permute-start(bf16[1152,128]{1,0:T(8,128)(2,1)S(1)} %get-tuple-element.35), channel_id=1, source_target_pairs={{0,32},{8,40},{16,48},{24,56},{32,64},{40,72},{48,80},{56,88},{64,... | collective-permute-start | bytes 884744 | tf_op jit(solution)/shard_map/ppermute | solution.py:343
  37.7 4.5 %collective-permute-start.6 = (bf16[1152,128]{1,0:T(8,128)(2,1)S(1)}, bf16[1152,128]{1,0:T(8,128)(2,1)S(1)}, u32[]{:S(2)}, u32[]{:S(2)}) collective-permute-start(bf16[1152,128]{1,0:T(8,128)(2,1)S(1)} %get-tuple-element.35), channel_id=1, source_target_pairs={{0,1},{1,32},{2,3},{3,34},{4,5},{5,36},{6,7},{7,38},{8,9},{9,40},{... | collective-permute-start | bytes 884744 | tf_op jit(solution)/shard_map/ppermute | solution.py:342
  42.2 3.6 %collective-permute-done.3.d2_ref = bf16[1152,128]{1,0:T(8,128)(2,1)S(1)} collective-permute-done((bf16[1152,128]{1,0:T(8,128)(2,1)S(1)}, bf16[1152,128]{1,0:T(8,128)(2,1)S(1)}, u32[]{:S(2)}, u32[]{:S(2)}) %collective-permute-start.3) | collective-permute-done | bytes 294944 | tf_op jit(solution)/shard_map/ppermute | solution.py:343
  45.8 3.7 %collective-permute-start.4 = (bf16[1152,128]{1,0:T(8,128)(2,1)S(1)}, bf16[1152,128]{1,0:T(8,128)(2,1)S(1)}, u32[]{:S(2)}, u32[]{:S(2)}) collective-permute-start(bf16[1152,128]{1,0:T(8,128)(2,1)S(1)} %collective-permute-done.3.d2_ref), channel_id=1, source_target_pairs={{0,1},{1,32},{2,3},{3,34},{4,5},{5,36},{6,7},{7,38},{8,9},{9,40},{... | collective-permute-start | bytes 884744 | tf_op jit(solution)/shard_map/ppermute | solution.py:344
  49.5 1.9 %collective-permute-start.5 = (bf16[1152,128]{1,0:T(8,128)(2,1)S(1)}, bf16[1152,128]{1,0:T(8,128)(2,1)S(1)}, u32[]{:S(2)}, u32[]{:S(2)}) collective-permute-start(bf16[1152,128]{1,0:T(8,128)(2,1)S(1)} %collective-permute-done.3.d2_ref), channel_id=1, source_target_pairs={{0,32},{8,40},{16,48},{24,56},{32,64},{40,72},{48,80},{56,88},{64,... | collective-permute-start | bytes 884744 | tf_op jit(solution)/shard_map/ppermute | solution.py:345
  51.4 0.6 shard_map.89
  52.0 1.9 %collective-permute-start.10 = (bf16[4,256,256]{2,1,0:T(8,128)(2,1)S(1)}, bf16[4,256,256]{2,1,0:T(8,128)(2,1)S(1)}, u32[]{:S(2)}, u32[]{:S(2)}) collective-permute-start(bf16[4,256,256]{2,1,0:T(8,128)(2,1)S(1)} %shard_map.89), channel_id=1, source_target_pairs={{0,1},{1,0},{2,3},{3,2},{4,5},{5,4},{6,7},{7,6},{8,9},{9,8},{10,11... | collective-permute-start | bytes 1572872 | tf_op jit(solution)/shard_map/ppermute | solution.py:326
  54.0 2.1 %shard_map.85 = (f32[2,256,128]{2,1,0:T(8,128)S(1)}, f32[2,256,128]{2,1,0:T(8,128)S(1)}, f32[2,256,128]{2,1,0:T(8,128)S(1)}, bf16[2,256,128]{2,1,0:T(8,128)(2,1)S(1)}) custom-call(s32[3]{0:T(128)S(1)} %pad_add_fusion.at_ref, bf16[3,2,256,128]{3,2,1,0:T(8,128)(2,1)S(1)} %get-tuple-element.36.q_ref, f32[2,16,128]{2,1,0:T(8,128)S(1)} %get-tuple-element.34.hop_ref, ...), custom_call_target="tpu_custom_call" | custom-call | flops 2147483648 | bytes 1048576 | tf_op jit(solution)/shard_map/pallas_call | solution.py:347
  56.1 5.4 %collective-permute-done.5.d4_ref = bf16[1152,128]{1,0:T(8,128)(2,1)S(1)} collective-permute-done((bf16[1152,128]{1,0:T(8,128)(2,1)S(1)}, bf16[1152,128]{1,0:T(8,128)(2,1)S(1)}, u32[]{:S(2)}, u32[]{:S(2)}) %collective-permute-start.5) | collective-permute-done | bytes 294944 | tf_op jit(solution)/shard_map/ppermute | solution.py:345
  61.5 2.2 %shard_map.86 = (bf16[272,128]{1,0:T(8,128)(2,1)S(1)}, bf16[272,128]{1,0:T(8,128)(2,1)S(1)}) custom-call(s32[3]{0:T(128)S(1)} %pad_add_fusion.at_ref, f32[2,16,128]{2,1,0:T(8,128)S(1)} %get-tuple-element.34.hop_ref, bf16[1152,128]{1,0:T(8,128)(2,1)S(1)} %collective-permute-done.4.d3_ref, bf16[1152,128]{1,0:T(8,128)(2,1)S(1)} %collective-permute-done.5.d4_ref, ...), custom_call_target="tpu_custom_call" | custom-call | flops 1073741824 | bytes 1048576 | tf_op jit(solution)/shard_map/pallas_call | solution.py:348
  63.7 0.7 collective-permute-start.7
  64.4 4.4 %collective-permute-start.8 = (bf16[272,128]{1,0:T(8,128)(2,1)S(1)}, bf16[272,128]{1,0:T(8,128)(2,1)S(1)}, u32[]{:S(2)}, u32[]{:S(2)}) collective-permute-start(bf16[272,128]{1,0:T(8,128)(2,1)S(1)} %get-tuple-element.42), channel_id=1, source_target_pairs={{8,0},{24,1},{10,2},{26,3},{12,4},{28,5},{14,6},{30,7},{0,8},{16,9... | collective-permute-start | bytes 208904 | tf_op jit(solution)/shard_map/ppermute | solution.py:352
  68.8 0.9 shard_map.87
  69.7 1.5 %collective-permute-done.8.g1_ref = bf16[272,128]{1,0:T(8,128)(2,1)S(1)} collective-permute-done((bf16[272,128]{1,0:T(8,128)(2,1)S(1)}, bf16[272,128]{1,0:T(8,128)(2,1)S(1)}, u32[]{:S(2)}, u32[]{:S(2)}) %collective-permute-start.8) | collective-permute-done | bytes 69664 | tf_op jit(solution)/shard_map/ppermute | solution.py:352
  71.2 1.0 %shard_map.88.mine_ref = bf16[256,256]{1,0:T(8,128)(2,1)S(1)} custom-call(s32[3]{0:T(128)S(1)} %pad_add_fusion.at_ref, bf16[272,128]{1,0:T(8,128)(2,1)S(1)} %collective-permute-done.7.g0_ref, bf16[272,128]{1,0:T(8,128)(2,1)S(1)} %collective-permute-done.8.g1_ref, f32[2,256,128]{2,1,0:T(8,128)S(1)} %get-tuple-element.47.acc_ref, ...), custom_call_target="tpu_custom_call" | custom-call | flops 268435456 | bytes 1048576 | tf_op jit(solution)/shard_map/pallas_call | solution.py:353
  72.2 6.8 %collective-permute-start.9 = (bf16[256,256]{1,0:T(8,128)(2,1)S(1)}, bf16[256,256]{1,0:T(8,128)(2,1)S(1)}, u32[]{:S(2)}, u32[]{:S(2)}) collective-permute-start(bf16[256,256]{1,0:T(8,128)(2,1)S(1)} %shard_map.88.mine_ref), channel_id=1, source_target_pairs={{0,1},{1,0},{2,3},{3,2},{4,5},{5,4},{6,7},{7,6},{8,9},{9,8},{10,11... | collective-permute-start | bytes 393224 | tf_op jit(solution)/shard_map/ppermute | solution.py:354
  79.0 1.0 %collective-permute-done.9.theirs_ref = bf16[256,256]{1,0:T(8,128)(2,1)S(1)} collective-permute-done((bf16[256,256]{1,0:T(8,128)(2,1)S(1)}, bf16[256,256]{1,0:T(8,128)(2,1)S(1)}, u32[]{:S(2)}, u32[]{:S(2)}) %collective-permute-start.9) | collective-permute-done | bytes 131104 | tf_op jit(solution)/shard_map/ppermute | solution.py:354
  79.9 1.0 %shard_map.90 = bf16[4,256,256]{2,1,0:T(8,128)(2,1)S(1)} custom-call(s32[3]{0:T(128)S(1)} %pad_add_fusion.at_ref, bf16[256,256]{1,0:T(8,128)(2,1)S(1)} %shard_map.88.mine_ref, bf16[256,256]{1,0:T(8,128)(2,1)S(1)} %collective-permute-done.9.theirs_ref, bf16[256,2048]{1,0:T(8,128)(2,1)S(1)} %copy-done, bf16[4,256,256]{2,1,0:T(8,128)(2,1)S(1)} %collective-permute-done.10.other_ref), custom_call_target="tpu_custom_call" | custom-call | flops 536870912 | bytes 1048576 | tf_op jit(solution)/shard_map/pallas_call | solution.py:355
  80.9 12.7 %all_to_all.10.x_ref = bf16[4,256,256]{2,1,0:T(8,128)(2,1)S(1)} all-to-all(bf16[4,256,256]{2,1,0:T(8,128)(2,1)S(1)} %shard_map.90), channel_id=1, replica_groups={{0,2,4,6},{1,3,5,7},{8,10,12,14},{9,11,13,15},{16,18,20,22},{17,19,21,2..., dimensions={0} | all-to-all | bytes 1048576 | tf_op jit(solution)/shard_map/all_to_all | solution.py:358
  93.6 0.7 shard_map.91
  (17 shorter events, 0.1 us)
Async XLA Ops:
  1.7 4.6 %copy-start.4 = (bf16[256,256]{1,0:T(8,128)(2,1)S(1)}, bf16[256,256]{1,0:T(8,128)(2,1)}, u32[]{:S(2)}) copy-start(bf16[256,256]{1,0:T(8,128)(2,1)} %dirs_ref.1) | copy-start | bytes 393220
  1.7 4.6 %copy-start.5 = (f32[2,256]{1,0:T(2,128)S(1)}, f32[2,256]{1,0:T(2,128)}, u32[]{:S(2)}) copy-start(f32[2,256]{1,0:T(2,128)} %beta_ref.1) | copy-start | bytes 6148
  1.8 14.1 %all-to-all-start = ((bf16[4,256,256]{2,1,0:T(8,128)(2,1)}), bf16[4,256,256]{2,1,0:T(8,128)(2,1)S(1)}, u32[]{:S(2)}, u32[]{:S(2)}) async-start(bf16[4,256,256]{2,1,0:T(8,128)(2,1)} %broadcast_in_dim.2), calls=%async_computation | async-start | bytes 1048576 | tf_op jit(solution)/shard_map/all_to_all | solution.py:322
  6.4 13.3 %copy-start.1 = (bf16[2048,256]{1,0:T(8,128)(2,1)S(1)}, bf16[2048,256]{1,0:T(8,128)(2,1)}, u32[]{:S(2)}) copy-start(bf16[2048,256]{1,0:T(8,128)(2,1)} %wq_ref.1) | copy-start | bytes 3145732
  6.4 13.3 %copy-start.2 = (bf16[2048,256]{1,0:T(8,128)(2,1)S(1)}, bf16[2048,256]{1,0:T(8,128)(2,1)}, u32[]{:S(2)}) copy-start(bf16[2048,256]{1,0:T(8,128)(2,1)} %wk_ref.1) | copy-start | bytes 3145732
  15.8 3.8 %collective-permute-start = (bf16[4,256,256]{2,1,0:T(8,128)(2,1)S(1)}, bf16[4,256,256]{2,1,0:T(8,128)(2,1)S(1)}, u32[]{:S(2)}, u32[]{:S(2)}) collective-permute-start(bf16[4,256,256]{2,1,0:T(8,128)(2,1)S(1)} %all-to-all-done.x_ref), channel_id=1, source_target_pairs={{0,1},{1,0},{2,3},{3,2},{4,5},{5,4},{6,7},{7,6},{8,9},{9,8},{10,11... | collective-permute-start | bytes 1572872 | tf_op jit(solution)/shard_map/ppermute | solution.py:324
  19.6 1.2 %copy-start.3 = (bf16[2048,256]{1,0:T(8,128)(2,1)S(1)}, bf16[2048,256]{1,0:T(8,128)(2,1)}, u32[]{:S(2)}) copy-start(bf16[2048,256]{1,0:T(8,128)(2,1)} %wv_ref.1) | copy-start | bytes 3145732
  20.8 30.5 %copy-start = (bf16[256,2048]{1,0:T(8,128)(2,1)S(1)}, bf16[256,2048]{1,0:T(8,128)(2,1)}, u32[]{:S(2)}) copy-start(bf16[256,2048]{1,0:T(8,128)(2,1)} %wo_ref.3) | copy-start | bytes 3145732
  23.2 4.1 %collective-permute-start.1 = (bf16[912,128]{1,0:T(8,128)(2,1)S(1)}, bf16[912,128]{1,0:T(8,128)(2,1)S(1)}, u32[]{:S(2)}, u32[]{:S(2)}) collective-permute-start(bf16[912,128]{1,0:T(8,128)(2,1)S(1)} %get-tuple-element.32), channel_id=1, source_target_pairs={{0,0},{1,16},{2,2},{3,18},{4,4},{5,20},{6,6},{7,22},{8,8},{9,24},{... | collective-permute-start | bytes 700424 | tf_op jit(solution)/shard_map/ppermute | solution.py:332
  23.8 10.1 %collective-permute-start.2 = (bf16[912,128]{1,0:T(8,128)(2,1)S(1)}, bf16[912,128]{1,0:T(8,128)(2,1)S(1)}, u32[]{:S(2)}, u32[]{:S(2)}) collective-permute-start(bf16[912,128]{1,0:T(8,128)(2,1)S(1)} %get-tuple-element.33), channel_id=1, source_target_pairs={{0,8},{1,24},{2,10},{3,26},{4,12},{5,28},{6,14},{7,30},{8,0},{9,16... | collective-permute-start | bytes 700424 | tf_op jit(solution)/shard_map/ppermute | solution.py:333
  34.7 11.0 %collective-permute-start.3 = (bf16[1152,128]{1,0:T(8,128)(2,1)S(1)}, bf16[1152,128]{1,0:T(8,128)(2,1)S(1)}, u32[]{:S(2)}, u32[]{:S(2)}) collective-permute-start(bf16[1152,128]{1,0:T(8,128)(2,1)S(1)} %get-tuple-element.35), channel_id=1, source_target_pairs={{0,32},{8,40},{16,48},{24,56},{32,64},{40,72},{48,80},{56,88},{64,... | collective-permute-start | bytes 884744 | tf_op jit(solution)/shard_map/ppermute | solution.py:343
  37.7 16.3 %collective-permute-start.6 = (bf16[1152,128]{1,0:T(8,128)(2,1)S(1)}, bf16[1152,128]{1,0:T(8,128)(2,1)S(1)}, u32[]{:S(2)}, u32[]{:S(2)}) collective-permute-start(bf16[1152,128]{1,0:T(8,128)(2,1)S(1)} %get-tuple-element.35), channel_id=1, source_target_pairs={{0,1},{1,32},{2,3},{3,34},{4,5},{5,36},{6,7},{7,38},{8,9},{9,40},{... | collective-permute-start | bytes 884744 | tf_op jit(solution)/shard_map/ppermute | solution.py:342
  45.8 10.3 %collective-permute-start.4 = (bf16[1152,128]{1,0:T(8,128)(2,1)S(1)}, bf16[1152,128]{1,0:T(8,128)(2,1)S(1)}, u32[]{:S(2)}, u32[]{:S(2)}) collective-permute-start(bf16[1152,128]{1,0:T(8,128)(2,1)S(1)} %collective-permute-done.3.d2_ref), channel_id=1, source_target_pairs={{0,1},{1,32},{2,3},{3,34},{4,5},{5,36},{6,7},{7,38},{8,9},{9,40},{... | collective-permute-start | bytes 884744 | tf_op jit(solution)/shard_map/ppermute | solution.py:344
  49.5 12.0 %collective-permute-start.5 = (bf16[1152,128]{1,0:T(8,128)(2,1)S(1)}, bf16[1152,128]{1,0:T(8,128)(2,1)S(1)}, u32[]{:S(2)}, u32[]{:S(2)}) collective-permute-start(bf16[1152,128]{1,0:T(8,128)(2,1)S(1)} %collective-permute-done.3.d2_ref), channel_id=1, source_target_pairs={{0,32},{8,40},{16,48},{24,56},{32,64},{40,72},{48,80},{56,88},{64,... | collective-permute-start | bytes 884744 | tf_op jit(solution)/shard_map/ppermute | solution.py:345
  52.0 27.0 %collective-permute-start.10 = (bf16[4,256,256]{2,1,0:T(8,128)(2,1)S(1)}, bf16[4,256,256]{2,1,0:T(8,128)(2,1)S(1)}, u32[]{:S(2)}, u32[]{:S(2)}) collective-permute-start(bf16[4,256,256]{2,1,0:T(8,128)(2,1)S(1)} %shard_map.89), channel_id=1, source_target_pairs={{0,1},{1,0},{2,3},{3,2},{4,5},{5,4},{6,7},{7,6},{8,9},{9,8},{10,11... | collective-permute-start | bytes 1572872 | tf_op jit(solution)/shard_map/ppermute | solution.py:326
  63.7 6.0 %collective-permute-start.7 = (bf16[272,128]{1,0:T(8,128)(2,1)S(1)}, bf16[272,128]{1,0:T(8,128)(2,1)S(1)}, u32[]{:S(2)}, u32[]{:S(2)}) collective-permute-start(bf16[272,128]{1,0:T(8,128)(2,1)S(1)} %get-tuple-element.41), channel_id=1, source_target_pairs={{0,0},{16,1},{2,2},{18,3},{4,4},{20,5},{6,6},{22,7},{8,8},{24,9},{... | collective-permute-start | bytes 208904 | tf_op jit(solution)/shard_map/ppermute | solution.py:351
  64.4 6.8 %collective-permute-start.8 = (bf16[272,128]{1,0:T(8,128)(2,1)S(1)}, bf16[272,128]{1,0:T(8,128)(2,1)S(1)}, u32[]{:S(2)}, u32[]{:S(2)}) collective-permute-start(bf16[272,128]{1,0:T(8,128)(2,1)S(1)} %get-tuple-element.42), channel_id=1, source_target_pairs={{8,0},{24,1},{10,2},{26,3},{12,4},{28,5},{14,6},{30,7},{0,8},{16,9... | collective-permute-start | bytes 208904 | tf_op jit(solution)/shard_map/ppermute | solution.py:352
  72.2 7.7 %collective-permute-start.9 = (bf16[256,256]{1,0:T(8,128)(2,1)S(1)}, bf16[256,256]{1,0:T(8,128)(2,1)S(1)}, u32[]{:S(2)}, u32[]{:S(2)}) collective-permute-start(bf16[256,256]{1,0:T(8,128)(2,1)S(1)} %shard_map.88.mine_ref), channel_id=1, source_target_pairs={{0,1},{1,0},{2,3},{3,2},{4,5},{5,4},{6,7},{7,6},{8,9},{9,8},{10,11... | collective-permute-start | bytes 393224 | tf_op jit(solution)/shard_map/ppermute | solution.py:354

commit v7 on v5

--- a/solution.py
+++ b/solution.py
@@ -37,12 +37,13 @@
     return dot(ah, bh) + (dot(ah, bl) + dot(al, bh))
 
 
-def call(body, outs, ins, flops=0, smem=0, late=0):
+def call(body, outs, ins, flops=0, smem=0, late=0, scratch=()):
     return pl.pallas_call(
         body,
         out_shape=outs,
         in_specs=[SMEM] * smem + [VMEM] * (ins - smem) + [pl.BlockSpec(memory_space=pl.ANY)] * late,
         out_specs=jax.tree.map(lambda _: VMEM, outs),
+        scratch_shapes=list(scratch),
         compiler_params=pltpu.CompilerParams(vmem_limit_bytes=48 * 2**20),
         cost_estimate=pl.CostEstimate(flops=flops, bytes_accessed=2**20, transcendentals=0),
     )
@@ -93,7 +94,7 @@
         t_ref[h] = t
 
 
-def copies_kernel(x_ref, out_ref, sems):
+def pieces_kernel(x_ref, out_ref, sems):
     copies = [pltpu.make_async_copy(x_ref, out_ref.at[p], sems.at[p]) for p in range(4)]
     for copy in copies:
         copy.start()
@@ -277,10 +278,14 @@
         out_ref[p] = wo_ref[:, columns(1 - at_ref[1], p)]
 
 
-def output_kernel(at_ref, mine_ref, theirs_ref, wo_ref, other_ref, out_ref):
+def mine_kernel(at_ref, mine_ref, wo_ref, out_ref):
     for p in range(4):
-        total = dot(mine_ref[...], wo_ref[:, columns(at_ref[1], p)])
-        out_ref[p] = (total + dot(theirs_ref[...], other_ref[p])).astype(BF16)
+        out_ref[p] = dot(mine_ref[...], wo_ref[:, columns(at_ref[1], p)])
+
+
+def output_kernel(part_ref, theirs_ref, other_ref, out_ref):
+    for p in range(4):
+        out_ref[p] = (part_ref[p] + dot(theirs_ref[...], other_ref[p])).astype(BF16)
 
 
 def sum_kernel(x_ref, out_ref):
@@ -332,10 +337,10 @@
     )(reflect_dir, strength)
     planes = [[0, 2, 4, 6], [1, 3, 5, 7]]
     copies = pl.pallas_call(
-        copies_kernel,
+        pieces_kernel,
         out_shape=shape((4, TOK, 256)),
-        in_specs=[pl.BlockSpec(memory_space=pl.ANY)],
-        out_specs=pl.BlockSpec(memory_space=pl.ANY),
+        in_specs=[VMEM],
+        out_specs=pl.BlockSpec(memory_space=pltpu.HBM),
         scratch_shapes=[pltpu.SemaphoreType.DMA((4,))],
         compiler_params=pltpu.CompilerParams(vmem_limit_bytes=62 * 2**20),
         cost_estimate=pl.CostEstimate(flops=0, bytes_accessed=2**20, transcendentals=0),
@@ -373,9 +378,8 @@
     g1 = lax.ppermute(o1, both, back[1])
     mine = call(merge_kernel, shape((TOK, 2 * DH)), 5, smem=1, flops=2**28)(at, g0, g1, acc, lse)
     theirs = lax.ppermute(mine, "head", twin)
-    partial = call(output_kernel, shape((4, TOK, 256)), 5, smem=1, flops=2**29)(
-        at, mine, theirs, w_out, other_out
-    )
+    part = call(mine_kernel, shape((4, TOK, 256), F32), 3, smem=1, flops=2**29)(at, mine, w_out)
+    partial = call(output_kernel, shape((4, TOK, 256)), 3, flops=2**28)(part, theirs, other_out)
     pieces = lax.all_to_all(partial, "head", 0, 0, axis_index_groups=planes)
     return call(sum_kernel, shape((TOK, 256)), 1)(pieces)
 

time: 110 us -> 94 us (0.85)
  Pallas kernels: 30.9 us -> 15.8 us
    pallas_call x2 -> x3, Pallas kernels: 18 us -> 2.9 us  [the longest x1 1.75 us: shards(): pl.pallas_call(pieces_kernel, out_shape=shape((4, TOK, 256)), in_specs=[V...]
  transfers between devices with their start and end apart: 12 -> 12, of which waited for: 7 -> 7; matrix products, arithmetic and copies ran while one was open for 0% -> 0% of each run, Pallas kernels for 8% -> 11%
where the time goes in v7:
time: 94 us; the launch traced here: 93.4 us
  starting transfers between devices  37.3 us (40%)
  waiting for transfers between devices  25.4 us (27%)
  Pallas kernels  15.8 us (17%)
  blocking collectives  12.7 us (14%)
  local copies, waits for them, and re-layouts  1.25 us (1%)
    all_to_all x1, blocking collectives, shards(): pieces = lax.all_to_all(partial, 'head', 0, 0, axis_index_groups=planes)  12.7 us
    all_to_all x1, waiting for transfers between devices, shards(): gathered = lax.all_to_all(copies, 'head', 0, 0, axis_index_groups=planes)  6.82 us
    ppermute x1, starting transfers between devices, shards(): theirs = lax.ppermute(mine, 'head', twin)  6.77 us
    ppermute x1, waiting for transfers between devices, shards(): r1 = lax.ppermute(p1, both, there[1])  6.69 us
    ppermute x1, waiting for transfers between devices, shards(): d4 = lax.ppermute(d2, 'ctx', down)  5.47 us
    all_to_all x1, starting transfers between devices, shards(): gathered = lax.all_to_all(copies, 'head', 0, 0, axis_index_groups=planes)  4.61 us
    ppermute x1, starting transfers between devices, shards(): d1 = lax.ppermute(own_pair, both, follow)  4.48 us
    ppermute x1, starting transfers between devices, shards(): g1 = lax.ppermute(o1, both, back[1])  4.4 us
  transfers between devices with their start and end apart: 12, of which 7 were waited for; matrix products, arithmetic and copies ran while one was open for 0% of the time, Pallas kernels for 11%

profile of v7, /device:TPU:384, one launch (start us, length us, event | category | flops | bytes accessed | tf_op | source)
XLA Modules:
  0.0 93.4 jit_solution(14954333626254174648)
XLA Ops:
  0.0 1.7 %shard_map.82 = bf16[4,256,256]{2,1,0:T(8,128)(2,1)} custom-call(bf16[256,256]{1,0:T(8,128)(2,1)} %x_ref.1), custom_call_target="tpu_custom_call" | custom-call | bytes 1048576 | tf_op jit(solution)/shard_map/pallas_call | solution.py:339
  1.8 4.6 %all-to-all-start = ((bf16[4,256,256]{2,1,0:T(8,128)(2,1)}), bf16[4,256,256]{2,1,0:T(8,128)(2,1)S(1)}, u32[]{:S(2)}, u32[]{:S(2)}) async-start(bf16[4,256,256]{2,1,0:T(8,128)(2,1)} %shard_map.82), calls=%async_computation | async-start | bytes 1048576 | tf_op jit(solution)/shard_map/all_to_all | solution.py:348
  6.4 2.6 %shard_map.83 = (bf16[2,256,128]{2,1,0:T(8,128)(2,1)S(1)}, bf16[2,256,256]{2,1,0:T(8,128)(2,1)S(1)}, f32[8,128]{1,0:T(8,128)S(1)}) custom-call(bf16[256,256]{1,0:T(8,128)(2,1)S(1)} %copy-done.4, f32[2,256]{1,0:T(2,128)S(1)} %copy-done.5), custom_call_target="tpu_custom_call" | custom-call | flops 4294967296 | bytes 1048576 | tf_op jit(solution)/shard_map/pallas_call | solution.py:335
  9.0 6.8 %all-to-all-done.x_ref = bf16[4,256,256]{2,1,0:T(8,128)(2,1)S(1)} async-done(((bf16[4,256,256]{2,1,0:T(8,128)(2,1)}), bf16[4,256,256]{2,1,0:T(8,128)(2,1)S(1)}, u32[]{:S(2)}, u32[]{:S(2)}) %all-to-all-start) | async-done | bytes 524320 | tf_op jit(solution)/shard_map/all_to_all | solution.py:348
  15.9 1.9 %collective-permute-start = (bf16[4,256,256]{2,1,0:T(8,128)(2,1)S(1)}, bf16[4,256,256]{2,1,0:T(8,128)(2,1)S(1)}, u32[]{:S(2)}, u32[]{:S(2)}) collective-permute-start(bf16[4,256,256]{2,1,0:T(8,128)(2,1)S(1)} %all-to-all-done.x_ref), channel_id=1, source_target_pairs={{0,1},{1,0},{2,3},{3,2},{4,5},{5,4},{6,7},{7,6},{8,9},{9,8},{10,11... | collective-permute-start | bytes 1572872 | tf_op jit(solution)/shard_map/ppermute | solution.py:350
  18.5 1.1 %collective-permute-done.o_ref = bf16[4,256,256]{2,1,0:T(8,128)(2,1)S(1)} collective-permute-done((bf16[4,256,256]{2,1,0:T(8,128)(2,1)S(1)}, bf16[4,256,256]{2,1,0:T(8,128)(2,1)S(1)}, u32[]{:S(2)}, u32[]{:S(2)}) %collective-permute-start) | collective-permute-done | bytes 524320 | tf_op jit(solution)/shard_map/ppermute | solution.py:350
  19.7 1.2 %copy-done.3 = bf16[2048,256]{1,0:T(8,128)(2,1)S(1)} copy-done((bf16[2048,256]{1,0:T(8,128)(2,1)S(1)}, bf16[2048,256]{1,0:T(8,128)(2,1)}, u32[]{:S(2)}) %copy-start.3) | copy-done | bytes 1048600
  20.9 2.2 %shard_map.84 = (bf16[912,128]{1,0:T(8,128)(2,1)S(1)}, bf16[912,128]{1,0:T(8,128)(2,1)S(1)}, bf16[2,256,128]{2,1,0:T(8,128)(2,1)S(1)}, bf16[2,256,128]{2,1,0:T(8...) custom-call(s32[3]{0:T(128)S(1)} %pad_add_fusion.at_ref, s32[1]{0:T(128)S(6)} %copy.9.hop_ref, ...), custom_call_target="tpu_custom_call" | custom-call | flops 1073741824 | bytes 1048576 | tf_op jit(solution)/shard_map/pallas_call | solution.py:353
  23.1 0.7 collective-permute-start.1
  23.8 3.4 %collective-permute-start.2 = (bf16[912,128]{1,0:T(8,128)(2,1)S(1)}, bf16[912,128]{1,0:T(8,128)(2,1)S(1)}, u32[]{:S(2)}, u32[]{:S(2)}) collective-permute-start(bf16[912,128]{1,0:T(8,128)(2,1)S(1)} %get-tuple-element.33), channel_id=1, source_target_pairs={{0,8},{1,24},{2,10},{3,26},{4,12},{5,28},{6,14},{7,30},{8,0},{9,16... | collective-permute-start | bytes 700424 | tf_op jit(solution)/shard_map/ppermute | solution.py:359
  27.2 6.7 %collective-permute-done.2.r1_ref = bf16[912,128]{1,0:T(8,128)(2,1)S(1)} collective-permute-done((bf16[912,128]{1,0:T(8,128)(2,1)S(1)}, bf16[912,128]{1,0:T(8,128)(2,1)S(1)}, u32[]{:S(2)}, u32[]{:S(2)}) %collective-permute-start.2) | collective-permute-done | bytes 233504 | tf_op jit(solution)/shard_map/ppermute | solution.py:359
  33.9 0.8 shard_map.85
  34.7 2.9 %collective-permute-start.3 = (bf16[1152,128]{1,0:T(8,128)(2,1)S(1)}, bf16[1152,128]{1,0:T(8,128)(2,1)S(1)}, u32[]{:S(2)}, u32[]{:S(2)}) collective-permute-start(bf16[1152,128]{1,0:T(8,128)(2,1)S(1)} %get-tuple-element.35), channel_id=1, source_target_pairs={{0,32},{8,40},{16,48},{24,56},{32,64},{40,72},{48,80},{56,88},{64,... | collective-permute-start | bytes 884744 | tf_op jit(solution)/shard_map/ppermute | solution.py:369
  37.6 4.5 %collective-permute-start.6 = (bf16[1152,128]{1,0:T(8,128)(2,1)S(1)}, bf16[1152,128]{1,0:T(8,128)(2,1)S(1)}, u32[]{:S(2)}, u32[]{:S(2)}) collective-permute-start(bf16[1152,128]{1,0:T(8,128)(2,1)S(1)} %get-tuple-element.35), channel_id=1, source_target_pairs={{0,1},{1,32},{2,3},{3,34},{4,5},{5,36},{6,7},{7,38},{8,9},{9,40},{... | collective-permute-start | bytes 884744 | tf_op jit(solution)/shard_map/ppermute | solution.py:368
  42.1 3.6 %collective-permute-done.3.d2_ref = bf16[1152,128]{1,0:T(8,128)(2,1)S(1)} collective-permute-done((bf16[1152,128]{1,0:T(8,128)(2,1)S(1)}, bf16[1152,128]{1,0:T(8,128)(2,1)S(1)}, u32[]{:S(2)}, u32[]{:S(2)}) %collective-permute-start.3) | collective-permute-done | bytes 294944 | tf_op jit(solution)/shard_map/ppermute | solution.py:369
  45.7 3.7 %collective-permute-start.4 = (bf16[1152,128]{1,0:T(8,128)(2,1)S(1)}, bf16[1152,128]{1,0:T(8,128)(2,1)S(1)}, u32[]{:S(2)}, u32[]{:S(2)}) collective-permute-start(bf16[1152,128]{1,0:T(8,128)(2,1)S(1)} %collective-permute-done.3.d2_ref), channel_id=1, source_target_pairs={{0,1},{1,32},{2,3},{3,34},{4,5},{5,36},{6,7},{7,38},{8,9},{9,40},{... | collective-permute-start | bytes 884744 | tf_op jit(solution)/shard_map/ppermute | solution.py:370
  49.4 1.9 %collective-permute-start.5 = (bf16[1152,128]{1,0:T(8,128)(2,1)S(1)}, bf16[1152,128]{1,0:T(8,128)(2,1)S(1)}, u32[]{:S(2)}, u32[]{:S(2)}) collective-permute-start(bf16[1152,128]{1,0:T(8,128)(2,1)S(1)} %collective-permute-done.3.d2_ref), channel_id=1, source_target_pairs={{0,32},{8,40},{16,48},{24,56},{32,64},{40,72},{48,80},{56,88},{64,... | collective-permute-start | bytes 884744 | tf_op jit(solution)/shard_map/ppermute | solution.py:371
  51.3 0.6 shard_map.91
  52.0 1.9 %collective-permute-start.10 = (bf16[4,256,256]{2,1,0:T(8,128)(2,1)S(1)}, bf16[4,256,256]{2,1,0:T(8,128)(2,1)S(1)}, u32[]{:S(2)}, u32[]{:S(2)}) collective-permute-start(bf16[4,256,256]{2,1,0:T(8,128)(2,1)S(1)} %shard_map.91), channel_id=1, source_target_pairs={{0,1},{1,0},{2,3},{3,2},{4,5},{5,4},{6,7},{7,6},{8,9},{9,8},{10,11... | collective-permute-start | bytes 1572872 | tf_op jit(solution)/shard_map/ppermute | solution.py:352
  53.9 2.0 %shard_map.86 = (f32[2,256,128]{2,1,0:T(8,128)S(1)}, f32[2,256,128]{2,1,0:T(8,128)S(1)}, f32[2,256,128]{2,1,0:T(8,128)S(1)}, bf16[2,256,128]{2,1,0:T(8,128)(2,1)S(1)}) custom-call(s32[3]{0:T(128)S(1)} %pad_add_fusion.at_ref, bf16[3,2,256,128]{3,2,1,0:T(8,128)(2,1)S(1)} %get-tuple-element.36.q_ref, f32[2,16,128]{2,1,0:T(8,128)S(1)} %get-tuple-element.34.hop_ref, ...), custom_call_target="tpu_custom_call" | custom-call | flops 2147483648 | bytes 1048576 | tf_op jit(solution)/shard_map/pallas_call | solution.py:373
  56.0 5.5 %collective-permute-done.5.d4_ref = bf16[1152,128]{1,0:T(8,128)(2,1)S(1)} collective-permute-done((bf16[1152,128]{1,0:T(8,128)(2,1)S(1)}, bf16[1152,128]{1,0:T(8,128)(2,1)S(1)}, u32[]{:S(2)}, u32[]{:S(2)}) %collective-permute-start.5) | collective-permute-done | bytes 294944 | tf_op jit(solution)/shard_map/ppermute | solution.py:371
  61.4 2.1 %shard_map.87 = (bf16[272,128]{1,0:T(8,128)(2,1)S(1)}, bf16[272,128]{1,0:T(8,128)(2,1)S(1)}) custom-call(s32[3]{0:T(128)S(1)} %pad_add_fusion.at_ref, f32[2,16,128]{2,1,0:T(8,128)S(1)} %get-tuple-element.34.hop_ref, bf16[1152,128]{1,0:T(8,128)(2,1)S(1)} %collective-permute-done.4.d3_ref, bf16[1152,128]{1,0:T(8,128)(2,1)S(1)} %collective-permute-done.5.d4_ref, ...), custom_call_target="tpu_custom_call" | custom-call | flops 1073741824 | bytes 1048576 | tf_op jit(solution)/shard_map/pallas_call | solution.py:374
  63.5 0.7 collective-permute-start.7
  64.2 4.4 %collective-permute-start.8 = (bf16[272,128]{1,0:T(8,128)(2,1)S(1)}, bf16[272,128]{1,0:T(8,128)(2,1)S(1)}, u32[]{:S(2)}, u32[]{:S(2)}) collective-permute-start(bf16[272,128]{1,0:T(8,128)(2,1)S(1)} %get-tuple-element.42), channel_id=1, source_target_pairs={{8,0},{24,1},{10,2},{26,3},{12,4},{28,5},{14,6},{30,7},{0,8},{16,9... | collective-permute-start | bytes 208904 | tf_op jit(solution)/shard_map/ppermute | solution.py:378
  68.6 0.9 shard_map.88
  69.5 1.5 %collective-permute-done.8.g1_ref = bf16[272,128]{1,0:T(8,128)(2,1)S(1)} collective-permute-done((bf16[272,128]{1,0:T(8,128)(2,1)S(1)}, bf16[272,128]{1,0:T(8,128)(2,1)S(1)}, u32[]{:S(2)}, u32[]{:S(2)}) %collective-permute-start.8) | collective-permute-done | bytes 69664 | tf_op jit(solution)/shard_map/ppermute | solution.py:378
  71.0 1.0 %shard_map.89.mine_ref = bf16[256,256]{1,0:T(8,128)(2,1)S(1)} custom-call(s32[3]{0:T(128)S(1)} %pad_add_fusion.at_ref, bf16[272,128]{1,0:T(8,128)(2,1)S(1)} %collective-permute-done.7.g0_ref, bf16[272,128]{1,0:T(8,128)(2,1)S(1)} %collective-permute-done.8.g1_ref, f32[2,256,128]{2,1,0:T(8,128)S(1)} %get-tuple-element.47.acc_ref, ...), custom_call_target="tpu_custom_call" | custom-call | flops 268435456 | bytes 1048576 | tf_op jit(solution)/shard_map/pallas_call | solution.py:379
  72.0 6.8 %collective-permute-start.9 = (bf16[256,256]{1,0:T(8,128)(2,1)S(1)}, bf16[256,256]{1,0:T(8,128)(2,1)S(1)}, u32[]{:S(2)}, u32[]{:S(2)}) collective-permute-start(bf16[256,256]{1,0:T(8,128)(2,1)S(1)} %shard_map.89.mine_ref), channel_id=1, source_target_pairs={{0,1},{1,0},{2,3},{3,2},{4,5},{5,4},{6,7},{7,6},{8,9},{9,8},{10,11... | collective-permute-start | bytes 393224 | tf_op jit(solution)/shard_map/ppermute | solution.py:380
  78.8 0.9 shard_map.90.part_ref
  79.7 0.3 shard_map.92
  80.0 12.7 %all_to_all.10.x_ref = bf16[4,256,256]{2,1,0:T(8,128)(2,1)S(1)} all-to-all(bf16[4,256,256]{2,1,0:T(8,128)(2,1)S(1)} %shard_map.92), channel_id=1, replica_groups={{0,2,4,6},{1,3,5,7},{8,10,12,14},{9,11,13,15},{16,18,20,22},{17,19,21,2..., dimensions={0} | all-to-all | bytes 1048576 | tf_op jit(solution)/shard_map/all_to_all | solution.py:383
  92.7 0.7 shard_map.93
  (18 shorter events, 0.2 us)
Async XLA Ops:
  1.8 4.6 %copy-start.4 = (bf16[256,256]{1,0:T(8,128)(2,1)S(1)}, bf16[256,256]{1,0:T(8,128)(2,1)}, u32[]{:S(2)}) copy-start(bf16[256,256]{1,0:T(8,128)(2,1)} %dirs_ref.1) | copy-start | bytes 393220
  1.8 4.6 %copy-start.5 = (f32[2,256]{1,0:T(2,128)S(1)}, f32[2,256]{1,0:T(2,128)}, u32[]{:S(2)}) copy-start(f32[2,256]{1,0:T(2,128)} %beta_ref.1) | copy-start | bytes 6148
  1.8 14.1 %all-to-all-start = ((bf16[4,256,256]{2,1,0:T(8,128)(2,1)}), bf16[4,256,256]{2,1,0:T(8,128)(2,1)S(1)}, u32[]{:S(2)}, u32[]{:S(2)}) async-start(bf16[4,256,256]{2,1,0:T(8,128)(2,1)} %shard_map.82), calls=%async_computation | async-start | bytes 1048576 | tf_op jit(solution)/shard_map/all_to_all | solution.py:348
  6.4 13.3 %copy-start.1 = (bf16[2048,256]{1,0:T(8,128)(2,1)S(1)}, bf16[2048,256]{1,0:T(8,128)(2,1)}, u32[]{:S(2)}) copy-start(bf16[2048,256]{1,0:T(8,128)(2,1)} %wq_ref.1) | copy-start | bytes 3145732
  6.4 13.3 %copy-start.2 = (bf16[2048,256]{1,0:T(8,128)(2,1)S(1)}, bf16[2048,256]{1,0:T(8,128)(2,1)}, u32[]{:S(2)}) copy-start(bf16[2048,256]{1,0:T(8,128)(2,1)} %wk_ref.1) | copy-start | bytes 3145732
  15.9 3.8 %collective-permute-start = (bf16[4,256,256]{2,1,0:T(8,128)(2,1)S(1)}, bf16[4,256,256]{2,1,0:T(8,128)(2,1)S(1)}, u32[]{:S(2)}, u32[]{:S(2)}) collective-permute-start(bf16[4,256,256]{2,1,0:T(8,128)(2,1)S(1)} %all-to-all-done.x_ref), channel_id=1, source_target_pairs={{0,1},{1,0},{2,3},{3,2},{4,5},{5,4},{6,7},{7,6},{8,9},{9,8},{10,11... | collective-permute-start | bytes 1572872 | tf_op jit(solution)/shard_map/ppermute | solution.py:350
  19.7 1.2 %copy-start.3 = (bf16[2048,256]{1,0:T(8,128)(2,1)S(1)}, bf16[2048,256]{1,0:T(8,128)(2,1)}, u32[]{:S(2)}) copy-start(bf16[2048,256]{1,0:T(8,128)(2,1)} %wv_ref.1) | copy-start | bytes 3145732
  20.9 30.4 %copy-start = (bf16[256,2048]{1,0:T(8,128)(2,1)S(1)}, bf16[256,2048]{1,0:T(8,128)(2,1)}, u32[]{:S(2)}) copy-start(bf16[256,2048]{1,0:T(8,128)(2,1)} %wo_ref.3) | copy-start | bytes 3145732
  23.1 4.1 %collective-permute-start.1 = (bf16[912,128]{1,0:T(8,128)(2,1)S(1)}, bf16[912,128]{1,0:T(8,128)(2,1)S(1)}, u32[]{:S(2)}, u32[]{:S(2)}) collective-permute-start(bf16[912,128]{1,0:T(8,128)(2,1)S(1)} %get-tuple-element.32), channel_id=1, source_target_pairs={{0,0},{1,16},{2,2},{3,18},{4,4},{5,20},{6,6},{7,22},{8,8},{9,24},{... | collective-permute-start | bytes 700424 | tf_op jit(solution)/shard_map/ppermute | solution.py:358
  23.8 10.1 %collective-permute-start.2 = (bf16[912,128]{1,0:T(8,128)(2,1)S(1)}, bf16[912,128]{1,0:T(8,128)(2,1)S(1)}, u32[]{:S(2)}, u32[]{:S(2)}) collective-permute-start(bf16[912,128]{1,0:T(8,128)(2,1)S(1)} %get-tuple-element.33), channel_id=1, source_target_pairs={{0,8},{1,24},{2,10},{3,26},{4,12},{5,28},{6,14},{7,30},{8,0},{9,16... | collective-permute-start | bytes 700424 | tf_op jit(solution)/shard_map/ppermute | solution.py:359
  34.7 11.0 %collective-permute-start.3 = (bf16[1152,128]{1,0:T(8,128)(2,1)S(1)}, bf16[1152,128]{1,0:T(8,128)(2,1)S(1)}, u32[]{:S(2)}, u32[]{:S(2)}) collective-permute-start(bf16[1152,128]{1,0:T(8,128)(2,1)S(1)} %get-tuple-element.35), channel_id=1, source_target_pairs={{0,32},{8,40},{16,48},{24,56},{32,64},{40,72},{48,80},{56,88},{64,... | collective-permute-start | bytes 884744 | tf_op jit(solution)/shard_map/ppermute | solution.py:369
  37.6 16.3 %collective-permute-start.6 = (bf16[1152,128]{1,0:T(8,128)(2,1)S(1)}, bf16[1152,128]{1,0:T(8,128)(2,1)S(1)}, u32[]{:S(2)}, u32[]{:S(2)}) collective-permute-start(bf16[1152,128]{1,0:T(8,128)(2,1)S(1)} %get-tuple-element.35), channel_id=1, source_target_pairs={{0,1},{1,32},{2,3},{3,34},{4,5},{5,36},{6,7},{7,38},{8,9},{9,40},{... | collective-permute-start | bytes 884744 | tf_op jit(solution)/shard_map/ppermute | solution.py:368
  45.7 10.2 %collective-permute-start.4 = (bf16[1152,128]{1,0:T(8,128)(2,1)S(1)}, bf16[1152,128]{1,0:T(8,128)(2,1)S(1)}, u32[]{:S(2)}, u32[]{:S(2)}) collective-permute-start(bf16[1152,128]{1,0:T(8,128)(2,1)S(1)} %collective-permute-done.3.d2_ref), channel_id=1, source_target_pairs={{0,1},{1,32},{2,3},{3,34},{4,5},{5,36},{6,7},{7,38},{8,9},{9,40},{... | collective-permute-start | bytes 884744 | tf_op jit(solution)/shard_map/ppermute | solution.py:370
  49.4 12.0 %collective-permute-start.5 = (bf16[1152,128]{1,0:T(8,128)(2,1)S(1)}, bf16[1152,128]{1,0:T(8,128)(2,1)S(1)}, u32[]{:S(2)}, u32[]{:S(2)}) collective-permute-start(bf16[1152,128]{1,0:T(8,128)(2,1)S(1)} %collective-permute-done.3.d2_ref), channel_id=1, source_target_pairs={{0,32},{8,40},{16,48},{24,56},{32,64},{40,72},{48,80},{56,88},{64,... | collective-permute-start | bytes 884744 | tf_op jit(solution)/shard_map/ppermute | solution.py:371
  52.0 27.7 %collective-permute-start.10 = (bf16[4,256,256]{2,1,0:T(8,128)(2,1)S(1)}, bf16[4,256,256]{2,1,0:T(8,128)(2,1)S(1)}, u32[]{:S(2)}, u32[]{:S(2)}) collective-permute-start(bf16[4,256,256]{2,1,0:T(8,128)(2,1)S(1)} %shard_map.91), channel_id=1, source_target_pairs={{0,1},{1,0},{2,3},{3,2},{4,5},{5,4},{6,7},{7,6},{8,9},{9,8},{10,11... | collective-permute-start | bytes 1572872 | tf_op jit(solution)/shard_map/ppermute | solution.py:352
  63.5 6.0 %collective-permute-start.7 = (bf16[272,128]{1,0:T(8,128)(2,1)S(1)}, bf16[272,128]{1,0:T(8,128)(2,1)S(1)}, u32[]{:S(2)}, u32[]{:S(2)}) collective-permute-start(bf16[272,128]{1,0:T(8,128)(2,1)S(1)} %get-tuple-element.41), channel_id=1, source_target_pairs={{0,0},{16,1},{2,2},{18,3},{4,4},{20,5},{6,6},{22,7},{8,8},{24,9},{... | collective-permute-start | bytes 208904 | tf_op jit(solution)/shard_map/ppermute | solution.py:377
  64.2 6.8 %collective-permute-start.8 = (bf16[272,128]{1,0:T(8,128)(2,1)S(1)}, bf16[272,128]{1,0:T(8,128)(2,1)S(1)}, u32[]{:S(2)}, u32[]{:S(2)}) collective-permute-start(bf16[272,128]{1,0:T(8,128)(2,1)S(1)} %get-tuple-element.42), channel_id=1, source_target_pairs={{8,0},{24,1},{10,2},{26,3},{12,4},{28,5},{14,6},{30,7},{0,8},{16,9... | collective-permute-start | bytes 208904 | tf_op jit(solution)/shard_map/ppermute | solution.py:378
  72.0 7.7 %collective-permute-start.9 = (bf16[256,256]{1,0:T(8,128)(2,1)S(1)}, bf16[256,256]{1,0:T(8,128)(2,1)S(1)}, u32[]{:S(2)}, u32[]{:S(2)}) collective-permute-start(bf16[256,256]{1,0:T(8,128)(2,1)S(1)} %shard_map.89.mine_ref), channel_id=1, source_target_pairs={{0,1},{1,0},{2,3},{3,2},{4,5},{5,4},{6,7},{7,6},{8,9},{9,8},{10,11... | collective-permute-start | bytes 393224 | tf_op jit(solution)/shard_map/ppermute | solution.py:380

commit v8 on v7

--- a/solution.py
+++ b/solution.py
@@ -217,27 +217,34 @@
         total_ref[i] = jnp.broadcast_to(total, (TOK, DH))
 
 
-def far_kernel(
-    at_ref, hop_ref, d3_ref, d4_ref, acc_ref, top_ref, total_ref, next_ref, o0_ref, o1_ref
+def grown(q, keys, d, i, hops, pair, acc_ref, top_ref, total_ref):
+    scores = window_step(q, keys, d, i, hops, pair)
+    before = top_ref[i, :, 0:1]
+    top = jnp.maximum(jnp.max(scores, axis=1, keepdims=True), before)
+    prob = jnp.exp2(scores - top)
+    kept = jnp.exp2(before - top)
+    total = total_ref[i, :, 0:1] * kept + jnp.sum(prob, axis=1, keepdims=True)
+    acc = acc_ref[i] * kept + dot(prob.astype(BF16), keys[2 * TOK : 4 * TOK])
+    return acc, top, total
+
+
+def middle_kernel(
+    at_ref, hop_ref, d3_ref, acc_ref, top_ref, total_ref, q_ref, acc_out, top_out, total_out, next_ref
 ):
-    pair = at_ref[2]
+    for i in range(2):
+        q, hops = q_ref[i], hop_ref[i, 0:1, 0:1]
+        acc, top, total = grown(q, d3_ref, 3, i, hops, at_ref[2], acc_ref, top_ref, total_ref)
+        acc_out[i] = acc
+        top_out[i] = jnp.broadcast_to(top, (TOK, DH))
+        total_out[i] = jnp.broadcast_to(total, (TOK, DH))
+        next_ref[i] = dot(q, d3_ref[4 * TOK : PAIR]).astype(BF16)
+
+
+def far_kernel(at_ref, hop_ref, d4_ref, acc_ref, top_ref, total_ref, q_ref, o0_ref, o1_ref):
     for j, out_ref in enumerate((o0_ref, o1_ref)):
         i = lax.rem(at_ref[0] + j, 2)
         hops = hop_ref[i, 0:1, 0:1]
-        q = next_ref[i]
-        third = window_step(q, d3_ref, 3, i, hops, pair)
-        q = dot(q, d3_ref[4 * TOK : PAIR]).astype(BF16)
-        fourth = window_step(q, d4_ref, 4, i, hops, pair)
-        before = top_ref[i, :, 0:1]
-        top = jnp.maximum(jnp.max(third, axis=1, keepdims=True), jnp.max(fourth, axis=1, keepdims=True))
-        top = jnp.maximum(top, before)
-        third, fourth = jnp.exp2(third - top), jnp.exp2(fourth - top)
-        kept = jnp.exp2(before - top)
-        total = total_ref[i, :, 0:1] * kept
-        total += jnp.sum(third, axis=1, keepdims=True) + jnp.sum(fourth, axis=1, keepdims=True)
-        acc = acc_ref[i] * kept
-        acc += dot(third.astype(BF16), d3_ref[2 * TOK : 4 * TOK])
-        acc += dot(fourth.astype(BF16), d4_ref[2 * TOK : 4 * TOK])
+        acc, top, total = grown(q_ref[i], d4_ref, 4, i, hops, at_ref[2], acc_ref, top_ref, total_ref)
         out_ref[0:TOK] = (acc / total).astype(BF16)
         lse = jnp.broadcast_to(top + jnp.log2(total), (TOK, DH)).T[0:16]
         high = lse.astype(BF16).astype(F32)
@@ -367,13 +374,15 @@
     )(at, r0, r1)
     d1 = lax.ppermute(own_pair, both, follow)
     d2 = lax.ppermute(own_pair, "ctx", down)
+    d2, other_out = lax.optimization_barrier((d2, other_out))
     d3 = lax.ppermute(d2, both, follow)
     d4 = lax.ppermute(d2, "ctx", down)
     state = [shape((2, TOK, DH), F32)] * 3 + [shape((2, TOK, DH))]
     near = call(near_kernel, state, 5, smem=1, flops=2**31)(at, qs, hops, d1, d2)
-    o0, o1 = call(
-        far_kernel, [shape((BACK, DH)), shape((BACK, DH))], 8, smem=1, flops=2**30
-    )(at, hops, d3, d4, *near)
+    middle = call(middle_kernel, state, 7, smem=1, flops=2**30)(at, hops, d3, *near)
+    o0, o1 = call(far_kernel, [shape((BACK, DH)), shape((BACK, DH))], 7, smem=1, flops=2**30)(
+        at, hops, d4, *middle
+    )
     g0 = lax.ppermute(o0, both, back[0])
     g1 = lax.ppermute(o1, both, back[1])
     mine = call(merge_kernel, shape((TOK, 2 * DH)), 5, smem=1, flops=2**28)(at, g0, g1, acc, lse)

time: 94 us -> 93.5 us (level)
  waiting for transfers between devices: 25.4 us -> 20.1 us
  starting transfers between devices: 37.3 us -> 41.1 us
  Pallas kernels: 15.8 us -> 16.8 us
    ppermute x1, waiting for transfers between devices: 6.69 us -> 0.38 us  [shards(): r1 = lax.ppermute(p1, both, there[1])]
    ppermute x1, starting transfers between devices: 1.92 us -> 5.67 us  [shards(): other_out = lax.ppermute(halves, 'head', twin)]
    ppermute x1, waiting for transfers between devices: 0.01 us -> 1.58 us  [shards(): d3 = lax.ppermute(d2, both, follow)]
    pallas_call x1 -> x2, Pallas kernels: 2.08 us -> 3.12 us  [the longest x1 1.6 us: shards(): call(far_kernel, [shape((BACK, DH)), shape((BACK, DH))], 7, smem=1, flops...]
  transfers between devices with their start and end apart: 12 -> 12, of which waited for: 7 -> 8; matrix products, arithmetic and copies ran while one was open for 0% -> 0% of each run, Pallas kernels for 11% -> 10%
where the time goes in v8:
time: 93.5 us; the launch traced here: 93 us
  starting transfers between devices  41.1 us (44%)
  waiting for transfers between devices  20.1 us (21%)
  Pallas kernels  16.8 us (18%)
  blocking collectives  12.7 us (14%)
  local copies, waits for them, and re-layouts  1.25 us (1%)
    all_to_all x1, blocking collectives, shards(): pieces = lax.all_to_all(partial, 'head', 0, 0, axis_index_groups=planes)  12.7 us
    all_to_all x1, waiting for transfers between devices, shards(): gathered = lax.all_to_all(copies, 'head', 0, 0, axis_index_groups=planes)  6.82 us
    ppermute x1, starting transfers between devices, shards(): theirs = lax.ppermute(mine, 'head', twin)  6.75 us
    ppermute x1, starting transfers between devices, shards(): other_out = lax.ppermute(halves, 'head', twin)  5.67 us
    ppermute x1, waiting for transfers between devices, shards(): d4 = lax.ppermute(d2, 'ctx', down)  4.94 us
    all_to_all x1, starting transfers between devices, shards(): gathered = lax.all_to_all(copies, 'head', 0, 0, axis_index_groups=planes)  4.61 us
    ppermute x1, starting transfers between devices, shards(): d1 = lax.ppermute(own_pair, both, follow)  4.48 us
    ppermute x1, starting transfers between devices, shards(): g1 = lax.ppermute(o1, both, back[1])  4.41 us
  transfers between devices with their start and end apart: 12, of which 8 were waited for; matrix products, arithmetic and copies ran while one was open for 0% of the time, Pallas kernels for 10%

profile of v8, /device:TPU:384, one launch (start us, length us, event | category | flops | bytes accessed | tf_op | source)
XLA Modules:
  0.0 93.0 jit_solution(5835199835133859203)
XLA Ops:
  0.0 1.7 %shard_map.82 = bf16[4,256,256]{2,1,0:T(8,128)(2,1)} custom-call(bf16[256,256]{1,0:T(8,128)(2,1)} %x_ref.1), custom_call_target="tpu_custom_call" | custom-call | bytes 1048576 | tf_op jit(solution)/shard_map/pallas_call | solution.py:346
  1.8 4.6 %all-to-all-start = ((bf16[4,256,256]{2,1,0:T(8,128)(2,1)}), bf16[4,256,256]{2,1,0:T(8,128)(2,1)S(1)}, u32[]{:S(2)}, u32[]{:S(2)}) async-start(bf16[4,256,256]{2,1,0:T(8,128)(2,1)} %shard_map.82), calls=%async_computation | async-start | bytes 1048576 | tf_op jit(solution)/shard_map/all_to_all | solution.py:355
  6.4 2.6 %shard_map.83 = (bf16[2,256,128]{2,1,0:T(8,128)(2,1)S(1)}, bf16[2,256,256]{2,1,0:T(8,128)(2,1)S(1)}, f32[8,128]{1,0:T(8,128)S(1)}) custom-call(bf16[256,256]{1,0:T(8,128)(2,1)S(1)} %copy-done.4, f32[2,256]{1,0:T(2,128)S(1)} %copy-done.5), custom_call_target="tpu_custom_call" | custom-call | flops 4294967296 | bytes 1048576 | tf_op jit(solution)/shard_map/pallas_call | solution.py:342
  9.0 6.8 %all-to-all-done.x_ref = bf16[4,256,256]{2,1,0:T(8,128)(2,1)S(1)} async-done(((bf16[4,256,256]{2,1,0:T(8,128)(2,1)}), bf16[4,256,256]{2,1,0:T(8,128)(2,1)S(1)}, u32[]{:S(2)}, u32[]{:S(2)}) %all-to-all-start) | async-done | bytes 524320 | tf_op jit(solution)/shard_map/all_to_all | solution.py:355
  15.9 1.9 %collective-permute-start = (bf16[4,256,256]{2,1,0:T(8,128)(2,1)S(1)}, bf16[4,256,256]{2,1,0:T(8,128)(2,1)S(1)}, u32[]{:S(2)}, u32[]{:S(2)}) collective-permute-start(bf16[4,256,256]{2,1,0:T(8,128)(2,1)S(1)} %all-to-all-done.x_ref), channel_id=1, source_target_pairs={{0,1},{1,0},{2,3},{3,2},{4,5},{5,4},{6,7},{7,6},{8,9},{9,8},{10,11... | collective-permute-start | bytes 1572872 | tf_op jit(solution)/shard_map/ppermute | solution.py:357
  18.5 1.1 %collective-permute-done.o_ref = bf16[4,256,256]{2,1,0:T(8,128)(2,1)S(1)} collective-permute-done((bf16[4,256,256]{2,1,0:T(8,128)(2,1)S(1)}, bf16[4,256,256]{2,1,0:T(8,128)(2,1)S(1)}, u32[]{:S(2)}, u32[]{:S(2)}) %collective-permute-start) | collective-permute-done | bytes 524320 | tf_op jit(solution)/shard_map/ppermute | solution.py:357
  19.7 1.2 %copy-done.3 = bf16[2048,256]{1,0:T(8,128)(2,1)S(1)} copy-done((bf16[2048,256]{1,0:T(8,128)(2,1)S(1)}, bf16[2048,256]{1,0:T(8,128)(2,1)}, u32[]{:S(2)}) %copy-start.3) | copy-done | bytes 1048600
  20.9 2.2 %shard_map.84 = (bf16[912,128]{1,0:T(8,128)(2,1)S(1)}, bf16[912,128]{1,0:T(8,128)(2,1)S(1)}, bf16[2,256,128]{2,1,0:T(8,128)(2,1)S(1)}, bf16[2,256,128]{2,1,0:T(8...) custom-call(s32[3]{0:T(128)S(1)} %pad_add_fusion.at_ref, s32[1]{0:T(128)S(6)} %copy.9.hop_ref, ...), custom_call_target="tpu_custom_call" | custom-call | flops 1073741824 | bytes 1048576 | tf_op jit(solution)/shard_map/pallas_call | solution.py:360
  23.1 0.7 collective-permute-start.1
  23.8 3.4 %collective-permute-start.2 = (bf16[912,128]{1,0:T(8,128)(2,1)S(1)}, bf16[912,128]{1,0:T(8,128)(2,1)S(1)}, u32[]{:S(2)}, u32[]{:S(2)}) collective-permute-start(bf16[912,128]{1,0:T(8,128)(2,1)S(1)} %get-tuple-element.39), channel_id=1, source_target_pairs={{0,8},{1,24},{2,10},{3,26},{4,12},{5,28},{6,14},{7,30},{8,0},{9,16... | collective-permute-start | bytes 700424 | tf_op jit(solution)/shard_map/ppermute | solution.py:366
  27.2 0.6 shard_map.86
  27.8 5.7 %collective-permute-start.4 = (bf16[4,256,256]{2,1,0:T(8,128)(2,1)S(1)}, bf16[4,256,256]{2,1,0:T(8,128)(2,1)S(1)}, u32[]{:S(2)}, u32[]{:S(2)}) collective-permute-start(bf16[4,256,256]{2,1,0:T(8,128)(2,1)S(1)} %shard_map.86), channel_id=1, source_target_pairs={{0,1},{1,0},{2,3},{3,2},{4,5},{5,4},{6,7},{7,6},{8,9},{9,8},{10,11... | collective-permute-start | bytes 1572872 | tf_op jit(solution)/shard_map/ppermute | solution.py:359
  33.9 0.8 shard_map.85
  34.7 2.9 %collective-permute-start.3 = (bf16[1152,128]{1,0:T(8,128)(2,1)S(1)}, bf16[1152,128]{1,0:T(8,128)(2,1)S(1)}, u32[]{:S(2)}, u32[]{:S(2)}) collective-permute-start(bf16[1152,128]{1,0:T(8,128)(2,1)S(1)} %get-tuple-element.41), channel_id=1, source_target_pairs={{0,32},{8,40},{16,48},{24,56},{32,64},{40,72},{48,80},{56,88},{64,... | collective-permute-start | bytes 884744 | tf_op jit(solution)/shard_map/ppermute | solution.py:376
  37.6 4.5 %collective-permute-start.7 = (bf16[1152,128]{1,0:T(8,128)(2,1)S(1)}, bf16[1152,128]{1,0:T(8,128)(2,1)S(1)}, u32[]{:S(2)}, u32[]{:S(2)}) collective-permute-start(bf16[1152,128]{1,0:T(8,128)(2,1)S(1)} %get-tuple-element.41), channel_id=1, source_target_pairs={{0,1},{1,32},{2,3},{3,34},{4,5},{5,36},{6,7},{7,38},{8,9},{9,40},{... | collective-permute-start | bytes 884744 | tf_op jit(solution)/shard_map/ppermute | solution.py:375
  42.1 3.6 %collective-permute-done.3.d2_ref = bf16[1152,128]{1,0:T(8,128)(2,1)S(1)} collective-permute-done((bf16[1152,128]{1,0:T(8,128)(2,1)S(1)}, bf16[1152,128]{1,0:T(8,128)(2,1)S(1)}, u32[]{:S(2)}, u32[]{:S(2)}) %collective-permute-start.3) | collective-permute-done | bytes 294944 | tf_op jit(solution)/shard_map/ppermute | solution.py:376
  45.7 3.7 %collective-permute-start.6 = (bf16[1152,128]{1,0:T(8,128)(2,1)S(1)}, bf16[1152,128]{1,0:T(8,128)(2,1)S(1)}, u32[]{:S(2)}, u32[]{:S(2)}) collective-permute-start(bf16[1152,128]{1,0:T(8,128)(2,1)S(1)} %collective-permute-done.3.d2_ref), channel_id=1, source_target_pairs={{0,1},{1,32},{2,3},{3,34},{4,5},{5,36},{6,7},{7,38},{8,9},{9,40},{... | collective-permute-start | bytes 884744 | tf_op jit(solution)/shard_map/ppermute | solution.py:378
  49.4 1.9 %collective-permute-start.5 = (bf16[1152,128]{1,0:T(8,128)(2,1)S(1)}, bf16[1152,128]{1,0:T(8,128)(2,1)S(1)}, u32[]{:S(2)}, u32[]{:S(2)}) collective-permute-start(bf16[1152,128]{1,0:T(8,128)(2,1)S(1)} %collective-permute-done.3.d2_ref), channel_id=1, source_target_pairs={{0,32},{8,40},{16,48},{24,56},{32,64},{40,72},{48,80},{56,88},{64,... | collective-permute-start | bytes 884744 | tf_op jit(solution)/shard_map/ppermute | solution.py:379
  51.3 2.0 %shard_map.87 = (f32[2,256,128]{2,1,0:T(8,128)S(1)}, f32[2,256,128]{2,1,0:T(8,128)S(1)}, f32[2,256,128]{2,1,0:T(8,128)S(1)}, bf16[2,256,128]{2,1,0:T(8,128)(2,1)S(1)}) custom-call(s32[3]{0:T(128)S(1)} %pad_add_fusion.at_ref, bf16[3,2,256,128]{3,2,1,0:T(8,128)(2,1)S(1)} %get-tuple-element.43.q_ref, f32[2,16,128]{2,1,0:T(8,128)S(1)} %get-tuple-element.40.hop_ref, ...), custom_call_target="tpu_custom_call" | custom-call | flops 2147483648 | bytes 1048576 | tf_op jit(solution)/shard_map/pallas_call | solution.py:381
  53.4 1.6 %collective-permute-done.6.d3_ref = bf16[1152,128]{1,0:T(8,128)(2,1)S(1)} collective-permute-done((bf16[1152,128]{1,0:T(8,128)(2,1)S(1)}, bf16[1152,128]{1,0:T(8,128)(2,1)S(1)}, u32[]{:S(2)}, u32[]{:S(2)}) %collective-permute-start.6) | collective-permute-done | bytes 294944 | tf_op jit(solution)/shard_map/ppermute | solution.py:378
  55.0 1.5 %shard_map.88 = (f32[2,256,128]{2,1,0:T(8,128)S(1)}, f32[2,256,128]{2,1,0:T(8,128)S(1)}, f32[2,256,128]{2,1,0:T(8,128)S(1)}, bf16[2,256,128]{2,1,0:T(8,128)(2,1)S(1)}) custom-call(s32[3]{0:T(128)S(1)} %pad_add_fusion.at_ref, f32[2,16,128]{2,1,0:T(8,128)S(1)} %get-tuple-element.40.hop_ref, bf16[1152,128]{1,0:T(8,128)(2,1)S(1)} %collective-permute-done.6.d3_ref, ...), custom_call_target="tpu_custom_call" | custom-call | flops 1073741824 | bytes 1048576 | tf_op jit(solution)/shard_map/pallas_call | solution.py:382
  56.5 4.9 %collective-permute-done.5.d4_ref = bf16[1152,128]{1,0:T(8,128)(2,1)S(1)} collective-permute-done((bf16[1152,128]{1,0:T(8,128)(2,1)S(1)}, bf16[1152,128]{1,0:T(8,128)(2,1)S(1)}, u32[]{:S(2)}, u32[]{:S(2)}) %collective-permute-start.5) | collective-permute-done | bytes 294944 | tf_op jit(solution)/shard_map/ppermute | solution.py:379
  61.4 1.6 %shard_map.89 = (bf16[272,128]{1,0:T(8,128)(2,1)S(1)}, bf16[272,128]{1,0:T(8,128)(2,1)S(1)}) custom-call(s32[3]{0:T(128)S(1)} %pad_add_fusion.at_ref, f32[2,16,128]{2,1,0:T(8,128)S(1)} %get-tuple-element.40.hop_ref, bf16[1152,128]{1,0:T(8,128)(2,1)S(1)} %collective-permute-done.5.d4_ref, f32[2,256,128]{2,1,0:T(8,128)S(1)} %get-tuple-element.48.acc_ref, ...), custom_call_target="tpu_custom_call" | custom-call | flops 1073741824 | bytes 1048576 | tf_op jit(solution)/shard_map/pallas_call | solution.py:383
  63.0 0.7 collective-permute-start.8
  63.7 4.4 %collective-permute-start.9 = (bf16[272,128]{1,0:T(8,128)(2,1)S(1)}, bf16[272,128]{1,0:T(8,128)(2,1)S(1)}, u32[]{:S(2)}, u32[]{:S(2)}) collective-permute-start(bf16[272,128]{1,0:T(8,128)(2,1)S(1)} %get-tuple-element.53), channel_id=1, source_target_pairs={{8,0},{24,1},{10,2},{26,3},{12,4},{28,5},{14,6},{30,7},{0,8},{16,9... | collective-permute-start | bytes 208904 | tf_op jit(solution)/shard_map/ppermute | solution.py:387
  68.1 0.9 shard_map.90
  69.0 1.5 %collective-permute-done.9.g1_ref = bf16[272,128]{1,0:T(8,128)(2,1)S(1)} collective-permute-done((bf16[272,128]{1,0:T(8,128)(2,1)S(1)}, bf16[272,128]{1,0:T(8,128)(2,1)S(1)}, u32[]{:S(2)}, u32[]{:S(2)}) %collective-permute-start.9) | collective-permute-done | bytes 69664 | tf_op jit(solution)/shard_map/ppermute | solution.py:387
  70.6 1.0 %shard_map.91.mine_ref = bf16[256,256]{1,0:T(8,128)(2,1)S(1)} custom-call(s32[3]{0:T(128)S(1)} %pad_add_fusion.at_ref, bf16[272,128]{1,0:T(8,128)(2,1)S(1)} %collective-permute-done.8.g0_ref, bf16[272,128]{1,0:T(8,128)(2,1)S(1)} %collective-permute-done.9.g1_ref, f32[2,256,128]{2,1,0:T(8,128)S(1)} %get-tuple-element.58.acc_ref, ...), custom_call_target="tpu_custom_call" | custom-call | flops 268435456 | bytes 1048576 | tf_op jit(solution)/shard_map/pallas_call | solution.py:388
  71.5 6.8 %collective-permute-start.10 = (bf16[256,256]{1,0:T(8,128)(2,1)S(1)}, bf16[256,256]{1,0:T(8,128)(2,1)S(1)}, u32[]{:S(2)}, u32[]{:S(2)}) collective-permute-start(bf16[256,256]{1,0:T(8,128)(2,1)S(1)} %shard_map.91.mine_ref), channel_id=1, source_target_pairs={{0,1},{1,0},{2,3},{3,2},{4,5},{5,4},{6,7},{7,6},{8,9},{9,8},{10,11... | collective-permute-start | bytes 393224 | tf_op jit(solution)/shard_map/ppermute | solution.py:389
  78.3 0.8 shard_map.92.part_ref
  79.6 12.7 %all_to_all.10.x_ref = bf16[4,256,256]{2,1,0:T(8,128)(2,1)S(1)} all-to-all(bf16[4,256,256]{2,1,0:T(8,128)(2,1)S(1)} %shard_map.93), channel_id=1, replica_groups={{0,2,4,6},{1,3,5,7},{8,10,12,14},{9,11,13,15},{16,18,20,22},{17,19,21,2..., dimensions={0} | all-to-all | bytes 1048576 | tf_op jit(solution)/shard_map/all_to_all | solution.py:392
  92.2 0.7 shard_map.94
  (19 shorter events, 0.9 us)
Async XLA Ops:
  1.7 4.6 %copy-start.4 = (bf16[256,256]{1,0:T(8,128)(2,1)S(1)}, bf16[256,256]{1,0:T(8,128)(2,1)}, u32[]{:S(2)}) copy-start(bf16[256,256]{1,0:T(8,128)(2,1)} %dirs_ref.1) | copy-start | bytes 393220
  1.8 4.6 %copy-start.5 = (f32[2,256]{1,0:T(2,128)S(1)}, f32[2,256]{1,0:T(2,128)}, u32[]{:S(2)}) copy-start(f32[2,256]{1,0:T(2,128)} %beta_ref.1) | copy-start | bytes 6148
  1.8 14.1 %all-to-all-start = ((bf16[4,256,256]{2,1,0:T(8,128)(2,1)}), bf16[4,256,256]{2,1,0:T(8,128)(2,1)S(1)}, u32[]{:S(2)}, u32[]{:S(2)}) async-start(bf16[4,256,256]{2,1,0:T(8,128)(2,1)} %shard_map.82), calls=%async_computation | async-start | bytes 1048576 | tf_op jit(solution)/shard_map/all_to_all | solution.py:355
  6.4 13.3 %copy-start.1 = (bf16[2048,256]{1,0:T(8,128)(2,1)S(1)}, bf16[2048,256]{1,0:T(8,128)(2,1)}, u32[]{:S(2)}) copy-start(bf16[2048,256]{1,0:T(8,128)(2,1)} %wq_ref.1) | copy-start | bytes 3145732
  6.4 13.3 %copy-start.2 = (bf16[2048,256]{1,0:T(8,128)(2,1)S(1)}, bf16[2048,256]{1,0:T(8,128)(2,1)}, u32[]{:S(2)}) copy-start(bf16[2048,256]{1,0:T(8,128)(2,1)} %wk_ref.1) | copy-start | bytes 3145732
  15.9 3.8 %collective-permute-start = (bf16[4,256,256]{2,1,0:T(8,128)(2,1)S(1)}, bf16[4,256,256]{2,1,0:T(8,128)(2,1)S(1)}, u32[]{:S(2)}, u32[]{:S(2)}) collective-permute-start(bf16[4,256,256]{2,1,0:T(8,128)(2,1)S(1)} %all-to-all-done.x_ref), channel_id=1, source_target_pairs={{0,1},{1,0},{2,3},{3,2},{4,5},{5,4},{6,7},{7,6},{8,9},{9,8},{10,11... | collective-permute-start | bytes 1572872 | tf_op jit(solution)/shard_map/ppermute | solution.py:357
  19.7 1.2 %copy-start.3 = (bf16[2048,256]{1,0:T(8,128)(2,1)S(1)}, bf16[2048,256]{1,0:T(8,128)(2,1)}, u32[]{:S(2)}) copy-start(bf16[2048,256]{1,0:T(8,128)(2,1)} %wv_ref.1) | copy-start | bytes 3145732
  20.9 6.3 %copy-start = (bf16[256,2048]{1,0:T(8,128)(2,1)S(1)}, bf16[256,2048]{1,0:T(8,128)(2,1)}, u32[]{:S(2)}) copy-start(bf16[256,2048]{1,0:T(8,128)(2,1)} %wo_ref.3) | copy-start | bytes 3145732
  23.1 10.4 %collective-permute-start.1 = (bf16[912,128]{1,0:T(8,128)(2,1)S(1)}, bf16[912,128]{1,0:T(8,128)(2,1)S(1)}, u32[]{:S(2)}, u32[]{:S(2)}) collective-permute-start(bf16[912,128]{1,0:T(8,128)(2,1)S(1)} %get-tuple-element.38), channel_id=1, source_target_pairs={{0,0},{1,16},{2,2},{3,18},{4,4},{5,20},{6,6},{7,22},{8,8},{9,24},{... | collective-permute-start | bytes 700424 | tf_op jit(solution)/shard_map/ppermute | solution.py:365
  23.8 10.1 %collective-permute-start.2 = (bf16[912,128]{1,0:T(8,128)(2,1)S(1)}, bf16[912,128]{1,0:T(8,128)(2,1)S(1)}, u32[]{:S(2)}, u32[]{:S(2)}) collective-permute-start(bf16[912,128]{1,0:T(8,128)(2,1)S(1)} %get-tuple-element.39), channel_id=1, source_target_pairs={{0,8},{1,24},{2,10},{3,26},{4,12},{5,28},{6,14},{7,30},{8,0},{9,16... | collective-permute-start | bytes 700424 | tf_op jit(solution)/shard_map/ppermute | solution.py:366
  27.8 14.3 %collective-permute-start.4 = (bf16[4,256,256]{2,1,0:T(8,128)(2,1)S(1)}, bf16[4,256,256]{2,1,0:T(8,128)(2,1)S(1)}, u32[]{:S(2)}, u32[]{:S(2)}) collective-permute-start(bf16[4,256,256]{2,1,0:T(8,128)(2,1)S(1)} %shard_map.86), channel_id=1, source_target_pairs={{0,1},{1,0},{2,3},{3,2},{4,5},{5,4},{6,7},{7,6},{8,9},{9,8},{10,11... | collective-permute-start | bytes 1572872 | tf_op jit(solution)/shard_map/ppermute | solution.py:359
  34.7 11.0 %collective-permute-start.3 = (bf16[1152,128]{1,0:T(8,128)(2,1)S(1)}, bf16[1152,128]{1,0:T(8,128)(2,1)S(1)}, u32[]{:S(2)}, u32[]{:S(2)}) collective-permute-start(bf16[1152,128]{1,0:T(8,128)(2,1)S(1)} %get-tuple-element.41), channel_id=1, source_target_pairs={{0,32},{8,40},{16,48},{24,56},{32,64},{40,72},{48,80},{56,88},{64,... | collective-permute-start | bytes 884744 | tf_op jit(solution)/shard_map/ppermute | solution.py:376
  37.6 13.7 %collective-permute-start.7 = (bf16[1152,128]{1,0:T(8,128)(2,1)S(1)}, bf16[1152,128]{1,0:T(8,128)(2,1)S(1)}, u32[]{:S(2)}, u32[]{:S(2)}) collective-permute-start(bf16[1152,128]{1,0:T(8,128)(2,1)S(1)} %get-tuple-element.41), channel_id=1, source_target_pairs={{0,1},{1,32},{2,3},{3,34},{4,5},{5,36},{6,7},{7,38},{8,9},{9,40},{... | collective-permute-start | bytes 884744 | tf_op jit(solution)/shard_map/ppermute | solution.py:375
  45.7 9.2 %collective-permute-start.6 = (bf16[1152,128]{1,0:T(8,128)(2,1)S(1)}, bf16[1152,128]{1,0:T(8,128)(2,1)S(1)}, u32[]{:S(2)}, u32[]{:S(2)}) collective-permute-start(bf16[1152,128]{1,0:T(8,128)(2,1)S(1)} %collective-permute-done.3.d2_ref), channel_id=1, source_target_pairs={{0,1},{1,32},{2,3},{3,34},{4,5},{5,36},{6,7},{7,38},{8,9},{9,40},{... | collective-permute-start | bytes 884744 | tf_op jit(solution)/shard_map/ppermute | solution.py:378
  49.4 12.0 %collective-permute-start.5 = (bf16[1152,128]{1,0:T(8,128)(2,1)S(1)}, bf16[1152,128]{1,0:T(8,128)(2,1)S(1)}, u32[]{:S(2)}, u32[]{:S(2)}) collective-permute-start(bf16[1152,128]{1,0:T(8,128)(2,1)S(1)} %collective-permute-done.3.d2_ref), channel_id=1, source_target_pairs={{0,32},{8,40},{16,48},{24,56},{32,64},{40,72},{48,80},{56,88},{64,... | collective-permute-start | bytes 884744 | tf_op jit(solution)/shard_map/ppermute | solution.py:379
  63.0 6.0 %collective-permute-start.8 = (bf16[272,128]{1,0:T(8,128)(2,1)S(1)}, bf16[272,128]{1,0:T(8,128)(2,1)S(1)}, u32[]{:S(2)}, u32[]{:S(2)}) collective-permute-start(bf16[272,128]{1,0:T(8,128)(2,1)S(1)} %get-tuple-element.52), channel_id=1, source_target_pairs={{0,0},{16,1},{2,2},{18,3},{4,4},{20,5},{6,6},{22,7},{8,8},{24,9},{... | collective-permute-start | bytes 208904 | tf_op jit(solution)/shard_map/ppermute | solution.py:386
  63.7 6.9 %collective-permute-start.9 = (bf16[272,128]{1,0:T(8,128)(2,1)S(1)}, bf16[272,128]{1,0:T(8,128)(2,1)S(1)}, u32[]{:S(2)}, u32[]{:S(2)}) collective-permute-start(bf16[272,128]{1,0:T(8,128)(2,1)S(1)} %get-tuple-element.53), channel_id=1, source_target_pairs={{8,0},{24,1},{10,2},{26,3},{12,4},{28,5},{14,6},{30,7},{0,8},{16,9... | collective-permute-start | bytes 208904 | tf_op jit(solution)/shard_map/ppermute | solution.py:387
  71.5 7.7 %collective-permute-start.10 = (bf16[256,256]{1,0:T(8,128)(2,1)S(1)}, bf16[256,256]{1,0:T(8,128)(2,1)S(1)}, u32[]{:S(2)}, u32[]{:S(2)}) collective-permute-start(bf16[256,256]{1,0:T(8,128)(2,1)S(1)} %shard_map.91.mine_ref), channel_id=1, source_target_pairs={{0,1},{1,0},{2,3},{3,2},{4,5},{5,4},{6,7},{7,6},{8,9},{9,8},{10,11... | collective-permute-start | bytes 393224 | tf_op jit(solution)/shard_map/ppermute | solution.py:389

commit v9 on v8

--- a/solution.py
+++ b/solution.py
@@ -256,7 +256,7 @@
         out_ref[TOK:BACK] = tile.astype(BF16)
 
 
-def merge_kernel(at_ref, g0_ref, g1_ref, acc_ref, lse_ref, out_ref):
+def merge_kernel(at_ref, g1_ref, g0_ref, acc_ref, lse_ref, out_ref):
     swapped = at_ref[0] == 1
     row = lax.broadcasted_iota(jnp.int32, (DH, DH), 0)
     col = lax.broadcasted_iota(jnp.int32, (DH, DH), 1)
@@ -385,7 +385,7 @@
     )
     g0 = lax.ppermute(o0, both, back[0])
     g1 = lax.ppermute(o1, both, back[1])
-    mine = call(merge_kernel, shape((TOK, 2 * DH)), 5, smem=1, flops=2**28)(at, g0, g1, acc, lse)
+    mine = call(merge_kernel, shape((TOK, 2 * DH)), 5, smem=1, flops=2**28)(at, g1, g0, acc, lse)
     theirs = lax.ppermute(mine, "head", twin)
     part = call(mine_kernel, shape((4, TOK, 256), F32), 3, smem=1, flops=2**29)(at, mine, w_out)
     partial = call(output_kernel, shape((4, TOK, 256)), 3, flops=2**28)(part, theirs, other_out)

time: 93.5 us -> 93.8 us (level)
  starting transfers between devices: 41.1 us -> 42.3 us
    ppermute x1, starting transfers between devices: 6.75 us -> 7.91 us  [shards(): theirs = lax.ppermute(mine, 'head', twin)]
where the time goes in v9:
time: 93.8 us; the launch traced here: 93.3 us
  starting transfers between devices  42.3 us (45%)
  waiting for transfers between devices  19.3 us (21%)
  Pallas kernels  16.8 us (18%)
  blocking collectives  12.7 us (14%)
  local copies, waits for them, and re-layouts  1.25 us (1%)
    all_to_all x1, blocking collectives, shards(): pieces = lax.all_to_all(partial, 'head', 0, 0, axis_index_groups=planes)  12.7 us
    ppermute x1, starting transfers between devices, shards(): theirs = lax.ppermute(mine, 'head', twin)  7.91 us
    all_to_all x1, waiting for transfers between devices, shards(): gathered = lax.all_to_all(copies, 'head', 0, 0, axis_index_groups=planes)  6.82 us
    ppermute x1, starting transfers between devices, shards(): other_out = lax.ppermute(halves, 'head', twin)  5.67 us
    ppermute x1, waiting for transfers between devices, shards(): d4 = lax.ppermute(d2, 'ctx', down)  4.94 us
    all_to_all x1, starting transfers between devices, shards(): gathered = lax.all_to_all(copies, 'head', 0, 0, axis_index_groups=planes)  4.61 us
    ppermute x1, starting transfers between devices, shards(): d1 = lax.ppermute(own_pair, both, follow)  4.48 us
    ppermute x1, starting transfers between devices, shards(): g1 = lax.ppermute(o1, both, back[1])  4.41 us
  transfers between devices with their start and end apart: 12, of which 8 were waited for; matrix products, arithmetic and copies ran while one was open for 0% of the time, Pallas kernels for 10%

profile of v9, /device:TPU:384, one launch (start us, length us, event | category | flops | bytes accessed | tf_op | source)
XLA Modules:
  0.0 93.3 jit_solution(7754876032592125888)
XLA Ops:
  0.0 1.7 %shard_map.82 = bf16[4,256,256]{2,1,0:T(8,128)(2,1)} custom-call(bf16[256,256]{1,0:T(8,128)(2,1)} %x_ref.1), custom_call_target="tpu_custom_call" | custom-call | bytes 1048576 | tf_op jit(solution)/shard_map/pallas_call | solution.py:346
  1.8 4.6 %all-to-all-start = ((bf16[4,256,256]{2,1,0:T(8,128)(2,1)}), bf16[4,256,256]{2,1,0:T(8,128)(2,1)S(1)}, u32[]{:S(2)}, u32[]{:S(2)}) async-start(bf16[4,256,256]{2,1,0:T(8,128)(2,1)} %shard_map.82), calls=%async_computation | async-start | bytes 1048576 | tf_op jit(solution)/shard_map/all_to_all | solution.py:355
  6.4 2.6 %shard_map.83 = (bf16[2,256,128]{2,1,0:T(8,128)(2,1)S(1)}, bf16[2,256,256]{2,1,0:T(8,128)(2,1)S(1)}, f32[8,128]{1,0:T(8,128)S(1)}) custom-call(bf16[256,256]{1,0:T(8,128)(2,1)S(1)} %copy-done.4, f32[2,256]{1,0:T(2,128)S(1)} %copy-done.5), custom_call_target="tpu_custom_call" | custom-call | flops 4294967296 | bytes 1048576 | tf_op jit(solution)/shard_map/pallas_call | solution.py:342
  9.0 6.8 %all-to-all-done.x_ref = bf16[4,256,256]{2,1,0:T(8,128)(2,1)S(1)} async-done(((bf16[4,256,256]{2,1,0:T(8,128)(2,1)}), bf16[4,256,256]{2,1,0:T(8,128)(2,1)S(1)}, u32[]{:S(2)}, u32[]{:S(2)}) %all-to-all-start) | async-done | bytes 524320 | tf_op jit(solution)/shard_map/all_to_all | solution.py:355
  15.9 1.9 %collective-permute-start = (bf16[4,256,256]{2,1,0:T(8,128)(2,1)S(1)}, bf16[4,256,256]{2,1,0:T(8,128)(2,1)S(1)}, u32[]{:S(2)}, u32[]{:S(2)}) collective-permute-start(bf16[4,256,256]{2,1,0:T(8,128)(2,1)S(1)} %all-to-all-done.x_ref), channel_id=1, source_target_pairs={{0,1},{1,0},{2,3},{3,2},{4,5},{5,4},{6,7},{7,6},{8,9},{9,8},{10,11... | collective-permute-start | bytes 1572872 | tf_op jit(solution)/shard_map/ppermute | solution.py:357
  18.5 1.1 %collective-permute-done.o_ref = bf16[4,256,256]{2,1,0:T(8,128)(2,1)S(1)} collective-permute-done((bf16[4,256,256]{2,1,0:T(8,128)(2,1)S(1)}, bf16[4,256,256]{2,1,0:T(8,128)(2,1)S(1)}, u32[]{:S(2)}, u32[]{:S(2)}) %collective-permute-start) | collective-permute-done | bytes 524320 | tf_op jit(solution)/shard_map/ppermute | solution.py:357
  19.7 1.2 %copy-done.3 = bf16[2048,256]{1,0:T(8,128)(2,1)S(1)} copy-done((bf16[2048,256]{1,0:T(8,128)(2,1)S(1)}, bf16[2048,256]{1,0:T(8,128)(2,1)}, u32[]{:S(2)}) %copy-start.3) | copy-done | bytes 1048600
  20.9 2.2 %shard_map.84 = (bf16[912,128]{1,0:T(8,128)(2,1)S(1)}, bf16[912,128]{1,0:T(8,128)(2,1)S(1)}, bf16[2,256,128]{2,1,0:T(8,128)(2,1)S(1)}, bf16[2,256,128]{2,1,0:T(8...) custom-call(s32[3]{0:T(128)S(1)} %pad_add_fusion.at_ref, s32[1]{0:T(128)S(6)} %copy.9.hop_ref, ...), custom_call_target="tpu_custom_call" | custom-call | flops 1073741824 | bytes 1048576 | tf_op jit(solution)/shard_map/pallas_call | solution.py:360
  23.1 0.7 collective-permute-start.1
  23.8 3.4 %collective-permute-start.2 = (bf16[912,128]{1,0:T(8,128)(2,1)S(1)}, bf16[912,128]{1,0:T(8,128)(2,1)S(1)}, u32[]{:S(2)}, u32[]{:S(2)}) collective-permute-start(bf16[912,128]{1,0:T(8,128)(2,1)S(1)} %get-tuple-element.39), channel_id=1, source_target_pairs={{0,8},{1,24},{2,10},{3,26},{4,12},{5,28},{6,14},{7,30},{8,0},{9,16... | collective-permute-start | bytes 700424 | tf_op jit(solution)/shard_map/ppermute | solution.py:366
  27.2 0.6 shard_map.86
  27.8 5.7 %collective-permute-start.4 = (bf16[4,256,256]{2,1,0:T(8,128)(2,1)S(1)}, bf16[4,256,256]{2,1,0:T(8,128)(2,1)S(1)}, u32[]{:S(2)}, u32[]{:S(2)}) collective-permute-start(bf16[4,256,256]{2,1,0:T(8,128)(2,1)S(1)} %shard_map.86), channel_id=1, source_target_pairs={{0,1},{1,0},{2,3},{3,2},{4,5},{5,4},{6,7},{7,6},{8,9},{9,8},{10,11... | collective-permute-start | bytes 1572872 | tf_op jit(solution)/shard_map/ppermute | solution.py:359
  33.9 0.8 shard_map.85
  34.7 2.9 %collective-permute-start.3 = (bf16[1152,128]{1,0:T(8,128)(2,1)S(1)}, bf16[1152,128]{1,0:T(8,128)(2,1)S(1)}, u32[]{:S(2)}, u32[]{:S(2)}) collective-permute-start(bf16[1152,128]{1,0:T(8,128)(2,1)S(1)} %get-tuple-element.41), channel_id=1, source_target_pairs={{0,32},{8,40},{16,48},{24,56},{32,64},{40,72},{48,80},{56,88},{64,... | collective-permute-start | bytes 884744 | tf_op jit(solution)/shard_map/ppermute | solution.py:376
  37.6 4.5 %collective-permute-start.7 = (bf16[1152,128]{1,0:T(8,128)(2,1)S(1)}, bf16[1152,128]{1,0:T(8,128)(2,1)S(1)}, u32[]{:S(2)}, u32[]{:S(2)}) collective-permute-start(bf16[1152,128]{1,0:T(8,128)(2,1)S(1)} %get-tuple-element.41), channel_id=1, source_target_pairs={{0,1},{1,32},{2,3},{3,34},{4,5},{5,36},{6,7},{7,38},{8,9},{9,40},{... | collective-permute-start | bytes 884744 | tf_op jit(solution)/shard_map/ppermute | solution.py:375
  42.1 3.6 %collective-permute-done.3.d2_ref = bf16[1152,128]{1,0:T(8,128)(2,1)S(1)} collective-permute-done((bf16[1152,128]{1,0:T(8,128)(2,1)S(1)}, bf16[1152,128]{1,0:T(8,128)(2,1)S(1)}, u32[]{:S(2)}, u32[]{:S(2)}) %collective-permute-start.3) | collective-permute-done | bytes 294944 | tf_op jit(solution)/shard_map/ppermute | solution.py:376
  45.7 3.7 %collective-permute-start.6 = (bf16[1152,128]{1,0:T(8,128)(2,1)S(1)}, bf16[1152,128]{1,0:T(8,128)(2,1)S(1)}, u32[]{:S(2)}, u32[]{:S(2)}) collective-permute-start(bf16[1152,128]{1,0:T(8,128)(2,1)S(1)} %collective-permute-done.3.d2_ref), channel_id=1, source_target_pairs={{0,1},{1,32},{2,3},{3,34},{4,5},{5,36},{6,7},{7,38},{8,9},{9,40},{... | collective-permute-start | bytes 884744 | tf_op jit(solution)/shard_map/ppermute | solution.py:378
  49.4 1.9 %collective-permute-start.5 = (bf16[1152,128]{1,0:T(8,128)(2,1)S(1)}, bf16[1152,128]{1,0:T(8,128)(2,1)S(1)}, u32[]{:S(2)}, u32[]{:S(2)}) collective-permute-start(bf16[1152,128]{1,0:T(8,128)(2,1)S(1)} %collective-permute-done.3.d2_ref), channel_id=1, source_target_pairs={{0,32},{8,40},{16,48},{24,56},{32,64},{40,72},{48,80},{56,88},{64,... | collective-permute-start | bytes 884744 | tf_op jit(solution)/shard_map/ppermute | solution.py:379
  51.3 2.0 %shard_map.87 = (f32[2,256,128]{2,1,0:T(8,128)S(1)}, f32[2,256,128]{2,1,0:T(8,128)S(1)}, f32[2,256,128]{2,1,0:T(8,128)S(1)}, bf16[2,256,128]{2,1,0:T(8,128)(2,1)S(1)}) custom-call(s32[3]{0:T(128)S(1)} %pad_add_fusion.at_ref, bf16[3,2,256,128]{3,2,1,0:T(8,128)(2,1)S(1)} %get-tuple-element.43.q_ref, f32[2,16,128]{2,1,0:T(8,128)S(1)} %get-tuple-element.40.hop_ref, ...), custom_call_target="tpu_custom_call" | custom-call | flops 2147483648 | bytes 1048576 | tf_op jit(solution)/shard_map/pallas_call | solution.py:381
  53.4 1.6 %collective-permute-done.6.d3_ref = bf16[1152,128]{1,0:T(8,128)(2,1)S(1)} collective-permute-done((bf16[1152,128]{1,0:T(8,128)(2,1)S(1)}, bf16[1152,128]{1,0:T(8,128)(2,1)S(1)}, u32[]{:S(2)}, u32[]{:S(2)}) %collective-permute-start.6) | collective-permute-done | bytes 294944 | tf_op jit(solution)/shard_map/ppermute | solution.py:378
  55.0 1.5 %shard_map.88 = (f32[2,256,128]{2,1,0:T(8,128)S(1)}, f32[2,256,128]{2,1,0:T(8,128)S(1)}, f32[2,256,128]{2,1,0:T(8,128)S(1)}, bf16[2,256,128]{2,1,0:T(8,128)(2,1)S(1)}) custom-call(s32[3]{0:T(128)S(1)} %pad_add_fusion.at_ref, f32[2,16,128]{2,1,0:T(8,128)S(1)} %get-tuple-element.40.hop_ref, bf16[1152,128]{1,0:T(8,128)(2,1)S(1)} %collective-permute-done.6.d3_ref, ...), custom_call_target="tpu_custom_call" | custom-call | flops 1073741824 | bytes 1048576 | tf_op jit(solution)/shard_map/pallas_call | solution.py:382
  56.5 4.9 %collective-permute-done.5.d4_ref = bf16[1152,128]{1,0:T(8,128)(2,1)S(1)} collective-permute-done((bf16[1152,128]{1,0:T(8,128)(2,1)S(1)}, bf16[1152,128]{1,0:T(8,128)(2,1)S(1)}, u32[]{:S(2)}, u32[]{:S(2)}) %collective-permute-start.5) | collective-permute-done | bytes 294944 | tf_op jit(solution)/shard_map/ppermute | solution.py:379
  61.4 1.6 %shard_map.89 = (bf16[272,128]{1,0:T(8,128)(2,1)S(1)}, bf16[272,128]{1,0:T(8,128)(2,1)S(1)}) custom-call(s32[3]{0:T(128)S(1)} %pad_add_fusion.at_ref, f32[2,16,128]{2,1,0:T(8,128)S(1)} %get-tuple-element.40.hop_ref, bf16[1152,128]{1,0:T(8,128)(2,1)S(1)} %collective-permute-done.5.d4_ref, f32[2,256,128]{2,1,0:T(8,128)S(1)} %get-tuple-element.48.acc_ref, ...), custom_call_target="tpu_custom_call" | custom-call | flops 1073741824 | bytes 1048576 | tf_op jit(solution)/shard_map/pallas_call | solution.py:383
  63.0 4.4 %collective-permute-start.8 = (bf16[272,128]{1,0:T(8,128)(2,1)S(1)}, bf16[272,128]{1,0:T(8,128)(2,1)S(1)}, u32[]{:S(2)}, u32[]{:S(2)}) collective-permute-start(bf16[272,128]{1,0:T(8,128)(2,1)S(1)} %get-tuple-element.52), channel_id=1, source_target_pairs={{8,0},{24,1},{10,2},{26,3},{12,4},{28,5},{14,6},{30,7},{0,8},{16,9... | collective-permute-start | bytes 208904 | tf_op jit(solution)/shard_map/ppermute | solution.py:387
  67.4 0.7 collective-permute-start.9
  68.1 0.9 shard_map.90
  69.0 0.7 collective-permute-done.8.g1_ref
  69.7 1.0 %shard_map.91.mine_ref = bf16[256,256]{1,0:T(8,128)(2,1)S(1)} custom-call(s32[3]{0:T(128)S(1)} %pad_add_fusion.at_ref, bf16[272,128]{1,0:T(8,128)(2,1)S(1)} %collective-permute-done.8.g1_ref, bf16[272,128]{1,0:T(8,128)(2,1)S(1)} %collective-permute-done.9.g0_ref, f32[2,256,128]{2,1,0:T(8,128)S(1)} %get-tuple-element.58.acc_ref, ...), custom_call_target="tpu_custom_call" | custom-call | flops 268435456 | bytes 1048576 | tf_op jit(solution)/shard_map/pallas_call | solution.py:388
  70.7 7.9 %collective-permute-start.10 = (bf16[256,256]{1,0:T(8,128)(2,1)S(1)}, bf16[256,256]{1,0:T(8,128)(2,1)S(1)}, u32[]{:S(2)}, u32[]{:S(2)}) collective-permute-start(bf16[256,256]{1,0:T(8,128)(2,1)S(1)} %shard_map.91.mine_ref), channel_id=1, source_target_pairs={{0,1},{1,0},{2,3},{3,2},{4,5},{5,4},{6,7},{7,6},{8,9},{9,8},{10,11... | collective-permute-start | bytes 393224 | tf_op jit(solution)/shard_map/ppermute | solution.py:389
  78.6 0.9 shard_map.92.part_ref
  79.9 12.7 %all_to_all.10.x_ref = bf16[4,256,256]{2,1,0:T(8,128)(2,1)S(1)} all-to-all(bf16[4,256,256]{2,1,0:T(8,128)(2,1)S(1)} %shard_map.93), channel_id=1, replica_groups={{0,2,4,6},{1,3,5,7},{8,10,12,14},{9,11,13,15},{16,18,20,22},{17,19,21,2..., dimensions={0} | all-to-all | bytes 1048576 | tf_op jit(solution)/shard_map/all_to_all | solution.py:392
  92.6 0.7 shard_map.94
  (19 shorter events, 0.9 us)
Async XLA Ops:
  1.7 4.6 %copy-start.4 = (bf16[256,256]{1,0:T(8,128)(2,1)S(1)}, bf16[256,256]{1,0:T(8,128)(2,1)}, u32[]{:S(2)}) copy-start(bf16[256,256]{1,0:T(8,128)(2,1)} %dirs_ref.1) | copy-start | bytes 393220
  1.8 4.6 %copy-start.5 = (f32[2,256]{1,0:T(2,128)S(1)}, f32[2,256]{1,0:T(2,128)}, u32[]{:S(2)}) copy-start(f32[2,256]{1,0:T(2,128)} %beta_ref.1) | copy-start | bytes 6148
  1.8 14.1 %all-to-all-start = ((bf16[4,256,256]{2,1,0:T(8,128)(2,1)}), bf16[4,256,256]{2,1,0:T(8,128)(2,1)S(1)}, u32[]{:S(2)}, u32[]{:S(2)}) async-start(bf16[4,256,256]{2,1,0:T(8,128)(2,1)} %shard_map.82), calls=%async_computation | async-start | bytes 1048576 | tf_op jit(solution)/shard_map/all_to_all | solution.py:355
  6.4 13.3 %copy-start.1 = (bf16[2048,256]{1,0:T(8,128)(2,1)S(1)}, bf16[2048,256]{1,0:T(8,128)(2,1)}, u32[]{:S(2)}) copy-start(bf16[2048,256]{1,0:T(8,128)(2,1)} %wq_ref.1) | copy-start | bytes 3145732
  6.4 13.3 %copy-start.2 = (bf16[2048,256]{1,0:T(8,128)(2,1)S(1)}, bf16[2048,256]{1,0:T(8,128)(2,1)}, u32[]{:S(2)}) copy-start(bf16[2048,256]{1,0:T(8,128)(2,1)} %wk_ref.1) | copy-start | bytes 3145732
  15.9 3.8 %collective-permute-start = (bf16[4,256,256]{2,1,0:T(8,128)(2,1)S(1)}, bf16[4,256,256]{2,1,0:T(8,128)(2,1)S(1)}, u32[]{:S(2)}, u32[]{:S(2)}) collective-permute-start(bf16[4,256,256]{2,1,0:T(8,128)(2,1)S(1)} %all-to-all-done.x_ref), channel_id=1, source_target_pairs={{0,1},{1,0},{2,3},{3,2},{4,5},{5,4},{6,7},{7,6},{8,9},{9,8},{10,11... | collective-permute-start | bytes 1572872 | tf_op jit(solution)/shard_map/ppermute | solution.py:357
  19.7 1.2 %copy-start.3 = (bf16[2048,256]{1,0:T(8,128)(2,1)S(1)}, bf16[2048,256]{1,0:T(8,128)(2,1)}, u32[]{:S(2)}) copy-start(bf16[2048,256]{1,0:T(8,128)(2,1)} %wv_ref.1) | copy-start | bytes 3145732
  20.9 6.3 %copy-start = (bf16[256,2048]{1,0:T(8,128)(2,1)S(1)}, bf16[256,2048]{1,0:T(8,128)(2,1)}, u32[]{:S(2)}) copy-start(bf16[256,2048]{1,0:T(8,128)(2,1)} %wo_ref.3) | copy-start | bytes 3145732
  23.1 10.4 %collective-permute-start.1 = (bf16[912,128]{1,0:T(8,128)(2,1)S(1)}, bf16[912,128]{1,0:T(8,128)(2,1)S(1)}, u32[]{:S(2)}, u32[]{:S(2)}) collective-permute-start(bf16[912,128]{1,0:T(8,128)(2,1)S(1)} %get-tuple-element.38), channel_id=1, source_target_pairs={{0,0},{1,16},{2,2},{3,18},{4,4},{5,20},{6,6},{7,22},{8,8},{9,24},{... | collective-permute-start | bytes 700424 | tf_op jit(solution)/shard_map/ppermute | solution.py:365
  23.8 10.1 %collective-permute-start.2 = (bf16[912,128]{1,0:T(8,128)(2,1)S(1)}, bf16[912,128]{1,0:T(8,128)(2,1)S(1)}, u32[]{:S(2)}, u32[]{:S(2)}) collective-permute-start(bf16[912,128]{1,0:T(8,128)(2,1)S(1)} %get-tuple-element.39), channel_id=1, source_target_pairs={{0,8},{1,24},{2,10},{3,26},{4,12},{5,28},{6,14},{7,30},{8,0},{9,16... | collective-permute-start | bytes 700424 | tf_op jit(solution)/shard_map/ppermute | solution.py:366
  27.8 14.3 %collective-permute-start.4 = (bf16[4,256,256]{2,1,0:T(8,128)(2,1)S(1)}, bf16[4,256,256]{2,1,0:T(8,128)(2,1)S(1)}, u32[]{:S(2)}, u32[]{:S(2)}) collective-permute-start(bf16[4,256,256]{2,1,0:T(8,128)(2,1)S(1)} %shard_map.86), channel_id=1, source_target_pairs={{0,1},{1,0},{2,3},{3,2},{4,5},{5,4},{6,7},{7,6},{8,9},{9,8},{10,11... | collective-permute-start | bytes 1572872 | tf_op jit(solution)/shard_map/ppermute | solution.py:359
  34.7 11.0 %collective-permute-start.3 = (bf16[1152,128]{1,0:T(8,128)(2,1)S(1)}, bf16[1152,128]{1,0:T(8,128)(2,1)S(1)}, u32[]{:S(2)}, u32[]{:S(2)}) collective-permute-start(bf16[1152,128]{1,0:T(8,128)(2,1)S(1)} %get-tuple-element.41), channel_id=1, source_target_pairs={{0,32},{8,40},{16,48},{24,56},{32,64},{40,72},{48,80},{56,88},{64,... | collective-permute-start | bytes 884744 | tf_op jit(solution)/shard_map/ppermute | solution.py:376
  37.6 13.7 %collective-permute-start.7 = (bf16[1152,128]{1,0:T(8,128)(2,1)S(1)}, bf16[1152,128]{1,0:T(8,128)(2,1)S(1)}, u32[]{:S(2)}, u32[]{:S(2)}) collective-permute-start(bf16[1152,128]{1,0:T(8,128)(2,1)S(1)} %get-tuple-element.41), channel_id=1, source_target_pairs={{0,1},{1,32},{2,3},{3,34},{4,5},{5,36},{6,7},{7,38},{8,9},{9,40},{... | collective-permute-start | bytes 884744 | tf_op jit(solution)/shard_map/ppermute | solution.py:375
  45.7 9.2 %collective-permute-start.6 = (bf16[1152,128]{1,0:T(8,128)(2,1)S(1)}, bf16[1152,128]{1,0:T(8,128)(2,1)S(1)}, u32[]{:S(2)}, u32[]{:S(2)}) collective-permute-start(bf16[1152,128]{1,0:T(8,128)(2,1)S(1)} %collective-permute-done.3.d2_ref), channel_id=1, source_target_pairs={{0,1},{1,32},{2,3},{3,34},{4,5},{5,36},{6,7},{7,38},{8,9},{9,40},{... | collective-permute-start | bytes 884744 | tf_op jit(solution)/shard_map/ppermute | solution.py:378
  49.4 12.0 %collective-permute-start.5 = (bf16[1152,128]{1,0:T(8,128)(2,1)S(1)}, bf16[1152,128]{1,0:T(8,128)(2,1)S(1)}, u32[]{:S(2)}, u32[]{:S(2)}) collective-permute-start(bf16[1152,128]{1,0:T(8,128)(2,1)S(1)} %collective-permute-done.3.d2_ref), channel_id=1, source_target_pairs={{0,32},{8,40},{16,48},{24,56},{32,64},{40,72},{48,80},{56,88},{64,... | collective-permute-start | bytes 884744 | tf_op jit(solution)/shard_map/ppermute | solution.py:379
  63.0 6.7 %collective-permute-start.8 = (bf16[272,128]{1,0:T(8,128)(2,1)S(1)}, bf16[272,128]{1,0:T(8,128)(2,1)S(1)}, u32[]{:S(2)}, u32[]{:S(2)}) collective-permute-start(bf16[272,128]{1,0:T(8,128)(2,1)S(1)} %get-tuple-element.52), channel_id=1, source_target_pairs={{8,0},{24,1},{10,2},{26,3},{12,4},{28,5},{14,6},{30,7},{0,8},{16,9... | collective-permute-start | bytes 208904 | tf_op jit(solution)/shard_map/ppermute | solution.py:387
  67.4 2.3 %collective-permute-start.9 = (bf16[272,128]{1,0:T(8,128)(2,1)S(1)}, bf16[272,128]{1,0:T(8,128)(2,1)S(1)}, u32[]{:S(2)}, u32[]{:S(2)}) collective-permute-start(bf16[272,128]{1,0:T(8,128)(2,1)S(1)} %get-tuple-element.53), channel_id=1, source_target_pairs={{0,0},{16,1},{2,2},{18,3},{4,4},{20,5},{6,6},{22,7},{8,8},{24,9},{... | collective-permute-start | bytes 208904 | tf_op jit(solution)/shard_map/ppermute | solution.py:386
  70.7 8.9 %collective-permute-start.10 = (bf16[256,256]{1,0:T(8,128)(2,1)S(1)}, bf16[256,256]{1,0:T(8,128)(2,1)S(1)}, u32[]{:S(2)}, u32[]{:S(2)}) collective-permute-start(bf16[256,256]{1,0:T(8,128)(2,1)S(1)} %shard_map.91.mine_ref), channel_id=1, source_target_pairs={{0,1},{1,0},{2,3},{3,2},{4,5},{5,4},{6,7},{7,6},{8,9},{9,8},{10,11... | collective-permute-start | bytes 393224 | tf_op jit(solution)/shard_map/ppermute | solution.py:389

commit v10 on v9

--- a/solution.py
+++ b/solution.py
@@ -94,10 +94,18 @@
         t_ref[h] = t
 
 
-def pieces_kernel(x_ref, out_ref, sems):
-    copies = [pltpu.make_async_copy(x_ref, out_ref.at[p], sems.at[p]) for p in range(4)]
-    for copy in copies:
+def pieces_kernel(x_ref, out_ref, held, loads, sems):
+    half = TOK // 2
+    rows = [pl.ds(n * half, half) for n in range(2)]
+    brought = [pltpu.make_async_copy(x_ref.at[r], held.at[r], loads.at[n]) for n, r in enumerate(rows)]
+    for copy in brought:
         copy.start()
+    copies = []
+    for n, r in enumerate(rows):
+        brought[n].wait()
+        for p in range(4):
+            copies.append(pltpu.make_async_copy(held.at[r], out_ref.at[p, r], sems.at[n, p]))
+            copies[-1].start()
     for copy in copies:
         copy.wait()
 
@@ -346,9 +354,11 @@
     copies = pl.pallas_call(
         pieces_kernel,
         out_shape=shape((4, TOK, 256)),
-        in_specs=[VMEM],
+        in_specs=[pl.BlockSpec(memory_space=pltpu.HBM)],
         out_specs=pl.BlockSpec(memory_space=pltpu.HBM),
-        scratch_shapes=[pltpu.SemaphoreType.DMA((4,))],
+        scratch_shapes=[
+            pltpu.VMEM((TOK, 256), BF16), pltpu.SemaphoreType.DMA((2,)), pltpu.SemaphoreType.DMA((2, 4)),
+        ],
         compiler_params=pltpu.CompilerParams(vmem_limit_bytes=62 * 2**20),
         cost_estimate=pl.CostEstimate(flops=0, bytes_accessed=2**20, transcendentals=0),
     )(inputs)

time: 93.8 us -> 93.8 us (level)
  the two profiles are of different devices: /device:TPU:384 before, /device:TPU:256 now
where the time goes in v10:
time: 93.8 us; the launch traced here: 93.3 us
  starting transfers between devices  42.3 us (45%)
  waiting for transfers between devices  19.3 us (21%)
  Pallas kernels  16.8 us (18%)
  blocking collectives  12.7 us (14%)
  local copies, waits for them, and re-layouts  1.25 us (1%)
    all_to_all x1, blocking collectives, shards(): pieces = lax.all_to_all(partial, 'head', 0, 0, axis_index_groups=planes)  12.7 us
    ppermute x1, starting transfers between devices, shards(): theirs = lax.ppermute(mine, 'head', twin)  7.93 us
    all_to_all x1, waiting for transfers between devices, shards(): gathered = lax.all_to_all(copies, 'head', 0, 0, axis_index_groups=planes)  6.82 us
    ppermute x1, starting transfers between devices, shards(): other_out = lax.ppermute(halves, 'head', twin)  5.67 us
    ppermute x1, waiting for transfers between devices, shards(): d4 = lax.ppermute(d2, 'ctx', down)  4.94 us
    all_to_all x1, starting transfers between devices, shards(): gathered = lax.all_to_all(copies, 'head', 0, 0, axis_index_groups=planes)  4.61 us
    ppermute x1, starting transfers between devices, shards(): d1 = lax.ppermute(own_pair, both, follow)  4.48 us
    ppermute x1, starting transfers between devices, shards(): g1 = lax.ppermute(o1, both, back[1])  4.39 us
  transfers between devices with their start and end apart: 12, of which 8 were waited for; matrix products, arithmetic and copies ran while one was open for 0% of the time, Pallas kernels for 10%

profile of v10, /device:TPU:256, one launch (start us, length us, event | category | flops | bytes accessed | tf_op | source)
XLA Modules:
  0.0 93.3 jit_solution(11092181162192951109)
XLA Ops:
  0.0 1.7 %shard_map.82 = bf16[4,256,256]{2,1,0:T(8,128)(2,1)} custom-call(bf16[256,256]{1,0:T(8,128)(2,1)} %x_ref.1), custom_call_target="tpu_custom_call" | custom-call | bytes 1048576 | tf_op jit(solution)/shard_map/pallas_call | solution.py:354
  1.8 4.6 %all-to-all-start = ((bf16[4,256,256]{2,1,0:T(8,128)(2,1)}), bf16[4,256,256]{2,1,0:T(8,128)(2,1)S(1)}, u32[]{:S(2)}, u32[]{:S(2)}) async-start(bf16[4,256,256]{2,1,0:T(8,128)(2,1)} %shard_map.82), calls=%async_computation | async-start | bytes 1048576 | tf_op jit(solution)/shard_map/all_to_all | solution.py:365
  6.4 2.6 %shard_map.83 = (bf16[2,256,128]{2,1,0:T(8,128)(2,1)S(1)}, bf16[2,256,256]{2,1,0:T(8,128)(2,1)S(1)}, f32[8,128]{1,0:T(8,128)S(1)}) custom-call(bf16[256,256]{1,0:T(8,128)(2,1)S(1)} %copy-done.4, f32[2,256]{1,0:T(2,128)S(1)} %copy-done.5), custom_call_target="tpu_custom_call" | custom-call | flops 4294967296 | bytes 1048576 | tf_op jit(solution)/shard_map/pallas_call | solution.py:350
  9.0 6.8 %all-to-all-done.x_ref = bf16[4,256,256]{2,1,0:T(8,128)(2,1)S(1)} async-done(((bf16[4,256,256]{2,1,0:T(8,128)(2,1)}), bf16[4,256,256]{2,1,0:T(8,128)(2,1)S(1)}, u32[]{:S(2)}, u32[]{:S(2)}) %all-to-all-start) | async-done | bytes 524320 | tf_op jit(solution)/shard_map/all_to_all | solution.py:365
  15.8 1.9 %collective-permute-start = (bf16[4,256,256]{2,1,0:T(8,128)(2,1)S(1)}, bf16[4,256,256]{2,1,0:T(8,128)(2,1)S(1)}, u32[]{:S(2)}, u32[]{:S(2)}) collective-permute-start(bf16[4,256,256]{2,1,0:T(8,128)(2,1)S(1)} %all-to-all-done.x_ref), channel_id=1, source_target_pairs={{0,1},{1,0},{2,3},{3,2},{4,5},{5,4},{6,7},{7,6},{8,9},{9,8},{10,11... | collective-permute-start | bytes 1572872 | tf_op jit(solution)/shard_map/ppermute | solution.py:367
  18.5 1.1 %collective-permute-done.o_ref = bf16[4,256,256]{2,1,0:T(8,128)(2,1)S(1)} collective-permute-done((bf16[4,256,256]{2,1,0:T(8,128)(2,1)S(1)}, bf16[4,256,256]{2,1,0:T(8,128)(2,1)S(1)}, u32[]{:S(2)}, u32[]{:S(2)}) %collective-permute-start) | collective-permute-done | bytes 524320 | tf_op jit(solution)/shard_map/ppermute | solution.py:367
  19.6 1.2 %copy-done.3 = bf16[2048,256]{1,0:T(8,128)(2,1)S(1)} copy-done((bf16[2048,256]{1,0:T(8,128)(2,1)S(1)}, bf16[2048,256]{1,0:T(8,128)(2,1)}, u32[]{:S(2)}) %copy-start.3) | copy-done | bytes 1048600
  20.9 2.2 %shard_map.84 = (bf16[912,128]{1,0:T(8,128)(2,1)S(1)}, bf16[912,128]{1,0:T(8,128)(2,1)S(1)}, bf16[2,256,128]{2,1,0:T(8,128)(2,1)S(1)}, bf16[2,256,128]{2,1,0:T(8...) custom-call(s32[3]{0:T(128)S(1)} %pad_add_fusion.at_ref, s32[1]{0:T(128)S(6)} %copy.9.hop_ref, ...), custom_call_target="tpu_custom_call" | custom-call | flops 1073741824 | bytes 1048576 | tf_op jit(solution)/shard_map/pallas_call | solution.py:370
  23.1 0.7 collective-permute-start.1
  23.8 3.4 %collective-permute-start.2 = (bf16[912,128]{1,0:T(8,128)(2,1)S(1)}, bf16[912,128]{1,0:T(8,128)(2,1)S(1)}, u32[]{:S(2)}, u32[]{:S(2)}) collective-permute-start(bf16[912,128]{1,0:T(8,128)(2,1)S(1)} %get-tuple-element.39), channel_id=1, source_target_pairs={{0,8},{1,24},{2,10},{3,26},{4,12},{5,28},{6,14},{7,30},{8,0},{9,16... | collective-permute-start | bytes 700424 | tf_op jit(solution)/shard_map/ppermute | solution.py:376
  27.2 0.6 shard_map.86
  27.8 5.7 %collective-permute-start.4 = (bf16[4,256,256]{2,1,0:T(8,128)(2,1)S(1)}, bf16[4,256,256]{2,1,0:T(8,128)(2,1)S(1)}, u32[]{:S(2)}, u32[]{:S(2)}) collective-permute-start(bf16[4,256,256]{2,1,0:T(8,128)(2,1)S(1)} %shard_map.86), channel_id=1, source_target_pairs={{0,1},{1,0},{2,3},{3,2},{4,5},{5,4},{6,7},{7,6},{8,9},{9,8},{10,11... | collective-permute-start | bytes 1572872 | tf_op jit(solution)/shard_map/ppermute | solution.py:369
  33.9 0.8 shard_map.85
  34.7 2.9 %collective-permute-start.3 = (bf16[1152,128]{1,0:T(8,128)(2,1)S(1)}, bf16[1152,128]{1,0:T(8,128)(2,1)S(1)}, u32[]{:S(2)}, u32[]{:S(2)}) collective-permute-start(bf16[1152,128]{1,0:T(8,128)(2,1)S(1)} %get-tuple-element.41), channel_id=1, source_target_pairs={{0,32},{8,40},{16,48},{24,56},{32,64},{40,72},{48,80},{56,88},{64,... | collective-permute-start | bytes 884744 | tf_op jit(solution)/shard_map/ppermute | solution.py:386
  37.6 4.5 %collective-permute-start.7 = (bf16[1152,128]{1,0:T(8,128)(2,1)S(1)}, bf16[1152,128]{1,0:T(8,128)(2,1)S(1)}, u32[]{:S(2)}, u32[]{:S(2)}) collective-permute-start(bf16[1152,128]{1,0:T(8,128)(2,1)S(1)} %get-tuple-element.41), channel_id=1, source_target_pairs={{0,1},{1,32},{2,3},{3,34},{4,5},{5,36},{6,7},{7,38},{8,9},{9,40},{... | collective-permute-start | bytes 884744 | tf_op jit(solution)/shard_map/ppermute | solution.py:385
  42.1 3.6 %collective-permute-done.3.d2_ref = bf16[1152,128]{1,0:T(8,128)(2,1)S(1)} collective-permute-done((bf16[1152,128]{1,0:T(8,128)(2,1)S(1)}, bf16[1152,128]{1,0:T(8,128)(2,1)S(1)}, u32[]{:S(2)}, u32[]{:S(2)}) %collective-permute-start.3) | collective-permute-done | bytes 294944 | tf_op jit(solution)/shard_map/ppermute | solution.py:386
  45.7 3.7 %collective-permute-start.6 = (bf16[1152,128]{1,0:T(8,128)(2,1)S(1)}, bf16[1152,128]{1,0:T(8,128)(2,1)S(1)}, u32[]{:S(2)}, u32[]{:S(2)}) collective-permute-start(bf16[1152,128]{1,0:T(8,128)(2,1)S(1)} %collective-permute-done.3.d2_ref), channel_id=1, source_target_pairs={{0,1},{1,32},{2,3},{3,34},{4,5},{5,36},{6,7},{7,38},{8,9},{9,40},{... | collective-permute-start | bytes 884744 | tf_op jit(solution)/shard_map/ppermute | solution.py:388
  49.4 1.9 %collective-permute-start.5 = (bf16[1152,128]{1,0:T(8,128)(2,1)S(1)}, bf16[1152,128]{1,0:T(8,128)(2,1)S(1)}, u32[]{:S(2)}, u32[]{:S(2)}) collective-permute-start(bf16[1152,128]{1,0:T(8,128)(2,1)S(1)} %collective-permute-done.3.d2_ref), channel_id=1, source_target_pairs={{0,32},{8,40},{16,48},{24,56},{32,64},{40,72},{48,80},{56,88},{64,... | collective-permute-start | bytes 884744 | tf_op jit(solution)/shard_map/ppermute | solution.py:389
  51.3 2.0 %shard_map.87 = (f32[2,256,128]{2,1,0:T(8,128)S(1)}, f32[2,256,128]{2,1,0:T(8,128)S(1)}, f32[2,256,128]{2,1,0:T(8,128)S(1)}, bf16[2,256,128]{2,1,0:T(8,128)(2,1)S(1)}) custom-call(s32[3]{0:T(128)S(1)} %pad_add_fusion.at_ref, bf16[3,2,256,128]{3,2,1,0:T(8,128)(2,1)S(1)} %get-tuple-element.43.q_ref, f32[2,16,128]{2,1,0:T(8,128)S(1)} %get-tuple-element.40.hop_ref, ...), custom_call_target="tpu_custom_call" | custom-call | flops 2147483648 | bytes 1048576 | tf_op jit(solution)/shard_map/pallas_call | solution.py:391
  53.4 1.6 %collective-permute-done.6.d3_ref = bf16[1152,128]{1,0:T(8,128)(2,1)S(1)} collective-permute-done((bf16[1152,128]{1,0:T(8,128)(2,1)S(1)}, bf16[1152,128]{1,0:T(8,128)(2,1)S(1)}, u32[]{:S(2)}, u32[]{:S(2)}) %collective-permute-start.6) | collective-permute-done | bytes 294944 | tf_op jit(solution)/shard_map/ppermute | solution.py:388
  54.9 1.5 %shard_map.88 = (f32[2,256,128]{2,1,0:T(8,128)S(1)}, f32[2,256,128]{2,1,0:T(8,128)S(1)}, f32[2,256,128]{2,1,0:T(8,128)S(1)}, bf16[2,256,128]{2,1,0:T(8,128)(2,1)S(1)}) custom-call(s32[3]{0:T(128)S(1)} %pad_add_fusion.at_ref, f32[2,16,128]{2,1,0:T(8,128)S(1)} %get-tuple-element.40.hop_ref, bf16[1152,128]{1,0:T(8,128)(2,1)S(1)} %collective-permute-done.6.d3_ref, ...), custom_call_target="tpu_custom_call" | custom-call | flops 1073741824 | bytes 1048576 | tf_op jit(solution)/shard_map/pallas_call | solution.py:392
  56.5 4.9 %collective-permute-done.5.d4_ref = bf16[1152,128]{1,0:T(8,128)(2,1)S(1)} collective-permute-done((bf16[1152,128]{1,0:T(8,128)(2,1)S(1)}, bf16[1152,128]{1,0:T(8,128)(2,1)S(1)}, u32[]{:S(2)}, u32[]{:S(2)}) %collective-permute-start.5) | collective-permute-done | bytes 294944 | tf_op jit(solution)/shard_map/ppermute | solution.py:389
  61.4 1.6 %shard_map.89 = (bf16[272,128]{1,0:T(8,128)(2,1)S(1)}, bf16[272,128]{1,0:T(8,128)(2,1)S(1)}) custom-call(s32[3]{0:T(128)S(1)} %pad_add_fusion.at_ref, f32[2,16,128]{2,1,0:T(8,128)S(1)} %get-tuple-element.40.hop_ref, bf16[1152,128]{1,0:T(8,128)(2,1)S(1)} %collective-permute-done.5.d4_ref, f32[2,256,128]{2,1,0:T(8,128)S(1)} %get-tuple-element.48.acc_ref, ...), custom_call_target="tpu_custom_call" | custom-call | flops 1073741824 | bytes 1048576 | tf_op jit(solution)/shard_map/pallas_call | solution.py:393
  63.0 4.4 %collective-permute-start.8 = (bf16[272,128]{1,0:T(8,128)(2,1)S(1)}, bf16[272,128]{1,0:T(8,128)(2,1)S(1)}, u32[]{:S(2)}, u32[]{:S(2)}) collective-permute-start(bf16[272,128]{1,0:T(8,128)(2,1)S(1)} %get-tuple-element.52), channel_id=1, source_target_pairs={{8,0},{24,1},{10,2},{26,3},{12,4},{28,5},{14,6},{30,7},{0,8},{16,9... | collective-permute-start | bytes 208904 | tf_op jit(solution)/shard_map/ppermute | solution.py:397
  67.4 0.7 collective-permute-start.9
  68.1 0.9 shard_map.90
  69.0 0.7 collective-permute-done.8.g1_ref
  69.7 1.0 %shard_map.91.mine_ref = bf16[256,256]{1,0:T(8,128)(2,1)S(1)} custom-call(s32[3]{0:T(128)S(1)} %pad_add_fusion.at_ref, bf16[272,128]{1,0:T(8,128)(2,1)S(1)} %collective-permute-done.8.g1_ref, bf16[272,128]{1,0:T(8,128)(2,1)S(1)} %collective-permute-done.9.g0_ref, f32[2,256,128]{2,1,0:T(8,128)S(1)} %get-tuple-element.58.acc_ref, ...), custom_call_target="tpu_custom_call" | custom-call | flops 268435456 | bytes 1048576 | tf_op jit(solution)/shard_map/pallas_call | solution.py:398
  70.7 7.9 %collective-permute-start.10 = (bf16[256,256]{1,0:T(8,128)(2,1)S(1)}, bf16[256,256]{1,0:T(8,128)(2,1)S(1)}, u32[]{:S(2)}, u32[]{:S(2)}) collective-permute-start(bf16[256,256]{1,0:T(8,128)(2,1)S(1)} %shard_map.91.mine_ref), channel_id=1, source_target_pairs={{0,1},{1,0},{2,3},{3,2},{4,5},{5,4},{6,7},{7,6},{8,9},{9,8},{10,11... | collective-permute-start | bytes 393224 | tf_op jit(solution)/shard_map/ppermute | solution.py:399
  78.6 0.9 shard_map.92.part_ref
  79.9 12.7 %all_to_all.10.x_ref = bf16[4,256,256]{2,1,0:T(8,128)(2,1)S(1)} all-to-all(bf16[4,256,256]{2,1,0:T(8,128)(2,1)S(1)} %shard_map.93), channel_id=1, replica_groups={{0,2,4,6},{1,3,5,7},{8,10,12,14},{9,11,13,15},{16,18,20,22},{17,19,21,2..., dimensions={0} | all-to-all | bytes 1048576 | tf_op jit(solution)/shard_map/all_to_all | solution.py:402
  92.5 0.7 shard_map.94
  (19 shorter events, 0.9 us)
Async XLA Ops:
  1.7 4.6 %copy-start.4 = (bf16[256,256]{1,0:T(8,128)(2,1)S(1)}, bf16[256,256]{1,0:T(8,128)(2,1)}, u32[]{:S(2)}) copy-start(bf16[256,256]{1,0:T(8,128)(2,1)} %dirs_ref.1) | copy-start | bytes 393220
  1.7 4.6 %copy-start.5 = (f32[2,256]{1,0:T(2,128)S(1)}, f32[2,256]{1,0:T(2,128)}, u32[]{:S(2)}) copy-start(f32[2,256]{1,0:T(2,128)} %beta_ref.1) | copy-start | bytes 6148
  1.8 14.1 %all-to-all-start = ((bf16[4,256,256]{2,1,0:T(8,128)(2,1)}), bf16[4,256,256]{2,1,0:T(8,128)(2,1)S(1)}, u32[]{:S(2)}, u32[]{:S(2)}) async-start(bf16[4,256,256]{2,1,0:T(8,128)(2,1)} %shard_map.82), calls=%async_computation | async-start | bytes 1048576 | tf_op jit(solution)/shard_map/all_to_all | solution.py:365
  6.4 13.3 %copy-start.1 = (bf16[2048,256]{1,0:T(8,128)(2,1)S(1)}, bf16[2048,256]{1,0:T(8,128)(2,1)}, u32[]{:S(2)}) copy-start(bf16[2048,256]{1,0:T(8,128)(2,1)} %wq_ref.1) | copy-start | bytes 3145732
  6.4 13.3 %copy-start.2 = (bf16[2048,256]{1,0:T(8,128)(2,1)S(1)}, bf16[2048,256]{1,0:T(8,128)(2,1)}, u32[]{:S(2)}) copy-start(bf16[2048,256]{1,0:T(8,128)(2,1)} %wk_ref.1) | copy-start | bytes 3145732
  15.8 3.8 %collective-permute-start = (bf16[4,256,256]{2,1,0:T(8,128)(2,1)S(1)}, bf16[4,256,256]{2,1,0:T(8,128)(2,1)S(1)}, u32[]{:S(2)}, u32[]{:S(2)}) collective-permute-start(bf16[4,256,256]{2,1,0:T(8,128)(2,1)S(1)} %all-to-all-done.x_ref), channel_id=1, source_target_pairs={{0,1},{1,0},{2,3},{3,2},{4,5},{5,4},{6,7},{7,6},{8,9},{9,8},{10,11... | collective-permute-start | bytes 1572872 | tf_op jit(solution)/shard_map/ppermute | solution.py:367
  19.6 1.2 %copy-start.3 = (bf16[2048,256]{1,0:T(8,128)(2,1)S(1)}, bf16[2048,256]{1,0:T(8,128)(2,1)}, u32[]{:S(2)}) copy-start(bf16[2048,256]{1,0:T(8,128)(2,1)} %wv_ref.1) | copy-start | bytes 3145732
  20.9 6.3 %copy-start = (bf16[256,2048]{1,0:T(8,128)(2,1)S(1)}, bf16[256,2048]{1,0:T(8,128)(2,1)}, u32[]{:S(2)}) copy-start(bf16[256,2048]{1,0:T(8,128)(2,1)} %wo_ref.3) | copy-start | bytes 3145732
  23.1 10.4 %collective-permute-start.1 = (bf16[912,128]{1,0:T(8,128)(2,1)S(1)}, bf16[912,128]{1,0:T(8,128)(2,1)S(1)}, u32[]{:S(2)}, u32[]{:S(2)}) collective-permute-start(bf16[912,128]{1,0:T(8,128)(2,1)S(1)} %get-tuple-element.38), channel_id=1, source_target_pairs={{0,0},{1,16},{2,2},{3,18},{4,4},{5,20},{6,6},{7,22},{8,8},{9,24},{... | collective-permute-start | bytes 700424 | tf_op jit(solution)/shard_map/ppermute | solution.py:375
  23.8 10.1 %collective-permute-start.2 = (bf16[912,128]{1,0:T(8,128)(2,1)S(1)}, bf16[912,128]{1,0:T(8,128)(2,1)S(1)}, u32[]{:S(2)}, u32[]{:S(2)}) collective-permute-start(bf16[912,128]{1,0:T(8,128)(2,1)S(1)} %get-tuple-element.39), channel_id=1, source_target_pairs={{0,8},{1,24},{2,10},{3,26},{4,12},{5,28},{6,14},{7,30},{8,0},{9,16... | collective-permute-start | bytes 700424 | tf_op jit(solution)/shard_map/ppermute | solution.py:376
  27.8 14.3 %collective-permute-start.4 = (bf16[4,256,256]{2,1,0:T(8,128)(2,1)S(1)}, bf16[4,256,256]{2,1,0:T(8,128)(2,1)S(1)}, u32[]{:S(2)}, u32[]{:S(2)}) collective-permute-start(bf16[4,256,256]{2,1,0:T(8,128)(2,1)S(1)} %shard_map.86), channel_id=1, source_target_pairs={{0,1},{1,0},{2,3},{3,2},{4,5},{5,4},{6,7},{7,6},{8,9},{9,8},{10,11... | collective-permute-start | bytes 1572872 | tf_op jit(solution)/shard_map/ppermute | solution.py:369
  34.7 11.0 %collective-permute-start.3 = (bf16[1152,128]{1,0:T(8,128)(2,1)S(1)}, bf16[1152,128]{1,0:T(8,128)(2,1)S(1)}, u32[]{:S(2)}, u32[]{:S(2)}) collective-permute-start(bf16[1152,128]{1,0:T(8,128)(2,1)S(1)} %get-tuple-element.41), channel_id=1, source_target_pairs={{0,32},{8,40},{16,48},{24,56},{32,64},{40,72},{48,80},{56,88},{64,... | collective-permute-start | bytes 884744 | tf_op jit(solution)/shard_map/ppermute | solution.py:386
  37.6 13.7 %collective-permute-start.7 = (bf16[1152,128]{1,0:T(8,128)(2,1)S(1)}, bf16[1152,128]{1,0:T(8,128)(2,1)S(1)}, u32[]{:S(2)}, u32[]{:S(2)}) collective-permute-start(bf16[1152,128]{1,0:T(8,128)(2,1)S(1)} %get-tuple-element.41), channel_id=1, source_target_pairs={{0,1},{1,32},{2,3},{3,34},{4,5},{5,36},{6,7},{7,38},{8,9},{9,40},{... | collective-permute-start | bytes 884744 | tf_op jit(solution)/shard_map/ppermute | solution.py:385
  45.7 9.2 %collective-permute-start.6 = (bf16[1152,128]{1,0:T(8,128)(2,1)S(1)}, bf16[1152,128]{1,0:T(8,128)(2,1)S(1)}, u32[]{:S(2)}, u32[]{:S(2)}) collective-permute-start(bf16[1152,128]{1,0:T(8,128)(2,1)S(1)} %collective-permute-done.3.d2_ref), channel_id=1, source_target_pairs={{0,1},{1,32},{2,3},{3,34},{4,5},{5,36},{6,7},{7,38},{8,9},{9,40},{... | collective-permute-start | bytes 884744 | tf_op jit(solution)/shard_map/ppermute | solution.py:388
  49.4 12.0 %collective-permute-start.5 = (bf16[1152,128]{1,0:T(8,128)(2,1)S(1)}, bf16[1152,128]{1,0:T(8,128)(2,1)S(1)}, u32[]{:S(2)}, u32[]{:S(2)}) collective-permute-start(bf16[1152,128]{1,0:T(8,128)(2,1)S(1)} %collective-permute-done.3.d2_ref), channel_id=1, source_target_pairs={{0,32},{8,40},{16,48},{24,56},{32,64},{40,72},{48,80},{56,88},{64,... | collective-permute-start | bytes 884744 | tf_op jit(solution)/shard_map/ppermute | solution.py:389
  63.0 6.7 %collective-permute-start.8 = (bf16[272,128]{1,0:T(8,128)(2,1)S(1)}, bf16[272,128]{1,0:T(8,128)(2,1)S(1)}, u32[]{:S(2)}, u32[]{:S(2)}) collective-permute-start(bf16[272,128]{1,0:T(8,128)(2,1)S(1)} %get-tuple-element.52), channel_id=1, source_target_pairs={{8,0},{24,1},{10,2},{26,3},{12,4},{28,5},{14,6},{30,7},{0,8},{16,9... | collective-permute-start | bytes 208904 | tf_op jit(solution)/shard_map/ppermute | solution.py:397
  67.4 2.3 %collective-permute-start.9 = (bf16[272,128]{1,0:T(8,128)(2,1)S(1)}, bf16[272,128]{1,0:T(8,128)(2,1)S(1)}, u32[]{:S(2)}, u32[]{:S(2)}) collective-permute-start(bf16[272,128]{1,0:T(8,128)(2,1)S(1)} %get-tuple-element.53), channel_id=1, source_target_pairs={{0,0},{16,1},{2,2},{18,3},{4,4},{20,5},{6,6},{22,7},{8,8},{24,9},{... | collective-permute-start | bytes 208904 | tf_op jit(solution)/shard_map/ppermute | solution.py:396
  70.7 8.9 %collective-permute-start.10 = (bf16[256,256]{1,0:T(8,128)(2,1)S(1)}, bf16[256,256]{1,0:T(8,128)(2,1)S(1)}, u32[]{:S(2)}, u32[]{:S(2)}) collective-permute-start(bf16[256,256]{1,0:T(8,128)(2,1)S(1)} %shard_map.91.mine_ref), channel_id=1, source_target_pairs={{0,1},{1,0},{2,3},{3,2},{4,5},{5,4},{6,7},{7,6},{8,9},{9,8},{10,11... | collective-permute-start | bytes 393224 | tf_op jit(solution)/shard_map/ppermute | solution.py:399
